TPU v7x, 32 devices: a whole 2x2x4 slice. The times are simulated.
32 devices in a mesh: bx: 4 (over z), by: 2 (over y), bz: 4 (over x, core).
Axes of the slice: x: 2, y: 2, z: 4, core: 2. Of those that a mesh axis runs over, the one named last changes fastest.
Arguments:
- positions: float32 [3, 131072], P(None, ('bx', 'by', 'bz')), may hold values from -15 to 55, as said below
- velocities: float32 [3, 131072], P(None, ('bx', 'by', 'bz')), may hold values from -6 to 6
- species: int32 [131072], P(('bx', 'by', 'bz')), may hold values 0 or 1
- corner_slot: int32 [2, 8, 131072], P(None, None, ('bx', 'by', 'bz')), may hold values from 0 to 255, as said below
- corner_weight: float32 [8, 131072], P(None, ('bx', 'by', 'bz')), may hold values from 0 to 1, as said below
- slot_cell: int32 [3, 256, 256], P(None, ('bx', 'by', 'bz')), may hold values from 0 to 63, as said below
- bond_pairs: int32 [2, 122880], P(None, ('bx', 'by', 'bz')), may hold values from 0 to 4095, as said below
Outputs:
- new_positions: float32 [3, 131072], P(None, ('bx', 'by', 'bz'))
- new_velocities: float32 [3, 131072], P(None, ('bx', 'by', 'bz'))
- smoothed: float32 [2, 64, 128, 256], P(None, 'bx', 'by', 'bz')
Inputs may be any that keep to these rules, and one draw needn't show every extreme that they name: `corner_slot`: row 0 is below 8 and row 1 below 256. For every owner and destination brick the named slots are those below a count of at least 32; the count is 256 for some destination of every owner, and for some brick of every z plane from all owners of that plane. `corner_weight`: for each bead the eight weights are the trilinear weights of a point inside a cell, corner c taking the upper side along x, y, z by bits 4, 2, 1 of c; they sum to one. `slot_cell`: row 0 is below 16, row 1 below 64, row 2 below 64. `bond_pairs`: bonds join beads of one device into chains of 16 beads; each bead lies in at most two bonds. `positions`: bonded beads stand at distance 1.
All inputs are finite; a program needn't handle non-finite values. No bound on the sum of `species` on one device may be relied on, other than what follows from the above.
Results may differ from a plain program's by a relative error of at most 0.0003.
Values sent between devices are 32-bit elements; how exact they have to be, the bound alone decides.
No kernel may reach another device: no remote copies, remote signals or barrier semaphores. Data moves between devices by JAX's collectives and lax.ppermute only.
A program may use at most 128 MiB of HBM per device.

v0:
```python
import math

import jax
import jax.numpy as jnp
from jax import lax
from jax.sharding import PartitionSpec as P

CX = 16
CY = 64
CZ = 64
BEADS_DEV = 4096
REACH = 3
SWEEPS = 4


spread_cells = 1.0
mixing = 10.0
stiffness = 5.0
time_step = 0.1
bond_length = 1.0


def extended_2(cells, sides, width):
    for axis, dim in sides:
        count = lax.axis_size(axis)
        head = lax.slice_in_dim(cells, 0, width, axis=dim)
        tail = lax.slice_in_dim(cells, cells.shape[dim] - width, cells.shape[dim], axis=dim)
        cells = jnp.concatenate(
            [
                lax.ppermute(tail, axis, [(i, (i + 1) % count) for i in range(count)]),
                cells,
                lax.ppermute(head, axis, [((i + 1) % count, i) for i in range(count)]),
            ],
            axis=dim,
        )
    return cells


def gauss_taps():
    raw_list = [
        math.exp(-0.5 * (offset - REACH) ** 2 / spread_cells**2) for offset in range(2 * REACH + 1)
    ]
    tap_total = sum(raw_list)
    return [entry / tap_total for entry in raw_list]


def smooth_along(extended, axis):
    taps = gauss_taps()
    length = extended.shape[axis] - 2 * REACH
    result = jnp.zeros_like(lax.slice_in_dim(extended, 0, length, axis=axis))
    for offset in range(2 * REACH + 1):
        result = result + taps[offset] * lax.slice_in_dim(
            extended, offset, offset + length, axis=axis
        )
    return result


def smooth_brick(density, margin):
    width = REACH + margin
    field = smooth_along(extended_2(density, (("bx", 1),), width), 1)
    field = smooth_along(extended_2(field, (("by", 2),), width), 2)
    return smooth_along(extended_2(field, (("bz", 3),), width), 3)


def constrain(anchor, moved, first, second):
    separation = anchor[:, first] - anchor[:, second]
    for repeat in range(SWEEPS):
        stretch = moved[:, first] - moved[:, second]
        excess = jnp.sum(stretch * stretch, axis=0) - bond_length * bond_length
        intersection = jnp.maximum(
            jnp.sum(stretch * separation, axis=0), 0.5 * bond_length * bond_length
        )
        factor = excess / (4.0 * intersection)
        shifted = factor * separation
        moved = moved.at[:, first].add(-shifted).at[:, second].add(shifted)
    return moved


def on_device(positions, velocities, species, corner_slot, corner_weight, slot_cell, bond_pairs):
    plane = slot_cell.shape[1]
    slots = slot_cell.shape[2]
    cells = CX * CY * CZ
    is_lipid = (species == 0)[None, :]
    flat_slots = (corner_slot[0] * slots + corner_slot[1]).reshape(-1)
    both = jnp.stack(
        [jnp.where(is_lipid, corner_weight, 0.0), jnp.where(is_lipid, 0.0, corner_weight)]
    )
    packets = jnp.zeros((2, plane * slots), jnp.float32).at[:, flat_slots].add(both.reshape(2, -1))
    received = lax.all_to_all(
        packets.reshape(2, plane, slots), ("bx", "by"), split_axis=1, concat_axis=1, tiled=True
    )
    flat_cells = ((slot_cell[0] * CY + slot_cell[1]) * CZ + slot_cell[2]).reshape(-1)
    density = jnp.zeros((2, cells), jnp.float32).at[:, flat_cells].add(received.reshape(2, -1))
    density = density * (CX * CY * CZ / BEADS_DEV)
    density = density.reshape(2, CX, CY, CZ)
    margin = 1
    filtered = smooth_brick(density, margin)
    smoothed = filtered[:, margin : margin + CX, margin : margin + CY, margin : margin + CZ]
    combined = filtered[0] + filtered[1]
    potential = jnp.stack(
        [mixing * filtered[1] + stiffness * combined, mixing * filtered[0] + stiffness * combined]
    )
    slope_x = (potential[:, 2:, 1:-1, 1:-1] - potential[:, :-2, 1:-1, 1:-1]) * 0.5
    slope_y = (potential[:, 1:-1, 2:, 1:-1] - potential[:, 1:-1, :-2, 1:-1]) * 0.5
    slope_z = (potential[:, 1:-1, 1:-1, 2:] - potential[:, 1:-1, 1:-1, :-2]) * 0.5
    slopes = jnp.stack([slope_x, slope_y, slope_z], axis=1).reshape(6, cells)
    outgoing = slopes[:, flat_cells]
    returned = lax.all_to_all(
        outgoing.reshape(6, plane, slots), ("bx", "by"), split_axis=1, concat_axis=1, tiled=True
    )
    table = returned.reshape(2, 3, plane * slots)
    count = corner_weight.shape[1]
    picked = jnp.where(
        is_lipid[None],
        table[0][:, flat_slots].reshape(3, 8, count),
        table[1][:, flat_slots].reshape(3, 8, count),
    )
    force = -jnp.sum(corner_weight[None] * picked, axis=1)
    half = velocities + 0.5 * time_step * force
    moved = positions + time_step * half
    moved = constrain(positions, moved, bond_pairs[0], bond_pairs[1])
    new_velocities = (moved - positions) / time_step
    return (moved, new_velocities, smoothed)


def solution(mesh):
    in_specs = (
        P(None, ("bx", "by", "bz")),
        P(None, ("bx", "by", "bz")),
        P(("bx", "by", "bz")),
        P(None, None, ("bx", "by", "bz")),
        P(None, ("bx", "by", "bz")),
        P(None, ("bx", "by", "bz"), None),
        P(None, ("bx", "by", "bz")),
    )
    out_specs = (
        P(None, ("bx", "by", "bz")),
        P(None, ("bx", "by", "bz")),
        P(None, "bx", "by", "bz"),
    )
    return jax.shard_map(
        on_device, mesh=mesh, in_specs=in_specs, out_specs=out_specs, check_vma=False
    )
```

profile of v0, /device:TPU:0, one launch (start us, length us, event | category | flops | bytes accessed | tf_op | source)
XLA Modules:
  0.0 923.4 jit_solution(6195723974786675609)
XLA Ops:
  2.8 8.3 copy.147
  11.5 174.5 %scatter_custom_fusion = f32[2,2048]{0,1:T(8,128)S(1)} fusion(s32[32768]{0:T(1024)S(1)} %bitcast.55, f32[32768,2]{1,0:T(8,128)} %copy.147, f32[]{:T(128)} %constant.20.clone.1), kind=kCustom, calls=%fused_computation.165 | custom fusion | flops 65536 | bytes 16896 | tf_op jit(solution)/shard_map/scatter-add | solution.py:88
  186.9 7.3 all-to-all-start
  194.3 6.5 all-to-all-done
  201.2 24.6 %scatter_custom_fusion.1 = f32[2,65536]{0,1:T(8,128)} fusion(s32[2048]{0:T(1024)S(1)} %bitcast.61, f32[2048,2]{1,0:T(8,128)S(1)} %copy.149, f32[]{:T(128)} %constant.20.clone.1), kind=kCustom, calls=%fused_computation.25 | custom fusion | flops 4096 | bytes 524292 | tf_op jit(solution)/shard_map/scatter-add | solution.py:93
  225.8 22.3 %broadcast_multiply_fusion = f32[2,65536]{0,1:T(8,128)} fusion(f32[2,65536]{0,1:T(8,128)} %scatter_custom_fusion.1), kind=kLoop, calls=%fused_computation.24 | loop fusion | flops 131072 | bytes 1048576 | tf_op jit(solution)/shard_map/mul | solution.py:94
  248.1 18.1 %copy.150 = f32[2,16,64,64]{3,1,2,0:T(8,128)S(1)} copy(f32[2,16,64,64]{0,3,2,1:T(8,128)} %bitcast.48) | data formatting | bytes 1048576 | tf_op jit(solution)/shard_map/reshape | solution.py:95
  270.7 6.8 collective-permute-done
  303.0 8.7 fusion.37
  316.9 16.5 %copy.162 = f32[6,65536]{0,1:T(8,128)} copy(f32[6,65536]{1,0:T(8,128)} %reshape.218) | data formatting | bytes 3145728 | tf_op jit(solution)/shard_map/reshape | solution.py:106
  333.5 16.1 %gather_fusion = f32[2048,6]{1,0:T(8,128)S(1)} fusion(f32[6,65536]{0,1:T(8,128)} %copy.162, s32[2048]{0:T(1024)S(1)} %copy-done.11), kind=kCustom, calls=%fused_computation | custom fusion | bytes 106496 | tf_op jit(solution)/shard_map/gather | solution.py:107
  354.2 9.4 %gather_fusion.5 = f32[3840,3]{1,0:T(8,128)} fusion(f32[3,4096]{0,1:T(8,128)} %copy.169, s32[4096]{0:T(1024)S(1)} %get-tuple-element.51), kind=kCustom, calls=%fused_computation.5 | custom fusion | bytes 107520 | tf_op jit(solution)/shard_map/gather | solution.py:66
  363.6 9.4 %gather_fusion.6 = f32[3840,3]{1,0:T(8,128)} fusion(f32[3,4096]{0,1:T(8,128)} %copy.169, s32[4096]{0:T(1024)S(1)} %get-tuple-element.50), kind=kCustom, calls=%fused_computation.6 | custom fusion | bytes 107520 | tf_op jit(solution)/shard_map/gather | solution.py:66
  375.5 108.2 %gather_fusion.2 = f32[32768,3]{1,0:T(8,128)} fusion(f32[3,2048]{0,1:T(8,128)S(1)} %bitcast.49, s32[32768]{0:T(1024)S(1)} %broadcast_clamp_fusion), kind=kCustom, calls=%fused_computation.2 | custom fusion | bytes 917504 | tf_op jit(solution)/shard_map/gather | solution.py:116
  483.7 108.2 %gather_fusion.1 = f32[32768,3]{1,0:T(8,128)} fusion(f32[3,2048]{0,1:T(8,128)S(1)} %bitcast.50, s32[32768]{0:T(1024)S(1)} %broadcast_clamp_fusion), kind=kCustom, calls=%fused_computation.1 | custom fusion | bytes 917504 | tf_op jit(solution)/shard_map/gather | solution.py:115
  591.9 14.3 %multiply_reduce_fusion = f32[3,4096]{0,1:T(8,128)S(1)} fusion(f32[3,8,4096]{0,2,1:T(8,128)} %bitcast.52, f32[3,8,4096]{0,2,1:T(8,128)} %bitcast.51, f32[8,4096]{1,0:T(8,128)S(1)} %copy-done.4, pred[4096]{0:T(1024)(128)(4,1)S(1)} %copy-done.10), kind=kLoop, calls=%fused_computation.23 | loop fusion | flops 282624 | bytes 970752 | tf_op jit(solution)/shard_map/reduce_sum | solution.py:118
  607.7 7.9 gather_fusion.4
  615.7 7.9 gather_fusion.3
  627.9 27.5 %scatter_custom_fusion.2 = f32[3,4096]{0,1:T(8,128)} fusion(f32[3,4096]{0,1:T(8,128)} %copy-done, s32[3840]{0:T(1024)S(1)} %copy-done.8, f32[3840,3]{1,0:T(8,128)S(1)} %get-tuple-element.34, f32[3840]{0:T(1024)S(1)} %multiply_divide_fusion.3), kind=kCustom, calls=%fused_computation.53 | custom fusion | flops 34560 | bytes 2031616 | tf_op jit(solution)/shard_map/scatter-add | solution.py:75
  655.5 27.7 %scatter_custom_fusion.3 = f32[3,4096]{0,1:T(8,128)} fusion(f32[3,4096]{0,1:T(8,128)} %scatter_custom_fusion.2, s32[3840]{0:T(1024)S(1)} %get-tuple-element.32, f32[3840,3]{1,0:T(8,128)S(1)} %get-tuple-element.34, f32[3840]{0:T(1024)S(1)} %multiply_divide_fusion.3), kind=kCustom, calls=%fused_computation.72 | custom fusion | flops 23040 | bytes 2031616 | tf_op jit(solution)/shard_map/scatter-add | solution.py:75
  683.1 9.5 %gather_fusion.8 = f32[3840,3]{1,0:T(8,128)} fusion(f32[3,4096]{0,1:T(8,128)} %scatter_custom_fusion.3, s32[4096]{0:T(1024)S(1)} %get-tuple-element.50), kind=kCustom, calls=%fused_computation.8 | custom fusion | bytes 107520 | tf_op jit(solution)/shard_map/gather | solution.py:68
  692.6 9.4 %gather_fusion.7 = f32[3840,3]{1,0:T(8,128)} fusion(f32[3,4096]{0,1:T(8,128)} %scatter_custom_fusion.3, s32[4096]{0:T(1024)S(1)} %get-tuple-element.51), kind=kCustom, calls=%fused_computation.7 | custom fusion | bytes 107520 | tf_op jit(solution)/shard_map/gather | solution.py:68
  705.3 27.5 %scatter_custom_fusion.4 = f32[3,4096]{0,1:T(8,128)} fusion(f32[3,4096]{0,1:T(8,128)} %scatter_custom_fusion.3, s32[3840]{0:T(1024)S(1)} %copy-done.8, f32[3840,3]{1,0:T(8,128)S(1)} %get-tuple-element.34, f32[3840]{0:T(1024)S(1)} %multiply_divide_fusion.2), kind=kCustom, calls=%fused_computation.51 | custom fusion | flops 34560 | bytes 2031616 | tf_op jit(solution)/shard_map/scatter-add | solution.py:75
  732.9 27.5 %scatter_custom_fusion.5 = f32[3,4096]{0,1:T(8,128)} fusion(f32[3,4096]{0,1:T(8,128)} %scatter_custom_fusion.4, s32[3840]{0:T(1024)S(1)} %get-tuple-element.32, f32[3840,3]{1,0:T(8,128)S(1)} %get-tuple-element.34, f32[3840]{0:T(1024)S(1)} %multiply_divide_fusion.2), kind=kCustom, calls=%fused_computation.69 | custom fusion | flops 23040 | bytes 2031616 | tf_op jit(solution)/shard_map/scatter-add | solution.py:75
  760.3 9.5 %gather_fusion.10 = f32[3840,3]{1,0:T(8,128)} fusion(f32[3,4096]{0,1:T(8,128)} %scatter_custom_fusion.5, s32[4096]{0:T(1024)S(1)} %get-tuple-element.50), kind=kCustom, calls=%fused_computation.10 | custom fusion | bytes 107520 | tf_op jit(solution)/shard_map/gather | solution.py:68
  769.8 9.4 %gather_fusion.9 = f32[3840,3]{1,0:T(8,128)} fusion(f32[3,4096]{0,1:T(8,128)} %scatter_custom_fusion.5, s32[4096]{0:T(1024)S(1)} %get-tuple-element.51), kind=kCustom, calls=%fused_computation.9 | custom fusion | bytes 107520 | tf_op jit(solution)/shard_map/gather | solution.py:68
  782.5 27.8 %scatter_custom_fusion.6 = f32[3,4096]{0,1:T(8,128)} fusion(f32[3,4096]{0,1:T(8,128)} %scatter_custom_fusion.5, s32[3840]{0:T(1024)S(1)} %copy-done.8, f32[3840,3]{1,0:T(8,128)S(1)} %get-tuple-element.34, f32[3840]{0:T(1024)S(1)} %multiply_divide_fusion.1), kind=kCustom, calls=%fused_computation.49 | custom fusion | flops 34560 | bytes 2031616 | tf_op jit(solution)/shard_map/scatter-add | solution.py:75
  810.3 27.5 %scatter_custom_fusion.7 = f32[3,4096]{0,1:T(8,128)} fusion(f32[3,4096]{0,1:T(8,128)} %scatter_custom_fusion.6, s32[3840]{0:T(1024)S(1)} %get-tuple-element.32, f32[3840,3]{1,0:T(8,128)S(1)} %get-tuple-element.34, f32[3840]{0:T(1024)S(1)} %multiply_divide_fusion.1), kind=kCustom, calls=%fused_computation.66 | custom fusion | flops 23040 | bytes 2031616 | tf_op jit(solution)/shard_map/scatter-add | solution.py:75
  837.8 9.5 %gather_fusion.12 = f32[3840,3]{1,0:T(8,128)} fusion(f32[3,4096]{0,1:T(8,128)} %scatter_custom_fusion.7, s32[4096]{0:T(1024)S(1)} %get-tuple-element.50), kind=kCustom, calls=%fused_computation.12 | custom fusion | bytes 107520 | tf_op jit(solution)/shard_map/gather | solution.py:68
  847.3 9.4 %gather_fusion.11 = f32[3840,3]{1,0:T(8,128)} fusion(f32[3,4096]{0,1:T(8,128)} %scatter_custom_fusion.7, s32[4096]{0:T(1024)S(1)} %get-tuple-element.51), kind=kCustom, calls=%fused_computation.11 | custom fusion | bytes 107520 | tf_op jit(solution)/shard_map/gather | solution.py:68
  860.0 27.5 %scatter_custom_fusion.8 = f32[3,4096]{0,1:T(8,128)} fusion(f32[3,4096]{0,1:T(8,128)} %scatter_custom_fusion.7, s32[3840]{0:T(1024)S(1)} %copy-done.8, f32[3840,3]{1,0:T(8,128)S(1)} %get-tuple-element.34, f32[3840]{0:T(1024)S(1)} %multiply_divide_fusion), kind=kCustom, calls=%fused_computation.47 | custom fusion | flops 34560 | bytes 2031616 | tf_op jit(solution)/shard_map/scatter-add | solution.py:75
  887.5 27.5 %scatter_custom_fusion.9 = f32[3,4096]{0,1:T(8,128)} fusion(f32[3,4096]{0,1:T(8,128)} %scatter_custom_fusion.8, s32[3840]{0:T(1024)S(1)} %get-tuple-element.32, f32[3840,3]{1,0:T(8,128)S(1)} %get-tuple-element.34, f32[3840]{0:T(1024)S(1)} %multiply_divide_fusion), kind=kCustom, calls=%fused_computation.63 | custom fusion | flops 23040 | bytes 2031616 | tf_op jit(solution)/shard_map/scatter-add | solution.py:75
  (91 shorter events, 69.6 us)
Async XLA Ops:
  1.4 1.2 copy-start.9
  2.8 8.4 copy-start.5
  11.2 183.0 %copy-start.12 = (s32[3,8,256]{2,1,0:T(8,128)S(1)}, s32[3,8,256]{2,1,0:T(8,128)}, u32[]{:S(2)}) copy-start(s32[3,8,256]{2,1,0:T(8,128)} %param.12) | copy-start | bytes 73732
  186.9 13.9 %all-to-all-start = ((f32[2,8,256]{2,0,1:T(2,128)}), f32[2,8,256]{2,0,1:T(2,128)S(1)}, u32[]{:S(2)}, u32[]{:S(2)}) async-start(f32[2,8,256]{2,0,1:T(2,128)} %copy.148), calls=%async_computation | async-start | bytes 32768 | tf_op jit(solution)/shard_map/all_to_all | solution.py:89
  266.3 11.1 %collective-permute-start = (f32[2,4,64,64]{3,1,2,0:T(4,128)S(1)}, f32[2,4,64,64]{3,1,2,0:T(4,128)S(1)}, u32[]{:S(2)}, u32[]{:S(2)}) collective-permute-start(f32[2,4,64,64]{3,1,2,0:T(4,128)S(1)} %get-tuple-element.44), channel_id=1, source_target_pairs={{0,8},{8,16},{16,24},{24,0},{1,9},{9,17},{17,25},{25,1},{2,10},{10... | collective-permute-start | bytes 393224 | tf_op jit(solution)/shard_map/ppermute | solution.py:30
  266.9 12.4 %collective-permute-start.1 = (f32[2,4,64,64]{3,1,2,0:T(4,128)S(1)}, f32[2,4,64,64]{3,1,2,0:T(4,128)S(1)}, u32[]{:S(2)}, u32[]{:S(2)}) collective-permute-start(f32[2,4,64,64]{3,1,2,0:T(4,128)S(1)} %get-tuple-element.45), channel_id=1, source_target_pairs={{8,0},{16,8},{24,16},{0,24},{9,1},{17,9},{25,17},{1,25},{10,2},{18... | collective-permute-start | bytes 393224 | tf_op jit(solution)/shard_map/ppermute | solution.py:32
  281.2 4.7 collective-permute-start.2
  282.0 5.0 collective-permute-start.3
  290.1 6.7 copy-start.6
  292.1 6.6 collective-permute-start.4
  293.5 6.8 collective-permute-start.5
  311.7 1.6 copy-start.2
  316.9 16.5 %copy-start.11 = (s32[2048]{0:T(1024)S(1)}, s32[2048]{0:T(1024)}, u32[]{:S(2)}) copy-start(s32[2048]{0:T(1024)} %broadcast_clamp_fusion.1) | copy-start | bytes 24580
  316.9 37.3 %copy-start.8 = (s32[3840]{0:T(1024)S(1)}, s32[3840]{0:T(1024)}, u32[]{:S(2)}) copy-start(s32[3840]{0:T(1024)} %get-tuple-element.33) | copy-start | bytes 46084
  333.5 39.6 %copy-start.3 = (f32[2,18,66,66]{3,1,2,0:T(8,128)S(1)}, f32[2,18,66,66]{3,1,2,0:T(8,128)}, u32[]{:S(2)}) copy-start(f32[2,18,66,66]{3,1,2,0:T(8,128)} %copy-done.2) | copy-start | bytes 1881796
  350.6 24.2 %all-to-all-start.1 = ((f32[6,8,256]{2,0,1:T(8,128)}), f32[6,8,256]{2,0,1:T(8,128)S(1)}, u32[]{:S(2)}, u32[]{:S(2)}) async-start(f32[6,8,256]{2,0,1:T(8,128)} %copy.163), calls=%async_computation.1 | async-start | bytes 131072 | tf_op jit(solution)/shard_map/all_to_all | solution.py:108
  483.6 108.2 %copy-start.4 = (f32[8,4096]{1,0:T(8,128)S(1)}, f32[8,4096]{1,0:T(8,128)}, u32[]{:S(2)}) copy-start(f32[8,4096]{1,0:T(8,128)} %param.11) | copy-start | bytes 393220
  483.6 108.2 %copy-start.10 = (pred[4096]{0:T(1024)(128)(4,1)S(1)}, pred[4096]{0:T(1024)(128)(4,1)}, u32[]{:S(2)}) copy-start(pred[4096]{0:T(1024)(128)(4,1)} %copy-done.9) | copy-start | bytes 12292
  606.2 0.8 copy-start.7
  607.7 7.9 copy-start
  915.0 3.9 copy-start.1
where the time goes:
time: 933 us; the launch traced here: 923 us
  other arithmetic  492 us (53%)
  local copies, waits for them, and re-layouts  392 us (42%)
  starting transfers between devices  19.1 us (2%)
  waiting for transfers between devices  18.2 us (2%)
    scatter-add x8, other arithmetic, constrain(): moved = moved.at[:, first].add(-shifted).at[:, second].add(shifted)  220 us
    scatter-add x1, other arithmetic, on_device(): jnp.zeros((2, plane * slots), jnp.float32).at[:, flat_slots]  174 us
    gather x1, local copies, waits for them, and re-layouts, on_device(): table[0][:, flat_slots].reshape(3, 8, count)  108 us
    gather x1, local copies, waits for them, and re-layouts, on_device(): table[1][:, flat_slots].reshape(3, 8, count)  108 us
    gather x8, local copies, waits for them, and re-layouts, constrain(): stretch = moved[:, first] - moved[:, second]  72.6 us
    scatter-add x1, other arithmetic, on_device(): jnp.zeros((2, cells), jnp.float32).at[:, flat_cells]  24.6 us
    mul x1, other arithmetic, on_device(): density = density * (CX * CY * CZ / BEADS_DEV)  22.3 us
    gather x2, local copies, waits for them, and re-layouts, constrain(): separation = anchor[:, first] - anchor[:, second]  18.9 us
  transfers between devices with their start and end apart: 8, of which 5 were waited for; matrix products, arithmetic and copies ran while one was open for 3% of the time, Pallas kernels for 0%

commit v1 on v0

--- a/solution.py
+++ b/solution.py
@@ -3,6 +3,8 @@
 import jax
 import jax.numpy as jnp
 from jax import lax
+from jax.experimental import pallas as pl
+from jax.experimental.pallas import tpu as pltpu
 from jax.sharding import PartitionSpec as P
 
 CX = 16
@@ -62,32 +64,242 @@
     return smooth_along(extended_2(field, (("bz", 3),), width), 3)
 
 
-def constrain(anchor, moved, first, second):
-    separation = anchor[:, first] - anchor[:, second]
-    for repeat in range(SWEEPS):
-        stretch = moved[:, first] - moved[:, second]
-        excess = jnp.sum(stretch * stretch, axis=0) - bond_length * bond_length
-        intersection = jnp.maximum(
-            jnp.sum(stretch * separation, axis=0), 0.5 * bond_length * bond_length
-        )
-        factor = excess / (4.0 * intersection)
-        shifted = factor * separation
-        moved = moved.at[:, first].add(-shifted).at[:, second].add(shifted)
-    return moved
-
+LANES = 128
+VMEM_LIMIT = 56 * 1024 * 1024
+f32 = jnp.float32
+bf16 = jnp.bfloat16
+
+
+def parts_of(values, count):
+    parts = []
+    for _ in range(count):
+        part = values.astype(bf16)
+        parts.append(part)
+        values = values - part.astype(f32)
+    return parts
+
+
+def one_hot(index, size):
+    rows = lax.broadcasted_iota(jnp.int32, (size, index.shape[1]), 0)
+    return jnp.where(rows == index, 1.0, 0.0).astype(bf16)
+
+
+def dot_nn(left, right):
+    return lax.dot_general(left, right, (((1,), (0,)), ((), ())), preferred_element_type=f32)
+
+
+def dot_nt(left, right):
+    return lax.dot_general(left, right, (((1,), (1,)), ((), ())), preferred_element_type=f32)
+
+
+def chunk_of(length, most):
+    tiles = length // LANES
+    best = max(t for t in range(1, most + 1) if tiles % t == 0)
+    return best * LANES
+
+
+def corner_keys(species, corner_slot, corner, where, plane, blocks):
+    brick = corner_slot[0, pl.ds(corner, 1), where]
+    slot = corner_slot[1, pl.ds(corner, 1), where]
+    block = slot // LANES
+    high = (species * blocks + block) * plane + brick
+    return high, slot - block * LANES
+
+
+def deposit_kernel(species, corner_slot, corner_weight, packets):
+    plane, slots = packets.shape[1:]
+    blocks = slots // LANES
+    highs = 2 * blocks * plane
+    beads = corner_weight.shape[1]
+    step = chunk_of(beads, 4)
+
+    def body(j, total):
+        where = pl.ds(pl.multiple_of(j * step, step), step)
+        kind = species[:, where]
+        for corner in range(8):
+            high, low = corner_keys(kind, corner_slot, corner, where, plane, blocks)
+            weight = corner_weight[pl.ds(corner, 1), where]
+            rows = lax.broadcasted_iota(jnp.int32, (highs, step), 0) == high
+            left = [jnp.where(rows, p.astype(f32), 0.0).astype(bf16) for p in parts_of(weight, 2)]
+            total = total + dot_nt(jnp.concatenate(left, axis=0), one_hot(low, LANES))
+        return total
+
+    total = lax.fori_loop(0, beads // step, body, jnp.zeros((2 * highs, LANES), f32))
+    total = total[:highs] + total[highs:]
+    for kind in range(2):
+        for block in range(blocks):
+            start = (kind * blocks + block) * plane
+            packets[kind, :, block * LANES : (block + 1) * LANES] = total[start : start + plane]
+
+
+def deposit(species, corner_slot, corner_weight, plane, slots):
+    return pl.pallas_call(
+        deposit_kernel,
+        out_shape=jax.ShapeDtypeStruct((2, plane, slots), f32),
+        compiler_params=pltpu.CompilerParams(vmem_limit_bytes=VMEM_LIMIT),
+    )(species, corner_slot, corner_weight)
+
+
+def to_rows(store, base, row):
+    for tile in range(row.shape[1] // LANES):
+        store[pl.ds(base + tile, 1), :] = row[:, tile * LANES : (tile + 1) * LANES]
+
+
+def finish_kernel(
+    species,
+    corner_slot,
+    corner_weight,
+    slopes,
+    positions,
+    velocities,
+    bonds,
+    new_positions,
+    new_velocities,
+    table,
+    shift,
+    anchor,
+    hot,
+    separation,
+):
+    plane, slots = slopes.shape[1:]
+    blocks = slots // LANES
+    highs = 2 * blocks * plane
+    beads = corner_weight.shape[1]
+    bead_rows = beads // LANES
+    count = bonds.shape[1]
+
+    for axis in range(3):
+        for kind in range(2):
+            for block in range(blocks):
+                start = (axis * 2 * blocks + kind * blocks + block) * plane
+                for at, part in enumerate(
+                    parts_of(slopes[kind * 3 + axis, :, block * LANES : (block + 1) * LANES], 2)
+                ):
+                    table[start : start + plane, at * LANES : (at + 1) * LANES] = part.astype(f32)
+    slope_table = table[...].astype(bf16)
+
+    step = chunk_of(beads, 4)
+
+    def force_body(j, carry):
+        where = pl.ds(pl.multiple_of(j * step, step), step)
+        kind = species[:, where]
+        total = jnp.zeros((3 * highs, step), f32)
+        for corner in range(8):
+            high, low = corner_keys(kind, corner_slot, corner, where, plane, blocks)
+            weight = corner_weight[pl.ds(corner, 1), where]
+            rows = lax.broadcasted_iota(jnp.int32, (highs, step), 0) == high
+            weights = jnp.where(rows, weight, 0.0)
+            hot_low = one_hot(low, LANES)
+            picked = dot_nn(slope_table, jnp.concatenate([hot_low, hot_low], axis=0))
+            total = total + picked * jnp.concatenate([weights] * 3, axis=0)
+        for axis in range(3):
+            force = -jnp.sum(total[axis * highs : (axis + 1) * highs], axis=0, keepdims=True)
+            half = velocities[pl.ds(axis, 1), where] + 0.5 * time_step * force
+            to_rows(shift, axis * bead_rows + j * (step // LANES), time_step * half)
+            to_rows(anchor, axis * bead_rows + j * (step // LANES), positions[pl.ds(axis, 1), where])
+        return carry
+
+    lax.fori_loop(0, beads // step, force_body, 0)
+
+    bond_step = chunk_of(count, 6)
+    bond_rows = 3 * bead_rows
+    anchor_parts = parts_of(anchor[...], 3)
+    anchor_table = jnp.concatenate(anchor_parts, axis=1)
+
+    def ends(side, where):
+        index = bonds[pl.ds(side, 1), where]
+        high = index // LANES
+        return lax.broadcasted_iota(jnp.int32, (bead_rows, bond_step), 0) == high, index - high * LANES
+
+    def select(rows, picked):
+        return [
+            jnp.sum(
+                jnp.where(rows, picked[axis * bead_rows : (axis + 1) * bead_rows], 0.0),
+                axis=0,
+                keepdims=True,
+            )
+            for axis in range(3)
+        ]
+
+    for j in range(count // bond_step):
+        where = slice(j * bond_step, (j + 1) * bond_step)
+        found = []
+        for side in range(2):
+            rows, low = ends(side, where)
+            hot_low = one_hot(low, LANES)
+            hot[side, :, where] = hot_low
+            found.append(select(rows, dot_nn(anchor_table, jnp.concatenate([hot_low] * 3, axis=0))))
+        for axis in range(3):
+            separation[axis : axis + 1, where] = found[0][axis] - found[1][axis]
+
+    def sweep(repeat, carry):
+        shift_table = jnp.concatenate(parts_of(shift[...], 2), axis=1)
+        total = jnp.zeros((2 * bond_rows, LANES), f32)
+        for j in range(count // bond_step):
+            where = slice(j * bond_step, (j + 1) * bond_step)
+            hots = [hot[side, :, where] for side in range(2)]
+            rows = [ends(side, where)[0] for side in range(2)]
+            found = [
+                select(rows[side], dot_nn(shift_table, jnp.concatenate([hots[side]] * 2, axis=0)))
+                for side in range(2)
+            ]
+            apart = [separation[axis : axis + 1, where] for axis in range(3)]
+            stretch = [apart[axis] + (found[0][axis] - found[1][axis]) for axis in range(3)]
+            excess = sum(s * s for s in stretch) - bond_length * bond_length
+            along = sum(s * a for s, a in zip(stretch, apart))
+            factor = excess / (4.0 * jnp.maximum(along, 0.5 * bond_length * bond_length))
+            moves = [parts_of(factor * apart[axis], 2) for axis in range(3)]
+            for side in range(2):
+                sign = 1.0 if side else -1.0
+                left = jnp.concatenate(
+                    [
+                        jnp.where(rows[side], sign * moves[axis][part].astype(f32), 0.0).astype(bf16)
+                        for part in range(2)
+                        for axis in range(3)
+                    ],
+                    axis=0,
+                )
+                total = total + dot_nt(left, hots[side])
+        shift[...] = shift[...] + total[:bond_rows] + total[bond_rows:]
+        return carry
+
+    lax.fori_loop(0, SWEEPS, sweep, 0)
+
+    for axis in range(3):
+        for tile in range(bead_rows):
+            row = slice(axis * bead_rows + tile, axis * bead_rows + tile + 1)
+            where = slice(tile * LANES, (tile + 1) * LANES)
+            move = shift[row, :]
+            new_positions[axis : axis + 1, where] = anchor[row, :] + move
+            new_velocities[axis : axis + 1, where] = move / time_step
+
+
+def finish(species, corner_slot, corner_weight, slopes, positions, velocities, bonds):
+    beads = positions.shape[1]
+    count = bonds.shape[1]
+    plane, slots = slopes.shape[1:]
+    highs = 2 * (slots // LANES) * plane
+    return pl.pallas_call(
+        finish_kernel,
+        out_shape=[jax.ShapeDtypeStruct((3, beads), f32)] * 2,
+        scratch_shapes=[
+            pltpu.VMEM((3 * highs, 2 * LANES), f32),
+            pltpu.VMEM((3 * beads // LANES, LANES), f32),
+            pltpu.VMEM((3 * beads // LANES, LANES), f32),
+            pltpu.VMEM((2, LANES, count), bf16),
+            pltpu.VMEM((3, count), f32),
+        ],
+        compiler_params=pltpu.CompilerParams(vmem_limit_bytes=VMEM_LIMIT),
+    )(species, corner_slot, corner_weight, slopes, positions, velocities, bonds)
 
 def on_device(positions, velocities, species, corner_slot, corner_weight, slot_cell, bond_pairs):
     plane = slot_cell.shape[1]
     slots = slot_cell.shape[2]
     cells = CX * CY * CZ
-    is_lipid = (species == 0)[None, :]
-    flat_slots = (corner_slot[0] * slots + corner_slot[1]).reshape(-1)
-    both = jnp.stack(
-        [jnp.where(is_lipid, corner_weight, 0.0), jnp.where(is_lipid, 0.0, corner_weight)]
-    )
-    packets = jnp.zeros((2, plane * slots), jnp.float32).at[:, flat_slots].add(both.reshape(2, -1))
+    species = species.reshape(1, -1)
+    packets = deposit(species, corner_slot, corner_weight, plane, slots)
     received = lax.all_to_all(
-        packets.reshape(2, plane, slots), ("bx", "by"), split_axis=1, concat_axis=1, tiled=True
+        packets, ("bx", "by"), split_axis=1, concat_axis=1, tiled=True
     )
     flat_cells = ((slot_cell[0] * CY + slot_cell[1]) * CZ + slot_cell[2]).reshape(-1)
     density = jnp.zeros((2, cells), jnp.float32).at[:, flat_cells].add(received.reshape(2, -1))
@@ -108,18 +320,9 @@
     returned = lax.all_to_all(
         outgoing.reshape(6, plane, slots), ("bx", "by"), split_axis=1, concat_axis=1, tiled=True
     )
-    table = returned.reshape(2, 3, plane * slots)
-    count = corner_weight.shape[1]
-    picked = jnp.where(
-        is_lipid[None],
-        table[0][:, flat_slots].reshape(3, 8, count),
-        table[1][:, flat_slots].reshape(3, 8, count),
-    )
-    force = -jnp.sum(corner_weight[None] * picked, axis=1)
-    half = velocities + 0.5 * time_step * force
-    moved = positions + time_step * half
-    moved = constrain(positions, moved, bond_pairs[0], bond_pairs[1])
-    new_velocities = (moved - positions) / time_step
+    moved, new_velocities = finish(
+        species, corner_slot, corner_weight, returned, positions, velocities, bond_pairs
+    )
     return (moved, new_velocities, smoothed)
 
 

time: 933 us -> 201 us (0.22)
  other arithmetic: 492 us -> 61.6 us
  local copies, waits for them, and re-layouts: 392 us -> 67.8 us
  Pallas kernels: 0 us -> 24.5 us
  waiting for transfers between devices: 18.2 us -> 28.1 us
    scatter-add x9 -> x0, other arithmetic: 395 us -> none  [the longest x8 220 us: constrain(): moved = moved.at[:, first].add(-shifted).at[:, second].add(shifted)]
    gather x12 -> x0, local copies, waits for them, and re-layouts: 308 us -> none  [the longest x1 108 us: on_device(): table[0][:, flat_slots].reshape(3, 8, count)]
    reduce_sum x5 -> x0, other arithmetic: 28.4 us -> none  [the longest x1 14.3 us: on_device(): force = -jnp.sum(corner_weight[None] * picked, axis=1)]
    pallas_call x0 -> x2, Pallas kernels: none -> 24.5 us  [the longest x1 18.9 us: finish(): pl.pallas_call(finish_kernel, out_shape=[jax.ShapeDtypeStruct((3, beads),...]
  transfers between devices with their start and end apart: 8 -> 8, of which waited for: 5 -> 7; matrix products, arithmetic and copies ran while one was open for 3% -> 2% of each run, Pallas kernels for 0% -> 0%
where the time goes in v1:
time: 201 us; the launch traced here: 200 us
  local copies, waits for them, and re-layouts  67.8 us (34%)
  other arithmetic  61.6 us (31%)
  waiting for transfers between devices  28.1 us (14%)
  Pallas kernels  24.5 us (12%)
  starting transfers between devices  17.7 us (9%)
    scatter-add x1, other arithmetic, on_device(): jnp.zeros((2, cells), jnp.float32).at[:, flat_cells]  24.6 us
    mul x1, other arithmetic, on_device(): density = density * (CX * CY * CZ / BEADS_DEV)  22.3 us
    pallas_call x1, Pallas kernels, finish(): pl.pallas_call(finish_kernel, out_shape=[jax.ShapeDtypeStruct((3, beads),...  18.9 us
    reshape x2, local copies, waits for them, and re-layouts, on_device(): slopes = jnp.stack([slope_x, slope_y, slope_z], axis=1).reshape(6, cells)  18.7 us
    reshape x1, local copies, waits for them, and re-layouts, on_device(): density = density.reshape(2, CX, CY, CZ)  18.1 us
    gather x1, local copies, waits for them, and re-layouts, on_device(): outgoing = slopes[:, flat_cells]  16.1 us
    ppermute x3, waiting for transfers between devices, extended_2(): lax.ppermute(tail, axis, [(i, (i + 1) % count) for i in range(count)])  14.5 us
    add x3, other arithmetic, smooth_along(): result + taps[offset] * lax.slice_in_dim(extended, offset, offset + lengt...  12 us
  transfers between devices with their start and end apart: 8, of which 7 were waited for; matrix products, arithmetic and copies ran while one was open for 2% of the time, Pallas kernels for 0%

profile of v1, /device:TPU:0, one launch (start us, length us, event | category | flops | bytes accessed | tf_op | source)
XLA Modules:
  0.0 200.4 jit_solution(12398691676395135382)
XLA Ops:
  0.6 5.6 %shard_map.94 = f32[2,8,256]{2,1,0:T(8,128)} custom-call(s32[1,4096]{1,0:T(1,128)} %bitcast.24, s32[2,8,4096]{2,1,0:T(8,128)} %corner_slot.3, f32[8,4096]{1,0:T(8,128)} %corner_weight.3), custom_call_target="tpu_custom_call" | custom-call | tf_op jit(solution)/shard_map/pallas_call | solution.py:136
  6.2 1.3 copy.50
  7.6 7.3 %all-to-all-start = ((f32[2,8,256]{2,0,1:T(2,128)}), f32[2,8,256]{2,0,1:T(2,128)S(1)}, u32[]{:S(2)}, u32[]{:S(2)}) async-start(f32[2,8,256]{2,0,1:T(2,128)} %copy.50), calls=%async_computation | async-start | bytes 32768 | tf_op jit(solution)/shard_map/all_to_all | solution.py:301
  15.6 5.8 %all-to-all-done = f32[2,8,256]{2,0,1:T(2,128)S(1)} async-done(((f32[2,8,256]{2,0,1:T(2,128)}), f32[2,8,256]{2,0,1:T(2,128)S(1)}, u32[]{:S(2)}, u32[]{:S(2)}) %all-to-all-start) | async-done | bytes 16416 | tf_op jit(solution)/shard_map/all_to_all | solution.py:301
  21.8 24.6 %scatter_custom_fusion = f32[2,65536]{0,1:T(8,128)} fusion(s32[2048]{0:T(1024)S(1)} %bitcast.26, f32[2048,2]{1,0:T(8,128)S(1)} %copy.51, f32[]{:T(128)} %constant.12.clone.1), kind=kCustom, calls=%fused_computation.3 | custom fusion | flops 4096 | bytes 524292 | tf_op jit(solution)/shard_map/scatter-add | solution.py:305
  46.4 22.3 %broadcast_multiply_fusion = f32[2,65536]{0,1:T(8,128)} fusion(f32[2,65536]{0,1:T(8,128)} %scatter_custom_fusion), kind=kLoop, calls=%fused_computation.2 | loop fusion | flops 131072 | bytes 1048576 | tf_op jit(solution)/shard_map/mul | solution.py:306
  68.7 18.1 %copy.52 = f32[2,16,64,64]{3,1,2,0:T(8,128)S(1)} copy(f32[2,16,64,64]{0,3,2,1:T(8,128)} %bitcast.21) | data formatting | bytes 1048576 | tf_op jit(solution)/shard_map/reshape | solution.py:307
  87.5 3.3 %collective-permute-start.1 = (f32[2,4,64,64]{3,1,2,0:T(4,128)S(1)}, f32[2,4,64,64]{3,1,2,0:T(4,128)S(1)}, u32[]{:S(2)}, u32[]{:S(2)}) collective-permute-start(f32[2,4,64,64]{3,1,2,0:T(4,128)S(1)} %get-tuple-element.26), channel_id=1, source_target_pairs={{8,0},{16,8},{24,16},{0,24},{9,1},{17,9},{25,17},{1,25},{10,2},{18... | collective-permute-start | bytes 393224 | tf_op jit(solution)/shard_map/ppermute | solution.py:34
  90.8 7.2 %collective-permute-done = f32[2,4,64,64]{3,1,2,0:T(4,128)S(1)} collective-permute-done((f32[2,4,64,64]{3,1,2,0:T(4,128)S(1)}, f32[2,4,64,64]{3,1,2,0:T(4,128)S(1)}, u32[]{:S(2)}, u32[]{:S(2)}) %collective-permute-start) | collective-permute-done | bytes 131104 | tf_op jit(solution)/shard_map/ppermute | solution.py:32
  98.1 1.4 collective-permute-done.1
  99.4 1.9 fusion.31
  102.2 1.4 collective-permute-start.3
  103.5 2.6 %collective-permute-done.2 = f32[2,18,4,64]{3,1,2,0:T(8,128)S(1)} collective-permute-done((f32[2,18,4,64]{3,1,2,0:T(8,128)S(1)}, f32[2,18,4,64]{3,1,2,0:T(8,128)S(1)}, u32[]{:S(2)}, u32[]{:S(2)}) %collective-permute-start.2) | collective-permute-done | bytes 36896 | tf_op jit(solution)/shard_map/ppermute | solution.py:32
  106.1 1.1 collective-permute-done.3
  107.2 1.4 fusion.5
  108.6 1.7 fusion.59
  110.3 2.0 %copy.57 = f32[2,18,66,4]{2,1,3,0:T(8,128)S(1)} copy(f32[2,18,66,4]{3,1,2,0:T(8,128)} %get-tuple-element.21) | data formatting | bytes 76032 | tf_op jit(solution)/shard_map/slice | solution.py:29
  113.5 4.7 %collective-permute-done.4 = f32[2,18,66,4]{2,1,3,0:T(8,128)} collective-permute-done((f32[2,18,66,4]{2,1,3,0:T(8,128)S(1)}, f32[2,18,66,4]{2,1,3,0:T(8,128)}, u32[]{:S(2)}, u32[]{:S(2)}) %collective-permute-start.4) | collective-permute-done | bytes 38048 | tf_op jit(solution)/shard_map/ppermute | solution.py:32
  118.2 1.6 copy.58
  119.8 1.9 copy.61
  121.7 8.7 %fusion.17 = f32[2,18,66,66]{3,1,2,0:T(8,128)S(1)} fusion(f32[2,18,66,4]{3,1,2,0:T(8,128)} %copy.61, f32[2,18,66,64]{3,1,2,0:T(8,128)S(1)} %fusion.5, f32[2,18,66,4]{3,1,2,0:T(8,128)S(1)} %copy.58), kind=kLoop, calls=%fused_computation.44 | loop fusion | flops 3293136 | bytes 1311552 | tf_op jit(solution)/shard_map/add | solution.py:54
  130.5 1.0 copy-done
  131.5 1.4 fusion.52
  133.3 1.0 copy.63
  134.3 2.3 %reshape.76 = f32[6,65536]{1,0:T(8,128)} reshape(f32[2,3,16,64,64]{4,3,2,1,0:T(8,128)S(1)} %copy.63) | data formatting | bytes 3145728 | tf_op jit(solution)/shard_map/reshape | solution.py:318
  136.6 16.4 %copy.64 = f32[6,65536]{0,1:T(8,128)} copy(f32[6,65536]{1,0:T(8,128)} %reshape.76) | data formatting | bytes 3145728 | tf_op jit(solution)/shard_map/reshape | solution.py:318
  153.0 16.1 %gather_fusion = f32[2048,6]{1,0:T(8,128)S(1)} fusion(f32[6,65536]{0,1:T(8,128)} %copy.64, s32[2048]{0:T(1024)S(1)} %broadcast_clamp_fusion), kind=kCustom, calls=%fused_computation | custom fusion | bytes 106496 | tf_op jit(solution)/shard_map/gather | solution.py:319
  169.1 1.0 copy.65
  170.1 3.9 %all-to-all-start.1 = ((f32[6,8,256]{2,0,1:T(8,128)}), f32[6,8,256]{2,0,1:T(8,128)S(1)}, u32[]{:S(2)}, u32[]{:S(2)}) async-start(f32[6,8,256]{2,0,1:T(8,128)} %copy.65), calls=%async_computation.1 | async-start | bytes 131072 | tf_op jit(solution)/shard_map/all_to_all | solution.py:320
  174.3 1.3 copy.67
  175.6 5.3 %all-to-all-done.1 = f32[6,8,256]{2,0,1:T(8,128)S(1)} async-done(((f32[6,8,256]{2,0,1:T(8,128)}), f32[6,8,256]{2,0,1:T(8,128)S(1)}, u32[]{:S(2)}, u32[]{:S(2)}) %all-to-all-start.1) | async-done | bytes 49184 | tf_op jit(solution)/shard_map/all_to_all | solution.py:320
  181.5 18.9 %shard_map.95 = (f32[3,4096]{1,0:T(4,128)}, f32[3,4096]{1,0:T(4,128)}) custom-call(s32[1,4096]{1,0:T(1,128)} %bitcast.25, s32[2,8,4096]{2,1,0:T(8,128)} %corner_slot.3, f32[8,4096]{1,0:T(8,128)} %corner_weight.3, f32[6,8,256]{2,1,0:T(8,128)} %copy.66.slopes, f32[3,4096]{1,0:T(4,128)} %positions.1, f32[3,4096]{1,0:T(4,128)} %velocities.1, s32[2,3840]{1,0:T(2,128)} %bonds.1), custom_call_target="tpu_custom_call" | custom-call | tf_op jit(solution)/shard_map/pallas_call | solution.py:282
  (20 shorter events, 5.1 us)
Async XLA Ops:
  7.6 13.9 %all-to-all-start = ((f32[2,8,256]{2,0,1:T(2,128)}), f32[2,8,256]{2,0,1:T(2,128)S(1)}, u32[]{:S(2)}, u32[]{:S(2)}) async-start(f32[2,8,256]{2,0,1:T(2,128)} %copy.50), calls=%async_computation | async-start | bytes 32768 | tf_op jit(solution)/shard_map/all_to_all | solution.py:301
  87.0 11.1 %collective-permute-start = (f32[2,4,64,64]{3,1,2,0:T(4,128)S(1)}, f32[2,4,64,64]{3,1,2,0:T(4,128)S(1)}, u32[]{:S(2)}, u32[]{:S(2)}) collective-permute-start(f32[2,4,64,64]{3,1,2,0:T(4,128)S(1)} %get-tuple-element.25), channel_id=1, source_target_pairs={{0,8},{8,16},{16,24},{24,0},{1,9},{9,17},{17,25},{25,1},{2,10},{10... | collective-permute-start | bytes 393224 | tf_op jit(solution)/shard_map/ppermute | solution.py:32
  87.5 12.0 %collective-permute-start.1 = (f32[2,4,64,64]{3,1,2,0:T(4,128)S(1)}, f32[2,4,64,64]{3,1,2,0:T(4,128)S(1)}, u32[]{:S(2)}, u32[]{:S(2)}) collective-permute-start(f32[2,4,64,64]{3,1,2,0:T(4,128)S(1)} %get-tuple-element.26), channel_id=1, source_target_pairs={{8,0},{16,8},{24,16},{0,24},{9,1},{17,9},{25,17},{1,25},{10,2},{18... | collective-permute-start | bytes 393224 | tf_op jit(solution)/shard_map/ppermute | solution.py:34
  101.4 4.7 %collective-permute-start.2 = (f32[2,18,4,64]{3,1,2,0:T(8,128)S(1)}, f32[2,18,4,64]{3,1,2,0:T(8,128)S(1)}, u32[]{:S(2)}, u32[]{:S(2)}) collective-permute-start(f32[2,18,4,64]{3,1,2,0:T(8,128)S(1)} %get-tuple-element.23), channel_id=1, source_target_pairs={{0,4},{4,0},{1,5},{5,1},{2,6},{6,2},{3,7},{7,3},{8,12},{12,8},{9,1... | collective-permute-start | bytes 110600 | tf_op jit(solution)/shard_map/ppermute | solution.py:32
  102.2 5.0 %collective-permute-start.3 = (f32[2,18,4,64]{3,1,2,0:T(8,128)S(1)}, f32[2,18,4,64]{3,1,2,0:T(8,128)S(1)}, u32[]{:S(2)}, u32[]{:S(2)}) collective-permute-start(f32[2,18,4,64]{3,1,2,0:T(8,128)S(1)} %get-tuple-element.24), channel_id=1, source_target_pairs={{4,0},{0,4},{5,1},{1,5},{6,2},{2,6},{7,3},{3,7},{12,8},{8,12},{13,... | collective-permute-start | bytes 110600 | tf_op jit(solution)/shard_map/ppermute | solution.py:34
  113.0 6.9 %collective-permute-start.5 = (f32[2,18,66,4]{2,1,3,0:T(8,128)S(1)}, f32[2,18,66,4]{2,1,3,0:T(8,128)S(1)}, u32[]{:S(2)}, u32[]{:S(2)}) collective-permute-start(f32[2,18,66,4]{2,1,3,0:T(8,128)S(1)} %copy.59), channel_id=1, source_target_pairs={{1,0},{2,1},{3,2},{0,3},{5,4},{6,5},{7,6},{4,7},{9,8},{10,9},{11,1... | collective-permute-start | bytes 114056 | tf_op jit(solution)/shard_map/ppermute | solution.py:34
  113.0 5.2 %collective-permute-start.4 = (f32[2,18,66,4]{2,1,3,0:T(8,128)S(1)}, f32[2,18,66,4]{2,1,3,0:T(8,128)}, u32[]{:S(2)}, u32[]{:S(2)}) collective-permute-start(f32[2,18,66,4]{2,1,3,0:T(8,128)S(1)} %copy.57), channel_id=1, source_target_pairs={{0,1},{1,2},{2,3},{3,0},{4,5},{5,6},{6,7},{7,4},{8,9},{9,10},{10,1... | collective-permute-start | bytes 114056 | tf_op jit(solution)/shard_map/ppermute | solution.py:32
  130.4 1.2 copy-start
  153.0 21.0 %copy-start.1 = (f32[2,18,66,66]{3,1,2,0:T(8,128)S(1)}, f32[2,18,66,66]{3,1,2,0:T(8,128)}, u32[]{:S(2)}) copy-start(f32[2,18,66,66]{3,1,2,0:T(8,128)} %copy-done) | copy-start | bytes 1881796
  170.1 10.8 %all-to-all-start.1 = ((f32[6,8,256]{2,0,1:T(8,128)}), f32[6,8,256]{2,0,1:T(8,128)S(1)}, u32[]{:S(2)}, u32[]{:S(2)}) async-start(f32[6,8,256]{2,0,1:T(8,128)} %copy.65), calls=%async_computation.1 | async-start | bytes 131072 | tf_op jit(solution)/shard_map/all_to_all | solution.py:320

commit v2 on v1

--- a/solution.py
+++ b/solution.py
@@ -1,3 +1,4 @@
+import functools
 import math
 
 import jax
@@ -22,46 +23,12 @@
 bond_length = 1.0
 
 
-def extended_2(cells, sides, width):
-    for axis, dim in sides:
-        count = lax.axis_size(axis)
-        head = lax.slice_in_dim(cells, 0, width, axis=dim)
-        tail = lax.slice_in_dim(cells, cells.shape[dim] - width, cells.shape[dim], axis=dim)
-        cells = jnp.concatenate(
-            [
-                lax.ppermute(tail, axis, [(i, (i + 1) % count) for i in range(count)]),
-                cells,
-                lax.ppermute(head, axis, [((i + 1) % count, i) for i in range(count)]),
-            ],
-            axis=dim,
-        )
-    return cells
-
-
 def gauss_taps():
     raw_list = [
         math.exp(-0.5 * (offset - REACH) ** 2 / spread_cells**2) for offset in range(2 * REACH + 1)
     ]
     tap_total = sum(raw_list)
     return [entry / tap_total for entry in raw_list]
-
-
-def smooth_along(extended, axis):
-    taps = gauss_taps()
-    length = extended.shape[axis] - 2 * REACH
-    result = jnp.zeros_like(lax.slice_in_dim(extended, 0, length, axis=axis))
-    for offset in range(2 * REACH + 1):
-        result = result + taps[offset] * lax.slice_in_dim(
-            extended, offset, offset + length, axis=axis
-        )
-    return result
-
-
-def smooth_brick(density, margin):
-    width = REACH + margin
-    field = smooth_along(extended_2(density, (("bx", 1),), width), 1)
-    field = smooth_along(extended_2(field, (("by", 2),), width), 2)
-    return smooth_along(extended_2(field, (("bz", 3),), width), 3)
 
 
 LANES = 128
@@ -106,12 +73,13 @@
     return high, slot - block * LANES
 
 
-def deposit_kernel(species, corner_slot, corner_weight, packets):
-    plane, slots = packets.shape[1:]
+def deposit_kernel(bricks, species, corner_slot, corner_weight, packets, sums):
+    plane, _, slots = packets.shape
     blocks = slots // LANES
     highs = 2 * blocks * plane
     beads = corner_weight.shape[1]
     step = chunk_of(beads, 4)
+    count_x, count_y = bricks.counts
 
     def body(j, total):
         where = pl.ds(pl.multiple_of(j * step, step), step)
@@ -125,19 +93,284 @@
         return total
 
     total = lax.fori_loop(0, beads // step, body, jnp.zeros((2 * highs, LANES), f32))
-    total = total[:highs] + total[highs:]
-    for kind in range(2):
-        for block in range(blocks):
-            start = (kind * blocks + block) * plane
-            packets[kind, :, block * LANES : (block + 1) * LANES] = total[start : start + plane]
-
-
-def deposit(species, corner_slot, corner_weight, plane, slots):
+    sums[...] = total[:highs] + total[highs:]
+
+    def hand_out(target, carry):
+        for near, (step_x, step_y) in enumerate(bricks.offsets):
+            brick = lax.rem(target // count_y + step_x, count_x) * count_y + lax.rem(
+                lax.rem(target, count_y) + step_y, count_y
+            )
+            for kind in range(2):
+                for block in range(blocks):
+                    packets[target, near * 2 + kind : near * 2 + kind + 1, block * LANES : (block + 1) * LANES] = sums[
+                        pl.ds((kind * blocks + block) * plane + brick, 1), :
+                    ]
+        return carry
+
+    lax.fori_loop(0, plane, hand_out, 0, unroll=plane <= 8)
+
+
+def deposit(bricks, species, corner_slot, corner_weight, plane, slots):
     return pl.pallas_call(
-        deposit_kernel,
-        out_shape=jax.ShapeDtypeStruct((2, plane, slots), f32),
+        functools.partial(deposit_kernel, bricks),
+        out_shape=jax.ShapeDtypeStruct((plane, 2 * len(bricks.offsets), slots), f32),
+        scratch_shapes=[pltpu.VMEM((2 * slots // LANES * plane, LANES), f32)],
         compiler_params=pltpu.CompilerParams(vmem_limit_bytes=VMEM_LIMIT),
     )(species, corner_slot, corner_weight)
+
+
+HALO = REACH + 1
+PAD = 8
+
+
+class Bricks:
+    def __init__(self, count_x, count_y):
+        self.counts = (count_x, count_y)
+        self.sides_x = self.sides(count_x)
+        self.sides_y = self.sides(count_y)
+        self.offsets = [(x, y) for y in self.sides_y for x in self.sides_x]
+
+    @staticmethod
+    def sides(count):
+        found = {}
+        for side in (0, 1, -1):
+            found.setdefault(side % count, []).append(side)
+        return found
+
+
+def tap_of(distance):
+    taps = gauss_taps()
+    result = jnp.zeros(distance.shape, f32)
+    for far in range(REACH, -1, -1):
+        result = jnp.where(distance == far, taps[REACH + far], result)
+    return result
+
+
+def filter_rows(load):
+    taps = gauss_taps()
+    result = taps[REACH] * load(REACH)
+    for far in range(1, REACH + 1):
+        result = result + taps[REACH + far] * (load(REACH - far) + load(REACH + far))
+    return result
+
+
+def fill_kernel(bricks, group, received, *refs):
+    places = refs[: len(bricks.offsets)]
+    field, below, above, columns, edge_columns, edges = refs[len(bricks.offsets) :]
+    plane, _, slots = received.shape
+    scale = CX * CY * CZ / BEADS_DEV
+    edges[...] = jnp.zeros_like(edges)
+    if plane > group:
+        field[...] = jnp.zeros_like(field)
+
+    def put(ref, index, value):
+        if plane > group:
+            value = value + ref[index]
+        ref[index] = value
+
+    def sources(g, carry):
+        for near, (step_x, step_y) in enumerate(bricks.offsets):
+            place = places[near]
+            cells_xy = []
+            for p in range(group):
+                row = pl.ds(g * group + p, 1)
+                cells_xy.append((place[0, row, :], place[1, row, :]))
+                z = place[2, row, :]
+                amounts = [scale * received[g * group + p, near * 2 + k : near * 2 + k + 1, :] for k in range(2)]
+                tap = tap_of(jnp.abs(lax.broadcasted_iota(jnp.int32, (CZ, slots), 0) - z))
+                lane = slice(p * slots, (p + 1) * slots)
+                for k in range(2):
+                    for at, part in enumerate(parts_of(tap * amounts[k], 2)):
+                        columns[at * 2 * CZ + k * CZ : at * 2 * CZ + (k + 1) * CZ, lane] = part
+                row_of = lax.broadcasted_iota(jnp.int32, (4 * HALO, slots), 0)
+                layer = row_of % HALO
+                layer = jnp.where(row_of < 2 * HALO, layer - REACH, layer + (CZ - 1))
+                amount = jnp.where((row_of // HALO) % 2 == 0, amounts[0], amounts[1])
+                edge = tap_of(jnp.abs(layer - z)) * amount
+                for at, part in enumerate(parts_of(edge, 2)):
+                    edge_columns[at * 4 * HALO : (at + 1) * 4 * HALO, lane] = part
+            for side_x in bricks.sides_x[step_x]:
+                first_x, width_x, from_x = {
+                    0: (HALO, CX, 0),
+                    1: (HALO + CX, HALO, 0),
+                    -1: (0, HALO, CX - HALO),
+                }[side_x]
+                for side_y in bricks.sides_y[step_y]:
+                    first_y, width_y, from_y, lane_y = {
+                        0: (PAD, CY, 0, 0),
+                        1: (PAD + CY, PAD, 0, CY),
+                        -1: (0, PAD, CY - PAD, LANES - PAD),
+                    }[side_y]
+                    keys = [
+                        jnp.where(
+                            (y >= from_y) & (y < from_y + width_y), (x - from_x) * width_y + (y - from_y), -1
+                        )
+                        for x, y in cells_xy
+                    ]
+                    layers = min(width_x, 256 // width_y)
+                    rows = layers * width_y
+                    for start in range(0, width_x, layers):
+                        hot = jnp.concatenate(
+                            [one_hot(key - start * width_y, rows) for key in keys], axis=1
+                        )
+                        sums = dot_nt(hot, columns[...])
+                        sums = sums[:, : 2 * CZ] + sums[:, 2 * CZ :]
+                        outer = dot_nt(edge_columns[...], hot)
+                        outer = outer[: 4 * HALO] + outer[4 * HALO :]
+                        for layer in range(layers):
+                            at = first_x + start + layer
+                            piece = slice(layer * width_y, (layer + 1) * width_y)
+                            put(field, (at, slice(first_y, first_y + width_y), slice(None)), sums[piece])
+                            put(edges, (at, slice(None), slice(lane_y, lane_y + width_y)), outer[:, piece])
+        return carry
+
+    lax.fori_loop(0, plane // group, sources, 0)
+
+    for layer in range(CX + 2):
+        along_x = filter_rows(lambda j: edges[layer + j])
+        both = filter_rows(lambda j: pltpu.roll(along_x, (REACH - j) % LANES, 1))
+        below[layer] = both[: 2 * HALO]
+        above[layer] = both[2 * HALO :]
+
+
+def fill(bricks, received, places):
+    plane, _, slots = received.shape
+    group = 8 if plane % 8 == 0 else plane
+    return pl.pallas_call(
+        functools.partial(fill_kernel, bricks, group),
+        out_shape=[
+            jax.ShapeDtypeStruct((CX + 2 * HALO, CY + 2 * PAD, 2 * CZ), f32),
+            jax.ShapeDtypeStruct((CX + 2, 2 * HALO, LANES), f32),
+            jax.ShapeDtypeStruct((CX + 2, 2 * HALO, LANES), f32),
+        ],
+        scratch_shapes=[
+            pltpu.VMEM((4 * CZ, group * slots), bf16),
+            pltpu.VMEM((8 * HALO, group * slots), bf16),
+            pltpu.VMEM((CX + 2 * HALO, 4 * HALO, LANES), f32),
+        ],
+        compiler_params=pltpu.CompilerParams(vmem_limit_bytes=VMEM_LIMIT),
+    )(received, *places)
+
+
+def smooth_kernel(field, below, above, turned, line):
+    line[...] = jnp.zeros_like(line)
+    wide = CY + PAD
+    for layer in range(CX + 2):
+        line[PAD : PAD + CY + 2 * PAD, :] = filter_rows(lambda j: field[layer + j])
+        main = filter_rows(lambda j: line[2 * PAD + j - REACH : 2 * PAD + j - REACH + wide, :])
+        before = filter_rows(lambda j: line[PAD + j - REACH : 2 * PAD + j - REACH, :])
+        rest = jnp.zeros((LANES - wide - PAD, 2 * CZ), f32)
+        flipped = jnp.concatenate([main, rest, before], axis=0).T
+        for k in range(2):
+            turned[layer, k, PAD : PAD + CZ, :] = flipped[k * CZ : (k + 1) * CZ]
+            turned[layer, k, PAD - 1 : PAD, :] = below[layer, k * HALO + REACH - 1 : k * HALO + REACH, :]
+            turned[layer, k, PAD + CZ : PAD + CZ + 1, :] = above[layer, k * HALO + 1 : k * HALO + 2, :]
+
+
+def smooth(field, below, above):
+    return pl.pallas_call(
+        smooth_kernel,
+        out_shape=jax.ShapeDtypeStruct((CX + 2, 2, CZ + 2 * PAD, LANES), f32),
+        scratch_shapes=[pltpu.VMEM((CY + 5 * PAD, 2 * CZ), f32)],
+        compiler_params=pltpu.CompilerParams(vmem_limit_bytes=VMEM_LIMIT),
+    )(field, below, above)
+
+
+def slope_kernel(turned, from_below, from_above, place, slopes, whole, table):
+    plane, _, slots = slopes.shape
+    lanes = lax.broadcasted_iota(jnp.int32, (CZ, LANES), 1)
+    for layer in range(CX + 2):
+        for k in range(2):
+            whole[layer, k] = turned[layer, k]
+            at = slice(PAD - 1, PAD - 1 + HALO)
+            whole[layer, k, at, :] = whole[layer, k, at, :] + from_below[layer, k * HALO : (k + 1) * HALO, :]
+            at = slice(PAD + CZ - REACH, PAD + CZ - REACH + HALO)
+            whole[layer, k, at, :] = whole[layer, k, at, :] + from_above[layer, k * HALO : (k + 1) * HALO, :]
+    for pair in range(CX // 2):
+        for k in range(2):
+            halves = []
+            for layer in (1 + 2 * pair, 2 + 2 * pair):
+                inner = slice(PAD, PAD + CZ)
+                here = whole[layer, k, inner, :]
+                halves.append(
+                    (
+                        whole[layer + 1, k, inner, :] - whole[layer - 1, k, inner, :],
+                        pltpu.roll(here, LANES - 1, 1) - pltpu.roll(here, 1, 1),
+                        whole[layer, k, PAD + 1 : PAD + 1 + CZ, :] - whole[layer, k, PAD - 1 : PAD - 1 + CZ, :],
+                    )
+                )
+            for axis in range(3):
+                both = 0.5 * jnp.where(lanes < CY, halves[0][axis], pltpu.roll(halves[1][axis], CY, 1))
+                for at, part in enumerate(parts_of(both, 2)):
+                    start = at * CX * CY + pair * LANES
+                    table[(axis * 2 + k) * CZ : (axis * 2 + k + 1) * CZ, start : start + LANES] = part
+
+    def source(p, carry):
+        row = pl.ds(p, 1)
+        hot = one_hot(place[0, row, :] * CY + place[1, row, :], CX * CY)
+        picked = dot_nn(table[:, : CX * CY], hot) + dot_nn(table[:, CX * CY :], hot)
+        depth = lax.broadcasted_iota(jnp.int32, (CZ, slots), 0) == place[2, row, :]
+        for axis in range(3):
+            steep = [
+                jnp.sum(
+                    jnp.where(depth, picked[(axis * 2 + k) * CZ : (axis * 2 + k + 1) * CZ], 0.0),
+                    axis=0,
+                    keepdims=True,
+                )
+                for k in range(2)
+            ]
+            joint = stiffness * (steep[0] + steep[1])
+            for k in range(2):
+                slopes[p, k * 3 + axis : k * 3 + axis + 1, :] = mixing * steep[1 - k] + joint
+        return carry
+
+    lax.fori_loop(0, plane, source, 0)
+
+
+def pick_slopes(turned, from_below, from_above, place):
+    plane, slots = place.shape[1:]
+    return pl.pallas_call(
+        slope_kernel,
+        out_shape=[
+            jax.ShapeDtypeStruct((plane, 6, slots), f32),
+            jax.ShapeDtypeStruct(turned.shape, f32),
+        ],
+        scratch_shapes=[pltpu.VMEM((6 * CZ, 2 * CX * CY), bf16)],
+        compiler_params=pltpu.CompilerParams(vmem_limit_bytes=VMEM_LIMIT),
+    )(turned, from_below, from_above, place)
+
+
+def smoothed_kernel(whole, smoothed):
+    for layer in range(CX):
+        for k in range(2):
+            smoothed[k, layer] = whole[layer + 1, k, PAD : PAD + CZ, :].T[:CY]
+
+
+def smoothed_of(whole):
+    return pl.pallas_call(
+        smoothed_kernel,
+        out_shape=jax.ShapeDtypeStruct((2, CX, CY, CZ), f32),
+        compiler_params=pltpu.CompilerParams(vmem_limit_bytes=VMEM_LIMIT),
+    )(whole)
+
+
+def shifted(values, axis, step):
+    count = lax.axis_size(axis)
+    return lax.ppermute(values, axis, [((i + step) % count, i) for i in range(count)])
+
+
+def near_places(slot_cell, bricks):
+    found = {}
+    for step_y in bricks.sides_y:
+        for step_x in bricks.sides_x:
+            values = slot_cell if step_x == 0 else found[step_x, 0] if step_y else shifted(slot_cell, "bx", step_x)
+            found[step_x, step_y] = values
+        if step_y:
+            across = [found[step_x, 0] for step_x in bricks.sides_x]
+            moved = shifted(jnp.concatenate(across, axis=0), "by", step_y)
+            for at, step_x in enumerate(bricks.sides_x):
+                found[step_x, step_y] = moved[3 * at : 3 * at + 3]
+    return [found[offset] for offset in bricks.offsets]
 
 
 def to_rows(store, base, row):
@@ -161,22 +394,24 @@
     hot,
     separation,
 ):
-    plane, slots = slopes.shape[1:]
+    plane, _, slots = slopes.shape
     blocks = slots // LANES
     highs = 2 * blocks * plane
     beads = corner_weight.shape[1]
     bead_rows = beads // LANES
     count = bonds.shape[1]
 
-    for axis in range(3):
-        for kind in range(2):
-            for block in range(blocks):
-                start = (axis * 2 * blocks + kind * blocks + block) * plane
-                for at, part in enumerate(
-                    parts_of(slopes[kind * 3 + axis, :, block * LANES : (block + 1) * LANES], 2)
-                ):
-                    table[start : start + plane, at * LANES : (at + 1) * LANES] = part.astype(f32)
-    slope_table = table[...].astype(bf16)
+    def collect(brick, carry):
+        for axis in range(3):
+            for kind in range(2):
+                for block in range(blocks):
+                    row = pl.ds((axis * 2 * blocks + kind * blocks + block) * plane + brick, 1)
+                    at = kind * 3 + axis
+                    table[row, :] = slopes[brick, at : at + 1, block * LANES : (block + 1) * LANES]
+        return carry
+
+    lax.fori_loop(0, plane, collect, 0, unroll=plane <= 8)
+    slope_table = jnp.concatenate(parts_of(table[...], 2), axis=1)
 
     step = chunk_of(beads, 4)
 
@@ -277,13 +512,13 @@
 def finish(species, corner_slot, corner_weight, slopes, positions, velocities, bonds):
     beads = positions.shape[1]
     count = bonds.shape[1]
-    plane, slots = slopes.shape[1:]
+    plane, _, slots = slopes.shape
     highs = 2 * (slots // LANES) * plane
     return pl.pallas_call(
         finish_kernel,
         out_shape=[jax.ShapeDtypeStruct((3, beads), f32)] * 2,
         scratch_shapes=[
-            pltpu.VMEM((3 * highs, 2 * LANES), f32),
+            pltpu.VMEM((3 * highs, LANES), f32),
             pltpu.VMEM((3 * beads // LANES, LANES), f32),
             pltpu.VMEM((3 * beads // LANES, LANES), f32),
             pltpu.VMEM((2, LANES, count), bf16),
@@ -293,33 +528,19 @@
     )(species, corner_slot, corner_weight, slopes, positions, velocities, bonds)
 
 def on_device(positions, velocities, species, corner_slot, corner_weight, slot_cell, bond_pairs):
-    plane = slot_cell.shape[1]
-    slots = slot_cell.shape[2]
-    cells = CX * CY * CZ
+    plane, slots = slot_cell.shape[1:]
+    bricks = Bricks(lax.axis_size("bx"), lax.axis_size("by"))
+    places = near_places(slot_cell, bricks)
     species = species.reshape(1, -1)
-    packets = deposit(species, corner_slot, corner_weight, plane, slots)
-    received = lax.all_to_all(
-        packets, ("bx", "by"), split_axis=1, concat_axis=1, tiled=True
-    )
-    flat_cells = ((slot_cell[0] * CY + slot_cell[1]) * CZ + slot_cell[2]).reshape(-1)
-    density = jnp.zeros((2, cells), jnp.float32).at[:, flat_cells].add(received.reshape(2, -1))
-    density = density * (CX * CY * CZ / BEADS_DEV)
-    density = density.reshape(2, CX, CY, CZ)
-    margin = 1
-    filtered = smooth_brick(density, margin)
-    smoothed = filtered[:, margin : margin + CX, margin : margin + CY, margin : margin + CZ]
-    combined = filtered[0] + filtered[1]
-    potential = jnp.stack(
-        [mixing * filtered[1] + stiffness * combined, mixing * filtered[0] + stiffness * combined]
-    )
-    slope_x = (potential[:, 2:, 1:-1, 1:-1] - potential[:, :-2, 1:-1, 1:-1]) * 0.5
-    slope_y = (potential[:, 1:-1, 2:, 1:-1] - potential[:, 1:-1, :-2, 1:-1]) * 0.5
-    slope_z = (potential[:, 1:-1, 1:-1, 2:] - potential[:, 1:-1, 1:-1, :-2]) * 0.5
-    slopes = jnp.stack([slope_x, slope_y, slope_z], axis=1).reshape(6, cells)
-    outgoing = slopes[:, flat_cells]
-    returned = lax.all_to_all(
-        outgoing.reshape(6, plane, slots), ("bx", "by"), split_axis=1, concat_axis=1, tiled=True
-    )
+    packets = deposit(bricks, species, corner_slot, corner_weight, plane, slots)
+    received = lax.all_to_all(packets, ("bx", "by"), split_axis=0, concat_axis=0, tiled=True)
+    field, below, above = fill(bricks, received, places)
+    from_above = shifted(below, "bz", 1)
+    from_below = shifted(above, "bz", -1)
+    turned = smooth(field, below, above)
+    slopes, whole = pick_slopes(turned, from_below, from_above, slot_cell)
+    returned = lax.all_to_all(slopes, ("bx", "by"), split_axis=0, concat_axis=0, tiled=True)
+    smoothed = smoothed_of(whole)
     moved, new_velocities = finish(
         species, corner_slot, corner_weight, returned, positions, velocities, bond_pairs
     )

time: 201 us -> 82.1 us (0.41)
  local copies, waits for them, and re-layouts: 67.8 us -> 2.57 us
  other arithmetic: 61.6 us -> 0.75 us
  Pallas kernels: 24.5 us -> 47.5 us
  waiting for transfers between devices: 28.1 us -> 14.3 us
    reshape x5 -> x0, local copies, waits for them, and re-layouts: 38.2 us -> none  [the longest x2 18.7 us: on_device(): slopes = jnp.stack([slope_x, slope_y, slope_z], axis=1).reshape(6, cells)]
    scatter-add x1 -> x0, other arithmetic: 24.6 us -> none  [on_device(): jnp.zeros((2, cells), jnp.float32).at[:, flat_cells]]
    pallas_call x1 -> x5, Pallas kernels: 5.61 us -> 28.6 us  [the longest x1 8.66 us: pick_slopes(): pl.pallas_call(slope_kernel, out_shape=[jax.ShapeDtypeStruct((plane, 6, s...]
    mul x1 -> x0, other arithmetic: 22.3 us -> none  [on_device(): density = density * (CX * CY * CZ / BEADS_DEV)]
    gather x1 -> x0, local copies, waits for them, and re-layouts: 16.1 us -> none  [on_device(): outgoing = slopes[:, flat_cells]]
    ppermute x6 -> x5, waiting for transfers between devices: 17 us -> 3.31 us  [shifted(): lax.ppermute(values, axis, [((i + step) % count, i) for i in range(count)])]
    add x4 -> x0, other arithmetic: 12.2 us -> none  [the longest x3 12 us: smooth_along(): result + taps[offset] * lax.slice_in_dim(extended, offset, offset + lengt...]
    slice x6 -> x1, local copies, waits for them, and re-layouts: 4.85 us -> 0.62 us  [near_places(): found[step_x, step_y] = moved[3 * at:3 * at + 3]]
  transfers between devices with their start and end apart: 8 -> 7, of which waited for: 7 -> 5; matrix products, arithmetic and copies ran while one was open for 2% -> 1% of each run, Pallas kernels for 0% -> 14%
where the time goes in v2:
time: 82.1 us; the launch traced here: 81.5 us
  Pallas kernels  47.5 us (58%)
  starting transfers between devices  15.8 us (19%)
  waiting for transfers between devices  14.3 us (17%)
  local copies, waits for them, and re-layouts  2.57 us (3%)
    pallas_call x1, Pallas kernels, finish(): pl.pallas_call(finish_kernel, out_shape=[jax.ShapeDtypeStruct((3, beads),...  18.9 us
    pallas_call x1, Pallas kernels, pick_slopes(): pl.pallas_call(slope_kernel, out_shape=[jax.ShapeDtypeStruct((plane, 6, s...  8.66 us
    pallas_call x1, Pallas kernels, fill(): pl.pallas_call(functools.partial(fill_kernel, bricks, group), out_shape=[...  8.41 us
    ppermute x5, starting transfers between devices, shifted(): lax.ppermute(values, axis, [((i + step) % count, i) for i in range(count)])  7.21 us
    all_to_all x1, waiting for transfers between devices, on_device(): lax.all_to_all(packets, ('bx', 'by'), split_axis=0, concat_axis=0, tiled=...  6.71 us
    pallas_call x1, Pallas kernels, deposit(): pl.pallas_call(functools.partial(deposit_kernel, bricks), out_shape=jax.S...  5.71 us
    all_to_all x1, starting transfers between devices, on_device(): lax.all_to_all(packets, ('bx', 'by'), split_axis=0, concat_axis=0, tiled=...  5.05 us
    all_to_all x1, waiting for transfers between devices, on_device(): lax.all_to_all(slopes, ('bx', 'by'), split_axis=0, concat_axis=0, tiled=T...  4.28 us
  transfers between devices with their start and end apart: 7, of which 5 were waited for; matrix products, arithmetic and copies ran while one was open for 1% of the time, Pallas kernels for 14%

profile of v2, /device:TPU:0, one launch (start us, length us, event | category | flops | bytes accessed | tf_op | source)
XLA Modules:
  0.0 81.5 jit_solution(17843896908095477986)
XLA Ops:
  0.6 3.1 %collective-permute-start.1 = (s32[3,8,256]{2,1,0:T(8,128)}, s32[3,8,256]{2,1,0:T(8,128)S(1)}, u32[]{:S(2)}, u32[]{:S(2)}) collective-permute-start(s32[3,8,256]{2,1,0:T(8,128)} %place.1), channel_id=1, source_target_pairs={{24,0},{0,8},{8,16},{16,24},{25,1},{1,9},{9,17},{17,25},{26,2},{2,... | collective-permute-start | bytes 73736 | tf_op jit(solution)/shard_map/ppermute | solution.py:359
  3.7 2.1 %collective-permute-start = (s32[3,8,256]{2,1,0:T(8,128)}, s32[3,8,256]{2,1,0:T(8,128)S(1)}, u32[]{:S(2)}, u32[]{:S(2)}) collective-permute-start(s32[3,8,256]{2,1,0:T(8,128)} %place.1), channel_id=1, source_target_pairs={{8,0},{16,8},{24,16},{0,24},{9,1},{17,9},{25,17},{1,25},{10,2},{18... | collective-permute-start | bytes 73736 | tf_op jit(solution)/shard_map/ppermute | solution.py:359
  5.8 2.1 %collective-permute-done.1.refs_2_ = s32[3,8,256]{2,1,0:T(8,128)S(1)} collective-permute-done((s32[3,8,256]{2,1,0:T(8,128)}, s32[3,8,256]{2,1,0:T(8,128)S(1)}, u32[]{:S(2)}, u32[]{:S(2)}) %collective-permute-start.1) | collective-permute-done | bytes 24608 | tf_op jit(solution)/shard_map/ppermute | solution.py:359
  7.9 0.0 copy-start.2
  7.9 0.1 collective-permute-done.refs_1_
  8.0 0.8 pad_add_fusion
  8.8 1.5 %collective-permute-start.2 = (s32[9,8,256]{2,1,0:T(8,128)S(1)}, s32[9,8,256]{2,1,0:T(8,128)S(1)}, u32[]{:S(2)}, u32[]{:S(2)}) collective-permute-start(s32[9,8,256]{2,1,0:T(8,128)S(1)} %pad_add_fusion), channel_id=1, source_target_pairs={{4,0},{0,4},{5,1},{1,5},{6,2},{2,6},{7,3},{3,7},{12,8},{8,12},{13,... | collective-permute-start | bytes 221192 | tf_op jit(solution)/shard_map/ppermute | solution.py:359
  10.3 5.7 %shard_map.94 = f32[8,12,256]{2,1,0:T(8,128)} custom-call(s32[1,4096]{1,0:T(1,128)} %bitcast.1, s32[2,8,4096]{2,1,0:T(8,128)} %corner_slot.3, f32[8,4096]{1,0:T(8,128)} %corner_weight.3), custom_call_target="tpu_custom_call" | custom-call | tf_op jit(solution)/shard_map/pallas_call | solution.py:114
  16.0 5.0 %all-to-all-start = ((f32[8,12,256]{2,1,0:T(8,128)}), f32[8,12,256]{2,1,0:T(8,128)S(1)}, u32[]{:S(2)}, u32[]{:S(2)}) async-start(f32[8,12,256]{2,1,0:T(8,128)} %shard_map.94), calls=%async_computation | async-start | bytes 262144 | tf_op jit(solution)/shard_map/all_to_all | solution.py:536
  21.1 0.0 collective-permute-done.2
  21.1 0.6 fusion
  21.7 6.7 %all-to-all-done.received = f32[8,12,256]{2,1,0:T(8,128)S(1)} async-done(((f32[8,12,256]{2,1,0:T(8,128)}), f32[8,12,256]{2,1,0:T(8,128)S(1)}, u32[]{:S(2)}, u32[]{:S(2)}) %all-to-all-start) | async-done | bytes 98336 | tf_op jit(solution)/shard_map/all_to_all | solution.py:536
  28.4 0.0 copy-start
  28.4 0.0 copy-done.2
  28.4 0.0 copy-done.3
  28.4 0.7 copy-done
  29.1 8.4 %shard_map.95 = (f32[24,80,128]{2,1,0:T(8,128)}, f32[18,8,128]{2,1,0:T(8,128)}, f32[18,8,128]{2,1,0:T(8,128)}) custom-call(f32[8,12,256]{2,1,0:T(8,128)} %copy-done, s32[3,8,256]{2,1,0:T(8,128)} %place.1, s32[3,8,256]{2,1,0:T(8,128)} %copy-done.3, s32[3,8,256]{2,1,0:T(8,128)} %copy-done.2, s32[3,8,256]{2,1,0:T(8,128)} %get-tuple-element.19.refs_3_, ...), custom_call_target="tpu_custom_call" | custom-call | tf_op jit(solution)/shard_map/pallas_call | solution.py:239
  37.5 0.0 collective-permute-start.4
  37.5 0.5 collective-permute-start.3
  38.0 3.1 %shard_map.96.turned = f32[18,2,80,128]{3,2,1,0:T(8,128)} custom-call(f32[24,80,128]{2,1,0:T(8,128)} %get-tuple-element.10.field, f32[18,8,128]{2,1,0:T(8,128)} %get-tuple-element.11.below, f32[18,8,128]{2,1,0:T(8,128)} %get-tuple-element.12.above), custom_call_target="tpu_custom_call" | custom-call | tf_op jit(solution)/shard_map/pallas_call | solution.py:271
  41.1 0.0 collective-permute-done.4.from_above
  41.1 0.0 copy-start.4
  41.1 1.1 %collective-permute-done.3.from_below = f32[18,8,128]{2,1,0:T(8,128)S(1)} collective-permute-done((f32[18,8,128]{2,1,0:T(8,128)}, f32[18,8,128]{2,1,0:T(8,128)S(1)}, u32[]{:S(2)}, u32[]{:S(2)}) %collective-permute-start.3) | collective-permute-done | bytes 73760 | tf_op jit(solution)/shard_map/ppermute | solution.py:359
  42.2 0.0 copy-done.4
  42.2 0.6 copy-done.5
  42.9 8.7 %shard_map.97 = (f32[8,6,256]{2,1,0:T(8,128)}, f32[18,2,80,128]{3,2,1,0:T(8,128)}) custom-call(f32[18,2,80,128]{3,2,1,0:T(8,128)} %shard_map.96.turned, f32[18,8,128]{2,1,0:T(8,128)} %copy-done.5, f32[18,8,128]{2,1,0:T(8,128)} %copy-done.4, s32[3,8,256]{2,1,0:T(8,128)} %place.1), custom_call_target="tpu_custom_call" | custom-call | tf_op jit(solution)/shard_map/pallas_call | solution.py:332
  51.5 3.5 %all-to-all-start.1 = ((f32[8,6,256]{2,1,0:T(8,128)}), f32[8,6,256]{2,1,0:T(8,128)S(1)}, u32[]{:S(2)}, u32[]{:S(2)}) async-start(f32[8,6,256]{2,1,0:T(8,128)} %get-tuple-element.13), calls=%async_computation.1 | async-start | bytes 131072 | tf_op jit(solution)/shard_map/all_to_all | solution.py:542
  55.1 2.7 %shard_map.99 = f32[2,16,64,64]{3,2,1,0:T(8,128)} custom-call(f32[18,2,80,128]{3,2,1,0:T(8,128)} %get-tuple-element.16.whole), custom_call_target="tpu_custom_call" | custom-call | tf_op jit(solution)/shard_map/pallas_call | solution.py:350
  57.7 4.3 %all-to-all-done.1.slopes = f32[8,6,256]{2,1,0:T(8,128)S(1)} async-done(((f32[8,6,256]{2,1,0:T(8,128)}), f32[8,6,256]{2,1,0:T(8,128)S(1)}, u32[]{:S(2)}, u32[]{:S(2)}) %all-to-all-start.1) | async-done | bytes 49184 | tf_op jit(solution)/shard_map/all_to_all | solution.py:542
  62.0 0.0 copy-start.1
  62.0 0.6 copy-done.1
  62.7 18.9 %shard_map.98 = (f32[3,4096]{1,0:T(4,128)}, f32[3,4096]{1,0:T(4,128)}) custom-call(s32[1,4096]{1,0:T(1,128)} %bitcast.2, s32[2,8,4096]{2,1,0:T(8,128)} %corner_slot.3, f32[8,4096]{1,0:T(8,128)} %corner_weight.3, f32[8,6,256]{2,1,0:T(8,128)} %copy-done.1, f32[3,4096]{1,0:T(4,128)} %positions.1, f32[3,4096]{1,0:T(4,128)} %velocities.1, s32[2,3840]{1,0:T(2,128)} %bonds.1), custom_call_target="tpu_custom_call" | custom-call | tf_op jit(solution)/shard_map/pallas_call | solution.py:517
  (2 shorter events, 0.0 us)
Async XLA Ops:
  0.6 7.2 %collective-permute-start.1 = (s32[3,8,256]{2,1,0:T(8,128)}, s32[3,8,256]{2,1,0:T(8,128)S(1)}, u32[]{:S(2)}, u32[]{:S(2)}) collective-permute-start(s32[3,8,256]{2,1,0:T(8,128)} %place.1), channel_id=1, source_target_pairs={{24,0},{0,8},{8,16},{16,24},{25,1},{1,9},{9,17},{17,25},{26,2},{2,... | collective-permute-start | bytes 73736 | tf_op jit(solution)/shard_map/ppermute | solution.py:359
  3.7 4.3 %collective-permute-start = (s32[3,8,256]{2,1,0:T(8,128)}, s32[3,8,256]{2,1,0:T(8,128)S(1)}, u32[]{:S(2)}, u32[]{:S(2)}) collective-permute-start(s32[3,8,256]{2,1,0:T(8,128)} %place.1), channel_id=1, source_target_pairs={{8,0},{16,8},{24,16},{0,24},{9,1},{17,9},{25,17},{1,25},{10,2},{18... | collective-permute-start | bytes 73736 | tf_op jit(solution)/shard_map/ppermute | solution.py:359
  7.9 20.5 %copy-start.2 = (s32[3,8,256]{2,1,0:T(8,128)}, s32[3,8,256]{2,1,0:T(8,128)S(1)}, u32[]{:S(2)}) copy-start(s32[3,8,256]{2,1,0:T(8,128)S(1)} %collective-permute-done.1.refs_2_) | copy-start | bytes 73732
  8.0 20.4 %copy-start.3 = (s32[3,8,256]{2,1,0:T(8,128)}, s32[3,8,256]{2,1,0:T(8,128)S(1)}, u32[]{:S(2)}) copy-start(s32[3,8,256]{2,1,0:T(8,128)S(1)} %collective-permute-done.refs_1_) | copy-start | bytes 73732
  8.8 12.3 %collective-permute-start.2 = (s32[9,8,256]{2,1,0:T(8,128)S(1)}, s32[9,8,256]{2,1,0:T(8,128)S(1)}, u32[]{:S(2)}, u32[]{:S(2)}) collective-permute-start(s32[9,8,256]{2,1,0:T(8,128)S(1)} %pad_add_fusion), channel_id=1, source_target_pairs={{4,0},{0,4},{5,1},{1,5},{6,2},{2,6},{7,3},{3,7},{12,8},{8,12},{13,... | collective-permute-start | bytes 221192 | tf_op jit(solution)/shard_map/ppermute | solution.py:359
  16.0 12.4 %all-to-all-start = ((f32[8,12,256]{2,1,0:T(8,128)}), f32[8,12,256]{2,1,0:T(8,128)S(1)}, u32[]{:S(2)}, u32[]{:S(2)}) async-start(f32[8,12,256]{2,1,0:T(8,128)} %shard_map.94), calls=%async_computation | async-start | bytes 262144 | tf_op jit(solution)/shard_map/all_to_all | solution.py:536
  28.4 0.7 copy-start
  37.5 3.6 %collective-permute-start.4 = (f32[18,8,128]{2,1,0:T(8,128)}, f32[18,8,128]{2,1,0:T(8,128)S(1)}, u32[]{:S(2)}, u32[]{:S(2)}) collective-permute-start(f32[18,8,128]{2,1,0:T(8,128)} %get-tuple-element.11.below), channel_id=1, source_target_pairs={{1,0},{2,1},{3,2},{0,3},{5,4},{6,5},{7,6},{4,7},{9,8},{10,9},{11,1... | collective-permute-start | bytes 221192 | tf_op jit(solution)/shard_map/ppermute | solution.py:359
  37.5 4.7 %collective-permute-start.3 = (f32[18,8,128]{2,1,0:T(8,128)}, f32[18,8,128]{2,1,0:T(8,128)S(1)}, u32[]{:S(2)}, u32[]{:S(2)}) collective-permute-start(f32[18,8,128]{2,1,0:T(8,128)} %get-tuple-element.12.above), channel_id=1, source_target_pairs={{3,0},{0,1},{1,2},{2,3},{7,4},{4,5},{5,6},{6,7},{11,8},{8,9},{9,10... | collective-permute-start | bytes 221192 | tf_op jit(solution)/shard_map/ppermute | solution.py:359
  41.1 1.1 %copy-start.4 = (f32[18,8,128]{2,1,0:T(8,128)}, f32[18,8,128]{2,1,0:T(8,128)S(1)}, u32[]{:S(2)}) copy-start(f32[18,8,128]{2,1,0:T(8,128)S(1)} %collective-permute-done.4.from_above) | copy-start | bytes 221188
  42.2 0.6 copy-start.5
  51.5 10.5 %all-to-all-start.1 = ((f32[8,6,256]{2,1,0:T(8,128)}), f32[8,6,256]{2,1,0:T(8,128)S(1)}, u32[]{:S(2)}, u32[]{:S(2)}) async-start(f32[8,6,256]{2,1,0:T(8,128)} %get-tuple-element.13), calls=%async_computation.1 | async-start | bytes 131072 | tf_op jit(solution)/shard_map/all_to_all | solution.py:542
  62.0 0.6 copy-start.1

commit v3 on v2

--- a/solution.py
+++ b/solution.py
@@ -32,7 +32,9 @@
 
 
 LANES = 128
-VMEM_LIMIT = 56 * 1024 * 1024
+VMEM_LIMIT = 20 * 1024 * 1024
+VMEM_WIDE = 60 * 1024 * 1024
+HBM = pl.BlockSpec(memory_space=pltpu.HBM)
 f32 = jnp.float32
 bf16 = jnp.bfloat16
 
@@ -47,8 +49,8 @@
 
 
 def one_hot(index, size):
-    rows = lax.broadcasted_iota(jnp.int32, (size, index.shape[1]), 0)
-    return jnp.where(rows == index, 1.0, 0.0).astype(bf16)
+    rows = lax.broadcasted_iota(jnp.int16, (size, index.shape[1]), 0)
+    return jnp.where(rows == index.astype(jnp.int16), jnp.array(1, bf16), jnp.array(0, bf16))
 
 
 def dot_nn(left, right):
@@ -63,6 +65,27 @@
     tiles = length // LANES
     best = max(t for t in range(1, most + 1) if tiles % t == 0)
     return best * LANES
+
+
+def chunk_copies(pairs, sems, step, count):
+    def copies(j):
+        where = pl.ds(pl.multiple_of(j * step, step), step)
+        for at, (source, target) in enumerate(pairs):
+            lead = (slice(None),) * (len(source.shape) - 1)
+            yield pltpu.make_async_copy(source.at[lead + (where,)], target.at[lead + (where,)], sems.at[at, j])
+
+    def start(j, carry):
+        for copy in copies(j):
+            copy.start()
+        return carry
+
+    lax.fori_loop(0, count, start, 0, unroll=True)
+
+    def wait(j):
+        for copy in copies(j):
+            copy.wait()
+
+    return wait
 
 
 def corner_keys(species, corner_slot, corner, where, plane, blocks):
@@ -73,15 +96,38 @@
     return high, slot - block * LANES
 
 
-def deposit_kernel(bricks, species, corner_slot, corner_weight, packets, sums):
-    plane, _, slots = packets.shape
+def deposit_kernel(
+    bricks,
+    species_far,
+    corner_slot_far,
+    corner_weight_far,
+    slot_cell_far,
+    packets,
+    sums,
+    species,
+    corner_slot,
+    corner_weight,
+    slot_cell,
+    sems,
+    cell_sem,
+):
+    plane, slots = slot_cell.shape[1:]
     blocks = slots // LANES
     highs = 2 * blocks * plane
     beads = corner_weight.shape[1]
-    step = chunk_of(beads, 4)
+    step = chunk_of(beads, 8)
     count_x, count_y = bricks.counts
+    wait = chunk_copies(
+        [(species_far, species), (corner_slot_far, corner_slot), (corner_weight_far, corner_weight)],
+        sems,
+        step,
+        beads // step,
+    )
+    cell_copy = pltpu.make_async_copy(slot_cell_far, slot_cell, cell_sem)
+    cell_copy.start()
 
     def body(j, total):
+        wait(j)
         where = pl.ds(pl.multiple_of(j * step, step), step)
         kind = species[:, where]
         for corner in range(8):
@@ -94,6 +140,9 @@
 
     total = lax.fori_loop(0, beads // step, body, jnp.zeros((2 * highs, LANES), f32))
     sums[...] = total[:highs] + total[highs:]
+    cell_copy.wait()
+    cells = (slot_cell[0] * CY + slot_cell[1]) * CZ + slot_cell[2]
+    first = 2 * blocks * len(bricks.offsets)
 
     def hand_out(target, carry):
         for near, (step_x, step_y) in enumerate(bricks.offsets):
@@ -102,21 +151,37 @@
             )
             for kind in range(2):
                 for block in range(blocks):
-                    packets[target, near * 2 + kind : near * 2 + kind + 1, block * LANES : (block + 1) * LANES] = sums[
+                    row = (near * 2 + kind) * blocks + block
+                    packets[target, row : row + 1, :] = sums[
                         pl.ds((kind * blocks + block) * plane + brick, 1), :
                     ]
+        for block in range(blocks):
+            rows = slice(first + block * plane, first + (block + 1) * plane)
+            packets[target, rows, :] = cells[:, block * LANES : (block + 1) * LANES].astype(f32)
         return carry
 
     lax.fori_loop(0, plane, hand_out, 0, unroll=plane <= 8)
 
 
-def deposit(bricks, species, corner_slot, corner_weight, plane, slots):
+def deposit(bricks, species, corner_slot, corner_weight, slot_cell):
+    plane, slots = slot_cell.shape[1:]
+    blocks = slots // LANES
+    rows = blocks * (2 * len(bricks.offsets) + plane)
     return pl.pallas_call(
         functools.partial(deposit_kernel, bricks),
-        out_shape=jax.ShapeDtypeStruct((plane, 2 * len(bricks.offsets), slots), f32),
-        scratch_shapes=[pltpu.VMEM((2 * slots // LANES * plane, LANES), f32)],
-        compiler_params=pltpu.CompilerParams(vmem_limit_bytes=VMEM_LIMIT),
-    )(species, corner_slot, corner_weight)
+        out_shape=jax.ShapeDtypeStruct((plane, rows, LANES), f32),
+        in_specs=[HBM] * 4,
+        scratch_shapes=[
+            pltpu.VMEM((2 * blocks * plane, LANES), f32),
+            pltpu.VMEM(species.shape, species.dtype),
+            pltpu.VMEM(corner_slot.shape, corner_slot.dtype),
+            pltpu.VMEM(corner_weight.shape, corner_weight.dtype),
+            pltpu.VMEM(slot_cell.shape, slot_cell.dtype),
+            pltpu.SemaphoreType.DMA((3, species.shape[1] // chunk_of(species.shape[1], 8))),
+            pltpu.SemaphoreType.DMA(()),
+        ],
+        compiler_params=pltpu.CompilerParams(vmem_limit_bytes=VMEM_WIDE),
+    )(species, corner_slot, corner_weight, slot_cell)
 
 
 HALO = REACH + 1
@@ -154,10 +219,12 @@
     return result
 
 
-def fill_kernel(bricks, group, received, *refs):
-    places = refs[: len(bricks.offsets)]
-    field, below, above, columns, edge_columns, edges = refs[len(bricks.offsets) :]
-    plane, _, slots = received.shape
+def fill_kernel(bricks, group, slots, received, after, field, below, above, columns, edge_columns, edges):
+    plane = received.shape[0]
+    blocks = slots // LANES
+    first_cell = 2 * blocks * len(bricks.offsets)
+    count_x, count_y = bricks.counts
+    mine = (lax.axis_index("bx"), lax.axis_index("by"))
     scale = CX * CY * CZ / BEADS_DEV
     edges[...] = jnp.zeros_like(edges)
     if plane > group:
@@ -170,13 +237,25 @@
 
     def sources(g, carry):
         for near, (step_x, step_y) in enumerate(bricks.offsets):
-            place = places[near]
+            brick = lax.rem(mine[0] + step_x, count_x) * count_y + lax.rem(mine[1] + step_y, count_y)
             cells_xy = []
             for p in range(group):
-                row = pl.ds(g * group + p, 1)
-                cells_xy.append((place[0, row, :], place[1, row, :]))
-                z = place[2, row, :]
-                amounts = [scale * received[g * group + p, near * 2 + k : near * 2 + k + 1, :] for k in range(2)]
+                source = g * group + p
+                cell = jnp.concatenate(
+                    [received[brick, pl.ds(first_cell + block * plane + source, 1), :] for block in range(blocks)],
+                    axis=1,
+                ).astype(jnp.int32)
+                cells_xy.append((cell // (CY * CZ), cell // CZ % CY))
+                z = cell % CZ
+                amounts = []
+                for k in range(2):
+                    row = (near * 2 + k) * blocks
+                    amounts.append(
+                        scale
+                        * jnp.concatenate(
+                            [received[source, row + block : row + block + 1, :] for block in range(blocks)], axis=1
+                        )
+                    )
                 tap = tap_of(jnp.abs(lax.broadcasted_iota(jnp.int32, (CZ, slots), 0) - z))
                 lane = slice(p * slots, (p + 1) * slots)
                 for k in range(2):
@@ -233,23 +312,24 @@
         above[layer] = both[2 * HALO :]
 
 
-def fill(bricks, received, places):
-    plane, _, slots = received.shape
+def fill(bricks, received, slots, after):
+    plane = received.shape[0]
     group = 8 if plane % 8 == 0 else plane
     return pl.pallas_call(
-        functools.partial(fill_kernel, bricks, group),
+        functools.partial(fill_kernel, bricks, group, slots),
         out_shape=[
             jax.ShapeDtypeStruct((CX + 2 * HALO, CY + 2 * PAD, 2 * CZ), f32),
             jax.ShapeDtypeStruct((CX + 2, 2 * HALO, LANES), f32),
             jax.ShapeDtypeStruct((CX + 2, 2 * HALO, LANES), f32),
         ],
+        in_specs=[pl.BlockSpec(), pl.BlockSpec(memory_space=pl.ANY)],
         scratch_shapes=[
             pltpu.VMEM((4 * CZ, group * slots), bf16),
             pltpu.VMEM((8 * HALO, group * slots), bf16),
             pltpu.VMEM((CX + 2 * HALO, 4 * HALO, LANES), f32),
         ],
         compiler_params=pltpu.CompilerParams(vmem_limit_bytes=VMEM_LIMIT),
-    )(received, *places)
+    )(received, after)
 
 
 def smooth_kernel(field, below, above, turned, line):
@@ -324,7 +404,7 @@
                 slopes[p, k * 3 + axis : k * 3 + axis + 1, :] = mixing * steep[1 - k] + joint
         return carry
 
-    lax.fori_loop(0, plane, source, 0)
+    lax.fori_loop(0, plane, source, 0, unroll=4)
 
 
 def pick_slopes(turned, from_below, from_above, place):
@@ -359,40 +439,84 @@
     return lax.ppermute(values, axis, [((i + step) % count, i) for i in range(count)])
 
 
-def near_places(slot_cell, bricks):
-    found = {}
-    for step_y in bricks.sides_y:
-        for step_x in bricks.sides_x:
-            values = slot_cell if step_x == 0 else found[step_x, 0] if step_y else shifted(slot_cell, "bx", step_x)
-            found[step_x, step_y] = values
-        if step_y:
-            across = [found[step_x, 0] for step_x in bricks.sides_x]
-            moved = shifted(jnp.concatenate(across, axis=0), "by", step_y)
-            for at, step_x in enumerate(bricks.sides_x):
-                found[step_x, step_y] = moved[3 * at : 3 * at + 3]
-    return [found[offset] for offset in bricks.offsets]
-
-
 def to_rows(store, base, row):
     for tile in range(row.shape[1] // LANES):
         store[pl.ds(base + tile, 1), :] = row[:, tile * LANES : (tile + 1) * LANES]
 
 
+def bond_ends(bonds, side, where, bead_rows):
+    index = bonds[pl.ds(side, 1), where]
+    high = index // LANES
+    rows = lax.broadcasted_iota(jnp.int32, (bead_rows, index.shape[1]), 0) == high
+    return rows, index - high * LANES
+
+
+def select(rows, picked):
+    size = rows.shape[0]
+    return [
+        jnp.sum(jnp.where(rows, picked[axis * size : (axis + 1) * size], 0.0), axis=0, keepdims=True)
+        for axis in range(3)
+    ]
+
+
+def bonds_kernel(positions, bonds, after, anchor, hot, separation):
+    bead_rows = positions.shape[1] // LANES
+    count = bonds.shape[1]
+    bond_step = chunk_of(count, 6)
+    for axis in range(3):
+        to_rows(anchor, axis * bead_rows, positions[axis : axis + 1, :])
+    anchor_table = jnp.concatenate(parts_of(anchor[...], 3), axis=1)
+    for j in range(count // bond_step):
+        where = slice(j * bond_step, (j + 1) * bond_step)
+        found = []
+        for side in range(2):
+            rows, low = bond_ends(bonds, side, where, bead_rows)
+            hot_low = one_hot(low, LANES)
+            hot[side, :, where] = hot_low
+            found.append(select(rows, dot_nn(anchor_table, jnp.concatenate([hot_low] * 3, axis=0))))
+        for axis in range(3):
+            separation[axis : axis + 1, where] = found[0][axis] - found[1][axis]
+
+
+def prepare_bonds(positions, bonds, after):
+    beads = positions.shape[1]
+    count = bonds.shape[1]
+    return pl.pallas_call(
+        bonds_kernel,
+        out_shape=[
+            jax.ShapeDtypeStruct((3 * beads // LANES, LANES), f32),
+            jax.ShapeDtypeStruct((2, LANES, count), bf16),
+            jax.ShapeDtypeStruct((3, count), f32),
+        ],
+        in_specs=[pl.BlockSpec(), pl.BlockSpec(), pl.BlockSpec(memory_space=pl.ANY)],
+        compiler_params=pltpu.CompilerParams(vmem_limit_bytes=VMEM_LIMIT),
+    )(positions, bonds, after)
+
+
 def finish_kernel(
-    species,
-    corner_slot,
-    corner_weight,
+    species_far,
+    corner_slot_far,
+    corner_weight_far,
+    velocities_far,
     slopes,
-    positions,
-    velocities,
-    bonds,
+    bonds_far,
+    anchor_far,
+    hot_far,
+    separation_far,
     new_positions,
     new_velocities,
     table,
     shift,
+    species,
+    corner_slot,
+    corner_weight,
+    velocities,
+    bonds,
     anchor,
     hot,
     separation,
+    sems,
+    late_sems,
 ):
     plane, _, slots = slopes.shape
     blocks = slots // LANES
@@ -400,6 +524,26 @@
     beads = corner_weight.shape[1]
     bead_rows = beads // LANES
     count = bonds.shape[1]
+    step = chunk_of(beads, 4)
+    wait = chunk_copies(
+        [
+            (species_far, species),
+            (corner_slot_far, corner_slot),
+            (corner_weight_far, corner_weight),
+            (velocities_far, velocities),
+        ],
+        sems,
+        step,
+        beads // step,
+    )
+    late = [
+        pltpu.make_async_copy(source, target, late_sems.at[at])
+        for at, (source, target) in enumerate(
+            [(bonds_far, bonds), (anchor_far, anchor), (hot_far, hot), (separation_far, separation)]
+        )
+    ]
+    for copy in late:
+        copy.start()
 
     def collect(brick, carry):
         for axis in range(3):
@@ -413,9 +557,8 @@
     lax.fori_loop(0, plane, collect, 0, unroll=plane <= 8)
     slope_table = jnp.concatenate(parts_of(table[...], 2), axis=1)
 
-    step = chunk_of(beads, 4)
-
     def force_body(j, carry):
+        wait(j)
         where = pl.ds(pl.multiple_of(j * step, step), step)
         kind = species[:, where]
         total = jnp.zeros((3 * highs, step), f32)
@@ -431,41 +574,14 @@
             force = -jnp.sum(total[axis * highs : (axis + 1) * highs], axis=0, keepdims=True)
             half = velocities[pl.ds(axis, 1), where] + 0.5 * time_step * force
             to_rows(shift, axis * bead_rows + j * (step // LANES), time_step * half)
-            to_rows(anchor, axis * bead_rows + j * (step // LANES), positions[pl.ds(axis, 1), where])
         return carry
 
     lax.fori_loop(0, beads // step, force_body, 0)
 
+    for copy in late:
+        copy.wait()
     bond_step = chunk_of(count, 6)
     bond_rows = 3 * bead_rows
-    anchor_parts = parts_of(anchor[...], 3)
-    anchor_table = jnp.concatenate(anchor_parts, axis=1)
-
-    def ends(side, where):
-        index = bonds[pl.ds(side, 1), where]
-        high = index // LANES
-        return lax.broadcasted_iota(jnp.int32, (bead_rows, bond_step), 0) == high, index - high * LANES
-
-    def select(rows, picked):
-        return [
-            jnp.sum(
-                jnp.where(rows, picked[axis * bead_rows : (axis + 1) * bead_rows], 0.0),
-                axis=0,
-                keepdims=True,
-            )
-            for axis in range(3)
-        ]
-
-    for j in range(count // bond_step):
-        where = slice(j * bond_step, (j + 1) * bond_step)
-        found = []
-        for side in range(2):
-            rows, low = ends(side, where)
-            hot_low = one_hot(low, LANES)
-            hot[side, :, where] = hot_low
-            found.append(select(rows, dot_nn(anchor_table, jnp.concatenate([hot_low] * 3, axis=0))))
-        for axis in range(3):
-            separation[axis : axis + 1, where] = found[0][axis] - found[1][axis]
 
     def sweep(repeat, carry):
         shift_table = jnp.concatenate(parts_of(shift[...], 2), axis=1)
@@ -473,7 +589,7 @@
         for j in range(count // bond_step):
             where = slice(j * bond_step, (j + 1) * bond_step)
             hots = [hot[side, :, where] for side in range(2)]
-            rows = [ends(side, where)[0] for side in range(2)]
+            rows = [bond_ends(bonds, side, where, bead_rows)[0] for side in range(2)]
             found = [
                 select(rows[side], dot_nn(shift_table, jnp.concatenate([hots[side]] * 2, axis=0)))
                 for side in range(2)
@@ -509,32 +625,35 @@
             new_velocities[axis : axis + 1, where] = move / time_step
 
 
-def finish(species, corner_slot, corner_weight, slopes, positions, velocities, bonds):
-    beads = positions.shape[1]
-    count = bonds.shape[1]
+def finish(species, corner_slot, corner_weight, slopes, velocities, bonds, prepared):
+    beads = velocities.shape[1]
     plane, _, slots = slopes.shape
     highs = 2 * (slots // LANES) * plane
+    early = (species, corner_slot, corner_weight, velocities)
+    late = (bonds, *prepared)
     return pl.pallas_call(
         finish_kernel,
         out_shape=[jax.ShapeDtypeStruct((3, beads), f32)] * 2,
+        in_specs=[HBM] * len(early) + [pl.BlockSpec()] + [HBM] * len(late),
         scratch_shapes=[
             pltpu.VMEM((3 * highs, LANES), f32),
             pltpu.VMEM((3 * beads // LANES, LANES), f32),
-            pltpu.VMEM((3 * beads // LANES, LANES), f32),
-            pltpu.VMEM((2, LANES, count), bf16),
-            pltpu.VMEM((3, count), f32),
+            *(pltpu.VMEM(a.shape, a.dtype) for a in early + late),
+            pltpu.SemaphoreType.DMA((len(early), beads // chunk_of(beads, 4))),
+            pltpu.SemaphoreType.DMA((len(late),)),
         ],
-        compiler_params=pltpu.CompilerParams(vmem_limit_bytes=VMEM_LIMIT),
-    )(species, corner_slot, corner_weight, slopes, positions, velocities, bonds)
+        compiler_params=pltpu.CompilerParams(vmem_limit_bytes=VMEM_WIDE),
+    )(*early, slopes, *late)
+
 
 def on_device(positions, velocities, species, corner_slot, corner_weight, slot_cell, bond_pairs):
-    plane, slots = slot_cell.shape[1:]
+    slots = slot_cell.shape[2]
     bricks = Bricks(lax.axis_size("bx"), lax.axis_size("by"))
-    places = near_places(slot_cell, bricks)
     species = species.reshape(1, -1)
-    packets = deposit(bricks, species, corner_slot, corner_weight, plane, slots)
+    packets = deposit(bricks, species, corner_slot, corner_weight, slot_cell)
     received = lax.all_to_all(packets, ("bx", "by"), split_axis=0, concat_axis=0, tiled=True)
-    field, below, above = fill(bricks, received, places)
+    prepared = prepare_bonds(positions, bond_pairs, packets)
+    field, below, above = fill(bricks, received, slots, prepared[2])
     from_above = shifted(below, "bz", 1)
     from_below = shifted(above, "bz", -1)
     turned = smooth(field, below, above)
@@ -542,7 +661,7 @@
     returned = lax.all_to_all(slopes, ("bx", "by"), split_axis=0, concat_axis=0, tiled=True)
     smoothed = smoothed_of(whole)
     moved, new_velocities = finish(
-        species, corner_slot, corner_weight, returned, positions, velocities, bond_pairs
+        species, corner_slot, corner_weight, returned, velocities, bond_pairs, prepared
     )
     return (moved, new_velocities, smoothed)
 

time: 82.1 us -> 66.8 us (0.81)
  Pallas kernels: 47.5 us -> 37.7 us
  starting transfers between devices: 15.8 us -> 12.1 us
  waiting for transfers between devices: 14.3 us -> 10.6 us
  local copies, waits for them, and re-layouts: 2.57 us -> 5.07 us
    ppermute x5 -> x2, starting transfers between devices: 7.21 us -> 0.55 us  [shifted(): lax.ppermute(values, axis, [((i + step) % count, i) for i in range(count)])]
    all_to_all x1, waiting for transfers between devices: 6.71 us -> 1.8 us  [on_device(): lax.all_to_all(packets, ('bx', 'by'), split_axis=0, concat_axis=0, tiled=...]
    unnamed x12 -> x16, local copies, waits for them, and re-layouts: 1.94 us -> 5.07 us
    pallas_call x1, Pallas kernels: 8.66 us -> 6.14 us  [pick_slopes(): pl.pallas_call(slope_kernel, out_shape=[jax.ShapeDtypeStruct((plane, 6, s...]
    pallas_call x1, Pallas kernels: 18.9 us -> 16.5 us  [finish(): pl.pallas_call(finish_kernel, out_shape=[jax.ShapeDtypeStruct((3, beads),...]
    pallas_call x1, Pallas kernels: 3.12 us -> 0.87 us  [smooth(): pl.pallas_call(smooth_kernel, out_shape=jax.ShapeDtypeStruct((CX + 2, 2,...]
    all_to_all x1, starting transfers between devices: 5.05 us -> 7.29 us  [on_device(): lax.all_to_all(packets, ('bx', 'by'), split_axis=0, concat_axis=0, tiled=...]
    pallas_call x1, Pallas kernels: 2.68 us -> 1.31 us  [smoothed_of(): pl.pallas_call(smoothed_kernel, out_shape=jax.ShapeDtypeStruct((2, CX, CY...]
  transfers between devices with their start and end apart: 7 -> 4, of which waited for: 5 -> 4; matrix products, arithmetic and copies ran while one was open for 1% -> 0% of each run, Pallas kernels for 14% -> 5%
where the time goes in v3:
time: 66.8 us; the launch traced here: 66.3 us
  Pallas kernels  37.7 us (56%)
  starting transfers between devices  12.1 us (18%)
  waiting for transfers between devices  10.6 us (16%)
  local copies, waits for them, and re-layouts  5.07 us (8%)
  between operations  0.85 us (1%)
    pallas_call x1, Pallas kernels, finish(): pl.pallas_call(finish_kernel, out_shape=[jax.ShapeDtypeStruct((3, beads),...  16.5 us
    all_to_all x1, starting transfers between devices, on_device(): lax.all_to_all(packets, ('bx', 'by'), split_axis=0, concat_axis=0, tiled=...  7.29 us
    pallas_call x1, Pallas kernels, fill(): pl.pallas_call(functools.partial(fill_kernel, bricks, group, slots), out_...  6.41 us
    pallas_call x1, Pallas kernels, pick_slopes(): pl.pallas_call(slope_kernel, out_shape=[jax.ShapeDtypeStruct((plane, 6, s...  6.14 us
    all_to_all x1, waiting for transfers between devices, on_device(): lax.all_to_all(slopes, ('bx', 'by'), split_axis=0, concat_axis=0, tiled=T...  5.6 us
    pallas_call x1, Pallas kernels, deposit(): pl.pallas_call(functools.partial(deposit_kernel, bricks), out_shape=jax.S...  5.14 us
    unnamed x16, local copies, waits for them, and re-layouts  5.07 us
    all_to_all x1, starting transfers between devices, on_device(): lax.all_to_all(slopes, ('bx', 'by'), split_axis=0, concat_axis=0, tiled=T...  4.2 us
  transfers between devices with their start and end apart: 4, of which 4 were waited for; matrix products, arithmetic and copies ran while one was open for 0% of the time, Pallas kernels for 5%

profile of v3, /device:TPU:0, one launch (start us, length us, event | category | flops | bytes accessed | tf_op | source)
XLA Modules:
  0.0 66.3 jit_solution(17630485301103810703)
XLA Ops:
  0.6 5.1 %shard_map.94.after = f32[8,40,128]{2,1,0:T(8,128)} custom-call(s32[1,4096]{1,0:T(1,128)} %bitcast.1, s32[2,8,4096]{2,1,0:T(8,128)} %corner_slot_far.3, f32[8,4096]{1,0:T(8,128)} %corner_weight_far.3, s32[3,8,256]{2,1,0:T(8,128)} %place.1), custom_call_target="tpu_custom_call" | custom-call | tf_op jit(solution)/shard_map/pallas_call | solution.py:170
  5.8 7.3 %all-to-all-start = ((f32[8,40,128]{2,1,0:T(8,128)}), f32[8,40,128]{2,1,0:T(8,128)S(1)}, u32[]{:S(2)}, u32[]{:S(2)}) async-start(f32[8,40,128]{2,1,0:T(8,128)} %shard_map.94.after), calls=%async_computation | async-start | bytes 327680 | tf_op jit(solution)/shard_map/all_to_all | solution.py:654
  13.1 0.0 copy-start.1
  13.1 0.9 %copy-done.1 = f32[8,40,128]{2,1,0:T(8,128)S(1)} copy-done((f32[8,40,128]{2,1,0:T(8,128)S(1)}, f32[8,40,128]{2,1,0:T(8,128)}, u32[]{:S(2)}) %copy-start.1) | copy-done | bytes 163864
  14.0 0.0 copy-start.3
  14.0 0.8 %copy-done.3 = s32[2,3840]{1,0:T(2,128)S(1)} copy-done((s32[2,3840]{1,0:T(2,128)S(1)}, s32[2,3840]{1,0:T(2,128)}, u32[]{:S(2)}) %copy-start.3) | copy-done | bytes 30744
  14.8 0.0 copy-start.5
  14.8 0.8 %copy-done.5 = f32[3,4096]{1,0:T(4,128)S(1)} copy-done((f32[3,4096]{1,0:T(4,128)S(1)}, f32[3,4096]{1,0:T(4,128)}, u32[]{:S(2)}) %copy-start.5) | copy-done | bytes 49176
  15.6 1.3 %shard_map.95 = (f32[96,128]{1,0:T(8,128)S(1)}, bf16[2,128,3840]{2,1,0:T(8,128)(2,1)S(1)}, f32[3,3840]{1,0:T(4,128)S(1)}) custom-call(f32[3,4096]{1,0:T(4,128)S(1)} %copy-done.5, s32[2,3840]{1,0:T(2,128)S(1)} %copy-done.3, f32[8,40,128]{2,1,0:T(8,128)S(1)} %copy-done.1), custom_call_target="tpu_custom_call" | custom-call | tf_op jit(solution)/shard_map/pallas_call | solution.py:484
  16.9 0.0 copy-start
  16.9 1.3 %copy-done = bf16[2,128,3840]{2,1,0:T(8,128)(2,1)} copy-done((bf16[2,128,3840]{2,1,0:T(8,128)(2,1)}, bf16[2,128,3840]{2,1,0:T(8,128)(2,1)S(1)}, u32[]{:S(2)}) %copy-start) | copy-done | bytes 1966104
  18.2 0.0 copy-start.6
  18.2 0.6 copy-done.6
  18.8 0.0 copy-start.2
  18.8 0.0 copy-start.4
  18.8 1.8 %all-to-all-done.received = f32[8,40,128]{2,1,0:T(8,128)S(1)} async-done(((f32[8,40,128]{2,1,0:T(8,128)}), f32[8,40,128]{2,1,0:T(8,128)S(1)}, u32[]{:S(2)}, u32[]{:S(2)}) %all-to-all-start) | async-done | bytes 163872 | tf_op jit(solution)/shard_map/all_to_all | solution.py:654
  20.6 6.4 %shard_map.96 = (f32[24,80,128]{2,1,0:T(8,128)S(1)}, f32[18,8,128]{2,1,0:T(8,128)S(1)}, f32[18,8,128]{2,1,0:T(8,128)S(1)}) custom-call(f32[8,40,128]{2,1,0:T(8,128)S(1)} %all-to-all-done.received, f32[3,3840]{1,0:T(4,128)S(1)} %get-tuple-element.13.after.separation_far), custom_call_target="tpu_custom_call" | custom-call | tf_op jit(solution)/shard_map/pallas_call | solution.py:318
  27.1 0.1 collective-permute-start.1
  27.1 0.5 collective-permute-start
  27.6 0.9 %shard_map.97.turned = f32[18,2,80,128]{3,2,1,0:T(8,128)S(1)} custom-call(f32[24,80,128]{2,1,0:T(8,128)S(1)} %get-tuple-element.14.field, f32[18,8,128]{2,1,0:T(8,128)S(1)} %get-tuple-element.15.below, f32[18,8,128]{2,1,0:T(8,128)S(1)} %get-tuple-element.16.above), custom_call_target="tpu_custom_call" | custom-call | tf_op jit(solution)/shard_map/pallas_call | solution.py:351
  28.5 0.6 collective-permute-done.1.from_above
  29.1 2.6 %collective-permute-done.from_below = f32[18,8,128]{2,1,0:T(8,128)S(1)} collective-permute-done((f32[18,8,128]{2,1,0:T(8,128)S(1)}, f32[18,8,128]{2,1,0:T(8,128)S(1)}, u32[]{:S(2)}, u32[]{:S(2)}) %collective-permute-start) | collective-permute-done | bytes 73760 | tf_op jit(solution)/shard_map/ppermute | solution.py:439
  31.7 0.0 copy-done.4
  31.7 6.1 %shard_map.98 = (f32[8,6,256]{2,1,0:T(8,128)}, f32[18,2,80,128]{3,2,1,0:T(8,128)S(1)}) custom-call(f32[18,2,80,128]{3,2,1,0:T(8,128)S(1)} %shard_map.97.turned, f32[18,8,128]{2,1,0:T(8,128)S(1)} %collective-permute-done.from_below, f32[18,8,128]{2,1,0:T(8,128)S(1)} %collective-permute-done.1.from_above, s32[3,8,256]{2,1,0:T(8,128)S(1)} %copy-done.4), custom_call_target="tpu_custom_call" | custom-call | tf_op jit(solution)/shard_map/pallas_call | solution.py:412
  37.9 0.0 copy-done.2
  37.9 4.2 %all-to-all-start.1 = ((f32[8,6,256]{2,1,0:T(8,128)}), f32[8,6,256]{2,1,0:T(8,128)S(1)}, u32[]{:S(2)}, u32[]{:S(2)}) async-start(f32[8,6,256]{2,1,0:T(8,128)} %get-tuple-element.17), calls=%async_computation.1 | async-start | bytes 131072 | tf_op jit(solution)/shard_map/all_to_all | solution.py:661
  42.1 1.3 %shard_map.100 = f32[2,16,64,64]{3,2,1,0:T(8,128)} custom-call(f32[18,2,80,128]{3,2,1,0:T(8,128)S(1)} %get-tuple-element.22.whole), custom_call_target="tpu_custom_call" | custom-call | tf_op jit(solution)/shard_map/pallas_call | solution.py:430
  43.4 5.6 %all-to-all-done.1.slopes = f32[8,6,256]{2,1,0:T(8,128)S(1)} async-done(((f32[8,6,256]{2,1,0:T(8,128)}), f32[8,6,256]{2,1,0:T(8,128)S(1)}, u32[]{:S(2)}, u32[]{:S(2)}) %all-to-all-start.1) | async-done | bytes 49184 | tf_op jit(solution)/shard_map/all_to_all | solution.py:661
  49.0 0.0 copy-start.7
  49.0 0.6 copy-done.7
  49.6 16.5 %shard_map.99 = (f32[3,4096]{1,0:T(4,128)}, f32[3,4096]{1,0:T(4,128)}) custom-call(s32[1,4096]{1,0:T(1,128)} %bitcast.2, s32[2,8,4096]{2,1,0:T(8,128)} %corner_slot_far.3, f32[8,4096]{1,0:T(8,128)} %corner_weight_far.3, f32[3,4096]{1,0:T(4,128)} %velocities_far.1, f32[8,6,256]{2,1,0:T(8,128)} %copy-done.7, s32[2,3840]{1,0:T(2,128)} %bonds_far.1, ...), custom_call_target="tpu_custom_call" | custom-call | tf_op jit(solution)/shard_map/pallas_call | solution.py:634
Async XLA Ops:
  5.8 14.9 %all-to-all-start = ((f32[8,40,128]{2,1,0:T(8,128)}), f32[8,40,128]{2,1,0:T(8,128)S(1)}, u32[]{:S(2)}, u32[]{:S(2)}) async-start(f32[8,40,128]{2,1,0:T(8,128)} %shard_map.94.after), calls=%async_computation | async-start | bytes 327680 | tf_op jit(solution)/shard_map/all_to_all | solution.py:654
  13.1 0.9 %copy-start.1 = (f32[8,40,128]{2,1,0:T(8,128)S(1)}, f32[8,40,128]{2,1,0:T(8,128)}, u32[]{:S(2)}) copy-start(f32[8,40,128]{2,1,0:T(8,128)} %shard_map.94.after) | copy-start | bytes 491524
  14.0 0.8 %copy-start.3 = (s32[2,3840]{1,0:T(2,128)S(1)}, s32[2,3840]{1,0:T(2,128)}, u32[]{:S(2)}) copy-start(s32[2,3840]{1,0:T(2,128)} %bonds_far.1) | copy-start | bytes 92164
  14.8 0.8 %copy-start.5 = (f32[3,4096]{1,0:T(4,128)S(1)}, f32[3,4096]{1,0:T(4,128)}, u32[]{:S(2)}) copy-start(f32[3,4096]{1,0:T(4,128)} %positions.1) | copy-start | bytes 147460
  16.9 1.3 %copy-start = (bf16[2,128,3840]{2,1,0:T(8,128)(2,1)}, bf16[2,128,3840]{2,1,0:T(8,128)(2,1)S(1)}, u32[]{:S(2)}) copy-start(bf16[2,128,3840]{2,1,0:T(8,128)(2,1)S(1)} %get-tuple-element.19.hot_far) | copy-start | bytes 5898244
  18.2 0.6 copy-start.6
  18.8 19.0 %copy-start.2 = (f32[3,3840]{1,0:T(4,128)}, f32[3,3840]{1,0:T(4,128)S(1)}, u32[]{:S(2)}) copy-start(f32[3,3840]{1,0:T(4,128)S(1)} %get-tuple-element.13.after.separation_far) | copy-start | bytes 138244
  18.8 12.9 %copy-start.4 = (s32[3,8,256]{2,1,0:T(8,128)S(1)}, s32[3,8,256]{2,1,0:T(8,128)}, u32[]{:S(2)}) copy-start(s32[3,8,256]{2,1,0:T(8,128)} %place.1) | copy-start | bytes 73732
  27.1 2.0 %collective-permute-start.1 = (f32[18,8,128]{2,1,0:T(8,128)S(1)}, f32[18,8,128]{2,1,0:T(8,128)S(1)}, u32[]{:S(2)}, u32[]{:S(2)}) collective-permute-start(f32[18,8,128]{2,1,0:T(8,128)S(1)} %get-tuple-element.15.below), channel_id=1, source_target_pairs={{1,0},{2,1},{3,2},{0,3},{5,4},{6,5},{7,6},{4,7},{9,8},{10,9},{11,1... | collective-permute-start | bytes 221192 | tf_op jit(solution)/shard_map/ppermute | solution.py:439
  27.1 4.6 %collective-permute-start = (f32[18,8,128]{2,1,0:T(8,128)S(1)}, f32[18,8,128]{2,1,0:T(8,128)S(1)}, u32[]{:S(2)}, u32[]{:S(2)}) collective-permute-start(f32[18,8,128]{2,1,0:T(8,128)S(1)} %get-tuple-element.16.above), channel_id=1, source_target_pairs={{3,0},{0,1},{1,2},{2,3},{7,4},{4,5},{5,6},{6,7},{11,8},{8,9},{9,10... | collective-permute-start | bytes 221192 | tf_op jit(solution)/shard_map/ppermute | solution.py:439
  37.9 11.1 %all-to-all-start.1 = ((f32[8,6,256]{2,1,0:T(8,128)}), f32[8,6,256]{2,1,0:T(8,128)S(1)}, u32[]{:S(2)}, u32[]{:S(2)}) async-start(f32[8,6,256]{2,1,0:T(8,128)} %get-tuple-element.17), calls=%async_computation.1 | async-start | bytes 131072 | tf_op jit(solution)/shard_map/all_to_all | solution.py:661
  49.0 0.6 copy-start.7

commit v4 on v3

--- a/solution.py
+++ b/solution.py
@@ -444,52 +444,120 @@
         store[pl.ds(base + tile, 1), :] = row[:, tile * LANES : (tile + 1) * LANES]
 
 
-def bond_ends(bonds, side, where, bead_rows):
-    index = bonds[pl.ds(side, 1), where]
-    high = index // LANES
-    rows = lax.broadcasted_iota(jnp.int32, (bead_rows, index.shape[1]), 0) == high
-    return rows, index - high * LANES
-
-
 def select(rows, picked):
     size = rows.shape[0]
     return [
-        jnp.sum(jnp.where(rows, picked[axis * size : (axis + 1) * size], 0.0), axis=0, keepdims=True)
-        for axis in range(3)
+        jnp.sum(jnp.where(rows, picked[at * size : (at + 1) * size], 0.0), axis=0, keepdims=True)
+        for at in range(picked.shape[0] // size)
     ]
 
 
-def bonds_kernel(positions, bonds, after, anchor, hot, separation):
-    bead_rows = positions.shape[1] // LANES
+def is_row(high, size):
+    return lax.broadcasted_iota(jnp.int32, (size, high.shape[1]), 0) == high
+
+
+def counted(flags):
+    lanes = lax.broadcasted_iota(jnp.int32, (LANES, 2 * LANES), 1)
+    upto = (lax.broadcasted_iota(jnp.int32, (LANES, 2 * LANES), 0) <= lanes) | (lanes >= LANES)
+    counts = dot_nn(flags.astype(bf16), jnp.where(upto, 1.0, 0.0).astype(bf16))
+    before = jnp.zeros((1, LANES), f32)
+    rows = []
+    for row in range(flags.shape[0]):
+        rows.append(counts[row : row + 1, :LANES] + before)
+        before = before + counts[row : row + 1, LANES:]
+    return rows
+
+
+def chains_kernel(positions, bonds, after, anchor, hot, high, apart, steps, placed):
+    beads = positions.shape[1]
+    bead_rows = beads // LANES
     count = bonds.shape[1]
+    chains = beads - count
+    length = beads // chains
+    ends = 2 * chains
     bond_step = chunk_of(count, 6)
     for axis in range(3):
         to_rows(anchor, axis * bead_rows, positions[axis : axis + 1, :])
-    anchor_table = jnp.concatenate(parts_of(anchor[...], 3), axis=1)
+
+    total = jnp.zeros((3 * bead_rows, LANES), f32)
     for j in range(count // bond_step):
         where = slice(j * bond_step, (j + 1) * bond_step)
-        found = []
+        index = [bonds[side : side + 1, where] for side in range(2)]
+        highs = [i // LANES for i in index]
+        lows = [i - h * LANES for i, h in zip(index, highs)]
         for side in range(2):
-            rows, low = bond_ends(bonds, side, where, bead_rows)
-            hot_low = one_hot(low, LANES)
-            hot[side, :, where] = hot_low
-            found.append(select(rows, dot_nn(anchor_table, jnp.concatenate([hot_low] * 3, axis=0))))
+            rows = is_row(highs[side], bead_rows)
+            values = (jnp.ones((1, bond_step), f32), highs[1 - side].astype(f32), lows[1 - side].astype(f32))
+            left = [jnp.where(rows, value, 0.0).astype(bf16) for value in values]
+            total = total + dot_nt(jnp.concatenate(left, axis=0), one_hot(lows[side], LANES))
+    single = total[:bead_rows] == 1.0
+    around = (total[bead_rows : 2 * bead_rows] * LANES + total[2 * bead_rows :]).astype(jnp.int32)
+    around_high = around // LANES
+    table = jnp.concatenate([around_high, around - around_high * LANES], axis=0).astype(f32).astype(bf16)
+
+    flags = jnp.where(single, 1.0, 0.0)
+    ranks = counted(flags)
+    rank = jnp.concatenate(
+        [jnp.where(flags[row : row + 1] > 0.0, ranks[row] - 1.0, -LANES) for row in range(bead_rows)], axis=1
+    ).astype(jnp.int32)
+    rank_high = jnp.where(rank < 0, -1, rank // LANES)
+    bead = lax.broadcasted_iota(jnp.int32, (1, beads), 1)
+    end_rows = -(-ends // (8 * LANES)) * 8
+    rows = is_row(rank_high, end_rows)
+    left = [jnp.where(rows, part.astype(f32), 0.0) for part in (bead // LANES, bead % LANES)]
+    found = dot_nt(jnp.concatenate(left, axis=0).astype(bf16), one_hot(rank - rank_high * LANES, LANES))
+    found = found[:end_rows] * LANES + found[end_rows:]
+    first = jnp.concatenate([found[row : row + 1] for row in range(ends // LANES)], axis=1)
+
+    def walk(m, carry):
+        before, here = carry
+        bead = here.astype(jnp.int32)
+        bead_high = bead // LANES
+        bead_low = bead - bead_high * LANES
+        steps[pl.ds(m, 1), :] = bead_high.astype(f32)
+        steps[pl.ds(length + m, 1), :] = bead_low.astype(f32)
+        next_high, next_low = select(is_row(bead_high, bead_rows), dot_nn(table, one_hot(bead_low, LANES)))
+        return here, next_high * LANES + next_low - before
+
+    last, _ = lax.fori_loop(0, length, walk, (jnp.zeros_like(first), first))
+    kept = jnp.where(first < last, 1.0, 0.0)
+    flags = jnp.concatenate([kept[:, at : at + LANES] for at in range(0, ends, LANES)], axis=0)
+    kept_rank = jnp.where(kept > 0.0, jnp.concatenate(counted(flags), axis=1) - 1.0, -1.0).astype(jnp.int32)
+    order = dot_nt(steps[...].astype(bf16), one_hot(kept_rank, chains)).astype(jnp.int32)
+    for m in range(length):
+        where = slice(m * chains, (m + 1) * chains)
+        high[:, where] = order[m : m + 1]
+        hot[:, where] = one_hot(order[length + m : length + m + 1], LANES)
+
+    anchor_table = jnp.concatenate(parts_of(anchor[...], 3), axis=1)
+    wide = 4 * chains
+    for j in range(beads // wide):
+        where = slice(j * wide, (j + 1) * wide)
+        rows = is_row(high[:, where], bead_rows)
+        found = select(rows, dot_nn(anchor_table, jnp.concatenate([hot[:, where]] * 3, axis=0)))
         for axis in range(3):
-            separation[axis : axis + 1, where] = found[0][axis] - found[1][axis]
-
-
-def prepare_bonds(positions, bonds, after):
+            for at in range(4):
+                placed[axis, 4 * j + at : 4 * j + at + 1, :] = found[axis][:, at * chains : (at + 1) * chains]
+    for axis in range(3):
+        apart[axis, : length - 1, :] = placed[axis, : length - 1, :] - placed[axis, 1:, :]
+        apart[axis, length - 1 :, :] = jnp.zeros((1, chains), f32)
+
+
+def order_chains(positions, bonds, after):
     beads = positions.shape[1]
-    count = bonds.shape[1]
+    chains = beads - bonds.shape[1]
+    length = beads // chains
     return pl.pallas_call(
-        bonds_kernel,
+        chains_kernel,
         out_shape=[
             jax.ShapeDtypeStruct((3 * beads // LANES, LANES), f32),
-            jax.ShapeDtypeStruct((2, LANES, count), bf16),
-            jax.ShapeDtypeStruct((3, count), f32),
+            jax.ShapeDtypeStruct((LANES, beads), bf16),
+            jax.ShapeDtypeStruct((1, beads), jnp.int32),
+            jax.ShapeDtypeStruct((3, length, chains), f32),
         ],
         in_specs=[pl.BlockSpec(), pl.BlockSpec(), pl.BlockSpec(memory_space=pl.ANY)],
-        compiler_params=pltpu.CompilerParams(vmem_limit_bytes=VMEM_LIMIT),
+        scratch_shapes=[pltpu.VMEM((2 * length, 2 * chains), f32), pltpu.VMEM((3, length, chains), f32)],
+        compiler_params=pltpu.CompilerParams(vmem_limit_bytes=VMEM_WIDE),
     )(positions, bonds, after)
 
 
@@ -499,10 +567,10 @@
     corner_weight_far,
     velocities_far,
     slopes,
-    bonds_far,
     anchor_far,
     hot_far,
-    separation_far,
+    high_far,
+    apart_far,
     new_positions,
     new_velocities,
     table,
@@ -511,10 +579,11 @@
     corner_slot,
     corner_weight,
     velocities,
-    bonds,
     anchor,
     hot,
-    separation,
+    high,
+    apart,
+    placed,
     sems,
     late_sems,
 ):
@@ -523,7 +592,7 @@
     highs = 2 * blocks * plane
     beads = corner_weight.shape[1]
     bead_rows = beads // LANES
-    count = bonds.shape[1]
+    length, chains = apart.shape[1:]
     step = chunk_of(beads, 4)
     wait = chunk_copies(
         [
@@ -539,7 +608,7 @@
     late = [
         pltpu.make_async_copy(source, target, late_sems.at[at])
         for at, (source, target) in enumerate(
-            [(bonds_far, bonds), (anchor_far, anchor), (hot_far, hot), (separation_far, separation)]
+            [(anchor_far, anchor), (hot_far, hot), (high_far, high), (apart_far, apart)]
         )
     ]
     for copy in late:
@@ -580,41 +649,40 @@
 
     for copy in late:
         copy.wait()
-    bond_step = chunk_of(count, 6)
-    bond_rows = 3 * bead_rows
-
-    def sweep(repeat, carry):
-        shift_table = jnp.concatenate(parts_of(shift[...], 2), axis=1)
-        total = jnp.zeros((2 * bond_rows, LANES), f32)
-        for j in range(count // bond_step):
-            where = slice(j * bond_step, (j + 1) * bond_step)
-            hots = [hot[side, :, where] for side in range(2)]
-            rows = [bond_ends(bonds, side, where, bead_rows)[0] for side in range(2)]
-            found = [
-                select(rows[side], dot_nn(shift_table, jnp.concatenate([hots[side]] * 2, axis=0)))
-                for side in range(2)
-            ]
-            apart = [separation[axis : axis + 1, where] for axis in range(3)]
-            stretch = [apart[axis] + (found[0][axis] - found[1][axis]) for axis in range(3)]
-            excess = sum(s * s for s in stretch) - bond_length * bond_length
-            along = sum(s * a for s, a in zip(stretch, apart))
-            factor = excess / (4.0 * jnp.maximum(along, 0.5 * bond_length * bond_length))
-            moves = [parts_of(factor * apart[axis], 2) for axis in range(3)]
-            for side in range(2):
-                sign = 1.0 if side else -1.0
-                left = jnp.concatenate(
-                    [
-                        jnp.where(rows[side], sign * moves[axis][part].astype(f32), 0.0).astype(bf16)
-                        for part in range(2)
-                        for axis in range(3)
-                    ],
-                    axis=0,
-                )
-                total = total + dot_nt(left, hots[side])
-        shift[...] = shift[...] + total[:bond_rows] + total[bond_rows:]
-        return carry
-
-    lax.fori_loop(0, SWEEPS, sweep, 0)
+    shift_table = jnp.concatenate(parts_of(shift[...], 2), axis=1)
+    wide = 4 * chains
+    for j in range(beads // wide):
+        where = slice(j * wide, (j + 1) * wide)
+        rows = is_row(high[:, where], bead_rows)
+        found = select(rows, dot_nn(shift_table, jnp.concatenate([hot[:, where]] * 2, axis=0)))
+        for axis in range(3):
+            for at in range(4):
+                placed[axis, 4 * j + at : 4 * j + at + 1, :] = found[axis][:, at * chains : (at + 1) * chains]
+    between = [apart[axis] for axis in range(3)]
+    before = [placed[axis] for axis in range(3)]
+    moved = before
+    for _ in range(SWEEPS):
+        stretch = [between[axis] + (moved[axis] - pltpu.roll(moved[axis], length - 1, 0)) for axis in range(3)]
+        excess = sum(s * s for s in stretch) - bond_length * bond_length
+        along = sum(s * a for s, a in zip(stretch, between))
+        factor = excess / (4.0 * jnp.maximum(along, 0.5 * bond_length * bond_length))
+        pulls = [factor * between[axis] for axis in range(3)]
+        moved = [moved[axis] - pulls[axis] + pltpu.roll(pulls[axis], 1, 0) for axis in range(3)]
+    for axis in range(3):
+        placed[axis] = moved[axis] - before[axis]
+    total = jnp.zeros((6 * bead_rows, LANES), f32)
+    for j in range(beads // wide):
+        where = slice(j * wide, (j + 1) * wide)
+        rows = is_row(high[:, where], bead_rows)
+        parts = [
+            parts_of(jnp.concatenate([placed[axis, 4 * j + at : 4 * j + at + 1, :] for at in range(4)], axis=1), 2)
+            for axis in range(3)
+        ]
+        left = [
+            jnp.where(rows, parts[axis][part].astype(f32), 0.0).astype(bf16) for part in range(2) for axis in range(3)
+        ]
+        total = total + dot_nt(jnp.concatenate(left, axis=0), hot[:, where])
+    shift[...] = shift[...] + total[: 3 * bead_rows] + total[3 * bead_rows :]
 
     for axis in range(3):
         for tile in range(bead_rows):
@@ -625,12 +693,12 @@
             new_velocities[axis : axis + 1, where] = move / time_step
 
 
-def finish(species, corner_slot, corner_weight, slopes, velocities, bonds, prepared):
+def finish(species, corner_slot, corner_weight, slopes, velocities, prepared):
     beads = velocities.shape[1]
     plane, _, slots = slopes.shape
     highs = 2 * (slots // LANES) * plane
     early = (species, corner_slot, corner_weight, velocities)
-    late = (bonds, *prepared)
+    late = tuple(prepared)
     return pl.pallas_call(
         finish_kernel,
         out_shape=[jax.ShapeDtypeStruct((3, beads), f32)] * 2,
@@ -639,6 +707,7 @@
             pltpu.VMEM((3 * highs, LANES), f32),
             pltpu.VMEM((3 * beads // LANES, LANES), f32),
             *(pltpu.VMEM(a.shape, a.dtype) for a in early + late),
+            pltpu.VMEM(prepared[3].shape, f32),
             pltpu.SemaphoreType.DMA((len(early), beads // chunk_of(beads, 4))),
             pltpu.SemaphoreType.DMA((len(late),)),
         ],
@@ -652,8 +721,8 @@
     species = species.reshape(1, -1)
     packets = deposit(bricks, species, corner_slot, corner_weight, slot_cell)
     received = lax.all_to_all(packets, ("bx", "by"), split_axis=0, concat_axis=0, tiled=True)
-    prepared = prepare_bonds(positions, bond_pairs, packets)
-    field, below, above = fill(bricks, received, slots, prepared[2])
+    prepared = order_chains(positions, bond_pairs, packets)
+    field, below, above = fill(bricks, received, slots, prepared[3])
     from_above = shifted(below, "bz", 1)
     from_below = shifted(above, "bz", -1)
     turned = smooth(field, below, above)
@@ -661,7 +730,7 @@
     returned = lax.all_to_all(slopes, ("bx", "by"), split_axis=0, concat_axis=0, tiled=True)
     smoothed = smoothed_of(whole)
     moved, new_velocities = finish(
-        species, corner_slot, corner_weight, returned, velocities, bond_pairs, prepared
+        species, corner_slot, corner_weight, returned, velocities, prepared
     )
     return (moved, new_velocities, smoothed)
 

time: 66.8 us -> 60.7 us (0.909)
  local copies, waits for them, and re-layouts: 5.07 us -> 1.43 us
  Pallas kernels: 37.7 us -> 35.3 us
  waiting for transfers between devices: 10.6 us -> 8.98 us
  starting transfers between devices: 12.1 us -> 13.6 us
    pallas_call x1, Pallas kernels: 16.5 us -> 8.03 us  [finish(): pl.pallas_call(finish_kernel, out_shape=[jax.ShapeDtypeStruct((3, beads),...]
    pallas_call x1, Pallas kernels: 1.3 us -> 7.34 us  [order_chains(): pl.pallas_call(chains_kernel, out_shape=[jax.ShapeDtypeStruct((3 * beads...]
    unnamed x16 -> x6, local copies, waits for them, and re-layouts: 5.07 us -> 1.43 us
    all_to_all x1, waiting for transfers between devices: 1.8 us -> 0.22 us  [on_device(): lax.all_to_all(packets, ('bx', 'by'), split_axis=0, concat_axis=0, tiled=...]
    all_to_all x1, starting transfers between devices: 4.2 us -> 5.78 us  [on_device(): lax.all_to_all(slopes, ('bx', 'by'), split_axis=0, concat_axis=0, tiled=T...]
  transfers between devices with their start and end apart: 4 -> 4, of which waited for: 4 -> 4; matrix products, arithmetic and copies ran while one was open for 0% -> 0% of each run, Pallas kernels for 5% -> 16%
where the time goes in v4:
time: 60.7 us; the launch traced here: 60.2 us
  Pallas kernels  35.3 us (58%)
  starting transfers between devices  13.6 us (22%)
  waiting for transfers between devices  8.98 us (15%)
  local copies, waits for them, and re-layouts  1.43 us (2%)
  between operations  0.82 us (1%)
    pallas_call x1, Pallas kernels, finish(): pl.pallas_call(finish_kernel, out_shape=[jax.ShapeDtypeStruct((3, beads),...  8.03 us
    pallas_call x1, Pallas kernels, order_chains(): pl.pallas_call(chains_kernel, out_shape=[jax.ShapeDtypeStruct((3 * beads...  7.34 us
    all_to_all x1, starting transfers between devices, on_device(): lax.all_to_all(packets, ('bx', 'by'), split_axis=0, concat_axis=0, tiled=...  7.29 us
    pallas_call x1, Pallas kernels, fill(): pl.pallas_call(functools.partial(fill_kernel, bricks, group, slots), out_...  6.42 us
    pallas_call x1, Pallas kernels, pick_slopes(): pl.pallas_call(slope_kernel, out_shape=[jax.ShapeDtypeStruct((plane, 6, s...  6.15 us
    all_to_all x1, starting transfers between devices, on_device(): lax.all_to_all(slopes, ('bx', 'by'), split_axis=0, concat_axis=0, tiled=T...  5.78 us
    all_to_all x1, waiting for transfers between devices, on_device(): lax.all_to_all(slopes, ('bx', 'by'), split_axis=0, concat_axis=0, tiled=T...  5.6 us
    pallas_call x1, Pallas kernels, deposit(): pl.pallas_call(functools.partial(deposit_kernel, bricks), out_shape=jax.S...  5.14 us
  transfers between devices with their start and end apart: 4, of which 4 were waited for; matrix products, arithmetic and copies ran while one was open for 0% of the time, Pallas kernels for 16%

profile of v4, /device:TPU:0, one launch (start us, length us, event | category | flops | bytes accessed | tf_op | source)
XLA Modules:
  0.0 60.2 jit_solution(16213651455618491324)
XLA Ops:
  0.6 5.1 %shard_map.94.after = f32[8,40,128]{2,1,0:T(8,128)} custom-call(s32[1,4096]{1,0:T(1,128)} %bitcast.1, s32[2,8,4096]{2,1,0:T(8,128)} %corner_slot_far.3, f32[8,4096]{1,0:T(8,128)} %corner_weight_far.3, s32[3,8,256]{2,1,0:T(8,128)} %place.1), custom_call_target="tpu_custom_call" | custom-call | tf_op jit(solution)/shard_map/pallas_call | solution.py:170
  5.8 7.3 %all-to-all-start = ((f32[8,40,128]{2,1,0:T(8,128)}), f32[8,40,128]{2,1,0:T(8,128)S(1)}, u32[]{:S(2)}, u32[]{:S(2)}) async-start(f32[8,40,128]{2,1,0:T(8,128)} %shard_map.94.after), calls=%async_computation | async-start | bytes 327680 | tf_op jit(solution)/shard_map/all_to_all | solution.py:723
  13.1 0.0 copy-start.1
  13.1 7.3 %shard_map.95 = (f32[96,128]{1,0:T(8,128)}, bf16[128,4096]{1,0:T(8,128)(2,1)}, s32[1,4096]{1,0:T(1,128)}, f32[3,16,256]{2,1,0:T(8,128)}) custom-call(f32[3,4096]{1,0:T(4,128)} %positions.1, s32[2,3840]{1,0:T(2,128)} %bonds.1, f32[8,40,128]{2,1,0:T(8,128)} %shard_map.94.after), custom_call_target="tpu_custom_call" | custom-call | tf_op jit(solution)/shard_map/pallas_call | solution.py:550
  20.4 0.2 all-to-all-done.received
  20.6 0.0 copy-start
  20.6 0.8 %copy-done = f32[3,16,256]{2,1,0:T(8,128)S(1)} copy-done((f32[3,16,256]{2,1,0:T(8,128)S(1)}, f32[3,16,256]{2,1,0:T(8,128)}, u32[]{:S(2)}) %copy-start) | copy-done | bytes 49176
  21.4 6.4 %shard_map.96 = (f32[24,80,128]{2,1,0:T(8,128)S(1)}, f32[18,8,128]{2,1,0:T(8,128)S(1)}, f32[18,8,128]{2,1,0:T(8,128)S(1)}) custom-call(f32[8,40,128]{2,1,0:T(8,128)S(1)} %all-to-all-done.received, f32[3,16,256]{2,1,0:T(8,128)S(1)} %copy-done), custom_call_target="tpu_custom_call" | custom-call | tf_op jit(solution)/shard_map/pallas_call | solution.py:318
  27.9 0.5 collective-permute-start.1
  28.3 0.1 collective-permute-start
  28.4 0.9 %shard_map.97.turned = f32[18,2,80,128]{3,2,1,0:T(8,128)S(1)} custom-call(f32[24,80,128]{2,1,0:T(8,128)S(1)} %get-tuple-element.15.field, f32[18,8,128]{2,1,0:T(8,128)S(1)} %get-tuple-element.16.below, f32[18,8,128]{2,1,0:T(8,128)S(1)} %get-tuple-element.17.above), custom_call_target="tpu_custom_call" | custom-call | tf_op jit(solution)/shard_map/pallas_call | solution.py:351
  29.4 0.9 %collective-permute-done.1.from_above = f32[18,8,128]{2,1,0:T(8,128)S(1)} collective-permute-done((f32[18,8,128]{2,1,0:T(8,128)S(1)}, f32[18,8,128]{2,1,0:T(8,128)S(1)}, u32[]{:S(2)}, u32[]{:S(2)}) %collective-permute-start.1) | collective-permute-done | bytes 73760 | tf_op jit(solution)/shard_map/ppermute | solution.py:439
  30.3 2.2 %collective-permute-done.from_below = f32[18,8,128]{2,1,0:T(8,128)S(1)} collective-permute-done((f32[18,8,128]{2,1,0:T(8,128)S(1)}, f32[18,8,128]{2,1,0:T(8,128)S(1)}, u32[]{:S(2)}, u32[]{:S(2)}) %collective-permute-start) | collective-permute-done | bytes 73760 | tf_op jit(solution)/shard_map/ppermute | solution.py:439
  32.5 0.0 copy-done.1
  32.5 6.2 %shard_map.98 = (f32[8,6,256]{2,1,0:T(8,128)}, f32[18,2,80,128]{3,2,1,0:T(8,128)S(1)}) custom-call(f32[18,2,80,128]{3,2,1,0:T(8,128)S(1)} %shard_map.97.turned, f32[18,8,128]{2,1,0:T(8,128)S(1)} %collective-permute-done.from_below, f32[18,8,128]{2,1,0:T(8,128)S(1)} %collective-permute-done.1.from_above, s32[3,8,256]{2,1,0:T(8,128)S(1)} %copy-done.1), custom_call_target="tpu_custom_call" | custom-call | tf_op jit(solution)/shard_map/pallas_call | solution.py:412
  38.7 5.8 %all-to-all-start.1 = ((f32[8,6,256]{2,1,0:T(8,128)}), f32[8,6,256]{2,1,0:T(8,128)S(1)}, u32[]{:S(2)}, u32[]{:S(2)}) async-start(f32[8,6,256]{2,1,0:T(8,128)} %get-tuple-element.18), calls=%async_computation.1 | async-start | bytes 131072 | tf_op jit(solution)/shard_map/all_to_all | solution.py:730
  44.5 1.3 %shard_map.100 = f32[2,16,64,64]{3,2,1,0:T(8,128)} custom-call(f32[18,2,80,128]{3,2,1,0:T(8,128)S(1)} %get-tuple-element.24.whole), custom_call_target="tpu_custom_call" | custom-call | tf_op jit(solution)/shard_map/pallas_call | solution.py:430
  45.8 5.6 %all-to-all-done.1.slopes = f32[8,6,256]{2,1,0:T(8,128)S(1)} async-done(((f32[8,6,256]{2,1,0:T(8,128)}), f32[8,6,256]{2,1,0:T(8,128)S(1)}, u32[]{:S(2)}, u32[]{:S(2)}) %all-to-all-start.1) | async-done | bytes 49184 | tf_op jit(solution)/shard_map/all_to_all | solution.py:730
  51.4 0.0 copy-start.2
  51.4 0.6 %copy-done.2 = f32[8,6,256]{2,1,0:T(8,128)} copy-done((f32[8,6,256]{2,1,0:T(8,128)}, f32[8,6,256]{2,1,0:T(8,128)S(1)}, u32[]{:S(2)}) %copy-start.2) | copy-done | bytes 49176
  52.0 8.0 %shard_map.99 = (f32[3,4096]{1,0:T(4,128)}, f32[3,4096]{1,0:T(4,128)}) custom-call(s32[1,4096]{1,0:T(1,128)} %bitcast.2, s32[2,8,4096]{2,1,0:T(8,128)} %corner_slot_far.3, f32[8,4096]{1,0:T(8,128)} %corner_weight_far.3, f32[3,4096]{1,0:T(4,128)} %velocities_far.1, f32[8,6,256]{2,1,0:T(8,128)} %copy-done.2, f32[96,128]{1,0:T(8,128)} %get-tuple-element.19.anchor_far, ...), custom_call_target="tpu_custom_call" | custom-call | tf_op jit(solution)/shard_map/pallas_call | solution.py:702
Async XLA Ops:
  5.8 14.9 %all-to-all-start = ((f32[8,40,128]{2,1,0:T(8,128)}), f32[8,40,128]{2,1,0:T(8,128)S(1)}, u32[]{:S(2)}, u32[]{:S(2)}) async-start(f32[8,40,128]{2,1,0:T(8,128)} %shard_map.94.after), calls=%async_computation | async-start | bytes 327680 | tf_op jit(solution)/shard_map/all_to_all | solution.py:723
  13.1 19.5 %copy-start.1 = (s32[3,8,256]{2,1,0:T(8,128)S(1)}, s32[3,8,256]{2,1,0:T(8,128)}, u32[]{:S(2)}) copy-start(s32[3,8,256]{2,1,0:T(8,128)} %place.1) | copy-start | bytes 73732
  20.6 0.8 %copy-start = (f32[3,16,256]{2,1,0:T(8,128)S(1)}, f32[3,16,256]{2,1,0:T(8,128)}, u32[]{:S(2)}) copy-start(f32[3,16,256]{2,1,0:T(8,128)} %get-tuple-element.14.after.apart_far) | copy-start | bytes 147460
  27.9 2.5 %collective-permute-start.1 = (f32[18,8,128]{2,1,0:T(8,128)S(1)}, f32[18,8,128]{2,1,0:T(8,128)S(1)}, u32[]{:S(2)}, u32[]{:S(2)}) collective-permute-start(f32[18,8,128]{2,1,0:T(8,128)S(1)} %get-tuple-element.16.below), channel_id=1, source_target_pairs={{1,0},{2,1},{3,2},{0,3},{5,4},{6,5},{7,6},{4,7},{9,8},{10,9},{11,1... | collective-permute-start | bytes 221192 | tf_op jit(solution)/shard_map/ppermute | solution.py:439
  28.3 4.2 %collective-permute-start = (f32[18,8,128]{2,1,0:T(8,128)S(1)}, f32[18,8,128]{2,1,0:T(8,128)S(1)}, u32[]{:S(2)}, u32[]{:S(2)}) collective-permute-start(f32[18,8,128]{2,1,0:T(8,128)S(1)} %get-tuple-element.17.above), channel_id=1, source_target_pairs={{3,0},{0,1},{1,2},{2,3},{7,4},{4,5},{5,6},{6,7},{11,8},{8,9},{9,10... | collective-permute-start | bytes 221192 | tf_op jit(solution)/shard_map/ppermute | solution.py:439
  38.7 12.7 %all-to-all-start.1 = ((f32[8,6,256]{2,1,0:T(8,128)}), f32[8,6,256]{2,1,0:T(8,128)S(1)}, u32[]{:S(2)}, u32[]{:S(2)}) async-start(f32[8,6,256]{2,1,0:T(8,128)} %get-tuple-element.18), calls=%async_computation.1 | async-start | bytes 131072 | tf_op jit(solution)/shard_map/all_to_all | solution.py:730
  51.4 0.6 %copy-start.2 = (f32[8,6,256]{2,1,0:T(8,128)}, f32[8,6,256]{2,1,0:T(8,128)S(1)}, u32[]{:S(2)}) copy-start(f32[8,6,256]{2,1,0:T(8,128)S(1)} %all-to-all-done.1.slopes) | copy-start | bytes 147460

commit v5 on v4

--- a/solution.py
+++ b/solution.py
@@ -135,10 +135,10 @@
             weight = corner_weight[pl.ds(corner, 1), where]
             rows = lax.broadcasted_iota(jnp.int32, (highs, step), 0) == high
             left = [jnp.where(rows, p.astype(f32), 0.0).astype(bf16) for p in parts_of(weight, 2)]
-            total = total + dot_nt(jnp.concatenate(left, axis=0), one_hot(low, LANES))
+            total = total + dot_nt(one_hot(low, LANES), jnp.concatenate(left, axis=0))
         return total
 
-    total = lax.fori_loop(0, beads // step, body, jnp.zeros((2 * highs, LANES), f32))
+    total = lax.fori_loop(0, beads // step, body, jnp.zeros((LANES, 2 * highs), f32)).T
     sums[...] = total[:highs] + total[highs:]
     cell_copy.wait()
     cells = (slot_cell[0] * CY + slot_cell[1]) * CZ + slot_cell[2]
@@ -219,14 +219,13 @@
     return result
 
 
-def fill_kernel(bricks, group, slots, received, after, field, below, above, columns, edge_columns, edges):
+def fill_kernel(bricks, group, slots, received, after, field, below, above, columns, edges):
     plane = received.shape[0]
     blocks = slots // LANES
     first_cell = 2 * blocks * len(bricks.offsets)
     count_x, count_y = bricks.counts
     mine = (lax.axis_index("bx"), lax.axis_index("by"))
     scale = CX * CY * CZ / BEADS_DEV
-    edges[...] = jnp.zeros_like(edges)
     if plane > group:
         field[...] = jnp.zeros_like(field)
 
@@ -256,18 +255,13 @@
                             [received[source, row + block : row + block + 1, :] for block in range(blocks)], axis=1
                         )
                     )
-                tap = tap_of(jnp.abs(lax.broadcasted_iota(jnp.int32, (CZ, slots), 0) - z))
+                layer = lax.broadcasted_iota(jnp.int32, (CZ, slots), 0) == z
                 lane = slice(p * slots, (p + 1) * slots)
                 for k in range(2):
-                    for at, part in enumerate(parts_of(tap * amounts[k], 2)):
-                        columns[at * 2 * CZ + k * CZ : at * 2 * CZ + (k + 1) * CZ, lane] = part
-                row_of = lax.broadcasted_iota(jnp.int32, (4 * HALO, slots), 0)
-                layer = row_of % HALO
-                layer = jnp.where(row_of < 2 * HALO, layer - REACH, layer + (CZ - 1))
-                amount = jnp.where((row_of // HALO) % 2 == 0, amounts[0], amounts[1])
-                edge = tap_of(jnp.abs(layer - z)) * amount
-                for at, part in enumerate(parts_of(edge, 2)):
-                    edge_columns[at * 4 * HALO : (at + 1) * 4 * HALO, lane] = part
+                    for at, part in enumerate(parts_of(amounts[k], 2)):
+                        columns[at * 2 * CZ + k * CZ : at * 2 * CZ + (k + 1) * CZ, lane] = jnp.where(
+                            layer, part.astype(f32), 0.0
+                        ).astype(bf16)
             for side_x in bricks.sides_x[step_x]:
                 first_x, width_x, from_x = {
                     0: (HALO, CX, 0),
@@ -275,10 +269,10 @@
                     -1: (0, HALO, CX - HALO),
                 }[side_x]
                 for side_y in bricks.sides_y[step_y]:
-                    first_y, width_y, from_y, lane_y = {
-                        0: (PAD, CY, 0, 0),
-                        1: (PAD + CY, PAD, 0, CY),
-                        -1: (0, PAD, CY - PAD, LANES - PAD),
+                    first_y, width_y, from_y = {
+                        0: (PAD, CY, 0),
+                        1: (PAD + CY, PAD, 0),
+                        -1: (0, PAD, CY - PAD),
                     }[side_y]
                     keys = [
                         jnp.where(
@@ -294,16 +288,43 @@
                         )
                         sums = dot_nt(hot, columns[...])
                         sums = sums[:, : 2 * CZ] + sums[:, 2 * CZ :]
-                        outer = dot_nt(edge_columns[...], hot)
-                        outer = outer[: 4 * HALO] + outer[4 * HALO :]
                         for layer in range(layers):
                             at = first_x + start + layer
                             piece = slice(layer * width_y, (layer + 1) * width_y)
                             put(field, (at, slice(first_y, first_y + width_y), slice(None)), sums[piece])
-                            put(edges, (at, slice(None), slice(lane_y, lane_y + width_y)), outer[:, piece])
         return carry
 
     lax.fori_loop(0, plane // group, sources, 0)
+
+    def pair_of(shape, dim):
+        index = lax.broadcasted_iota(jnp.int32, shape, dim)
+        return index // CZ, index % CZ
+
+    square = (2 * CZ, 2 * CZ)
+    (kind_from, z_from), (kind_to, z_to) = pair_of(square, 0), pair_of(square, 1)
+    inner = parts_of(jnp.where(kind_from == kind_to, tap_of(jnp.abs(z_to - z_from)), 0.0), 2)
+    shape = (4 * HALO, 2 * CZ)
+    kind_from, z_from = pair_of(shape, 1)
+    row_of = lax.broadcasted_iota(jnp.int32, shape, 0)
+    layer = row_of % HALO
+    layer = jnp.where(row_of < 2 * HALO, layer - REACH, layer + (CZ - 1))
+    kind_to = row_of // HALO % 2
+    outer = parts_of(jnp.where(kind_from == kind_to, tap_of(jnp.abs(layer - z_from)), 0.0), 2)
+    inner_both = jnp.concatenate([inner[0], inner[0]], axis=0)
+    outer_both = jnp.concatenate([outer[0], outer[0]], axis=1)
+    wide = CY + 2 * PAD
+    layers = 6 if (CX + 2 * HALO) % 6 == 0 else 1
+    for start in range(0, CX + 2 * HALO, layers):
+        parts = parts_of(field[start : start + layers].reshape(layers * wide, 2 * CZ), 2)
+        both = jnp.concatenate(parts, axis=1)
+        done = dot_nn(both, inner_both) + dot_nn(parts[0], inner[1])
+        field[start : start + layers] = done.reshape(layers, wide, 2 * CZ)
+        edge = dot_nt(outer_both, both) + dot_nt(outer[1], parts[0])
+        for at in range(layers):
+            row = jnp.concatenate(
+                [edge[:, at * wide : (at + 1) * wide], jnp.zeros((4 * HALO, LANES - wide), f32)], axis=1
+            )
+            edges[start + at] = pltpu.roll(row, LANES - PAD, 1)
 
     for layer in range(CX + 2):
         along_x = filter_rows(lambda j: edges[layer + j])
@@ -325,7 +346,6 @@
         in_specs=[pl.BlockSpec(), pl.BlockSpec(memory_space=pl.ANY)],
         scratch_shapes=[
             pltpu.VMEM((4 * CZ, group * slots), bf16),
-            pltpu.VMEM((8 * HALO, group * slots), bf16),
             pltpu.VMEM((CX + 2 * HALO, 4 * HALO, LANES), f32),
         ],
         compiler_params=pltpu.CompilerParams(vmem_limit_bytes=VMEM_LIMIT),
@@ -404,7 +424,7 @@
                 slopes[p, k * 3 + axis : k * 3 + axis + 1, :] = mixing * steep[1 - k] + joint
         return carry
 
-    lax.fori_loop(0, plane, source, 0, unroll=4)
+    lax.fori_loop(0, plane, source, 0, unroll=8 if plane % 8 == 0 else 1)
 
 
 def pick_slopes(turned, from_below, from_above, place):

time: 60.7 us -> 57.4 us (0.946)
  Pallas kernels: 35.3 us -> 32.2 us
    pallas_call x1, Pallas kernels: 6.42 us -> 4.97 us  [fill(): pl.pallas_call(functools.partial(fill_kernel, bricks, group, slots), out_...]
    pallas_call x1, Pallas kernels: 6.15 us -> 4.99 us  [pick_slopes(): pl.pallas_call(slope_kernel, out_shape=[jax.ShapeDtypeStruct((plane, 6, s...]
  transfers between devices with their start and end apart: 4 -> 4, of which waited for: 4 -> 4; matrix products, arithmetic and copies ran while one was open for 0% -> 0% of each run, Pallas kernels for 16% -> 17%
where the time goes in v5:
time: 57.4 us; the launch traced here: 56.9 us
  Pallas kernels  32.2 us (56%)
  starting transfers between devices  13.6 us (24%)
  waiting for transfers between devices  8.96 us (16%)
  local copies, waits for them, and re-layouts  1.43 us (2%)
  between operations  0.66 us (1%)
    pallas_call x1, Pallas kernels, finish(): pl.pallas_call(finish_kernel, out_shape=[jax.ShapeDtypeStruct((3, beads),...  8.04 us
    pallas_call x1, Pallas kernels, order_chains(): pl.pallas_call(chains_kernel, out_shape=[jax.ShapeDtypeStruct((3 * beads...  7.34 us
    all_to_all x1, starting transfers between devices, on_device(): lax.all_to_all(packets, ('bx', 'by'), split_axis=0, concat_axis=0, tiled=...  7.29 us
    all_to_all x1, starting transfers between devices, on_device(): lax.all_to_all(slopes, ('bx', 'by'), split_axis=0, concat_axis=0, tiled=T...  5.78 us
    all_to_all x1, waiting for transfers between devices, on_device(): lax.all_to_all(slopes, ('bx', 'by'), split_axis=0, concat_axis=0, tiled=T...  5.6 us
    pallas_call x1, Pallas kernels, pick_slopes(): pl.pallas_call(slope_kernel, out_shape=[jax.ShapeDtypeStruct((plane, 6, s...  4.99 us
    pallas_call x1, Pallas kernels, fill(): pl.pallas_call(functools.partial(fill_kernel, bricks, group, slots), out_...  4.97 us
    pallas_call x1, Pallas kernels, deposit(): pl.pallas_call(functools.partial(deposit_kernel, bricks), out_shape=jax.S...  4.63 us
  transfers between devices with their start and end apart: 4, of which 4 were waited for; matrix products, arithmetic and copies ran while one was open for 0% of the time, Pallas kernels for 17%

profile of v5, /device:TPU:0, one launch (start us, length us, event | category | flops | bytes accessed | tf_op | source)
XLA Modules:
  0.0 56.9 jit_solution(1314565109413305018)
XLA Ops:
  0.6 4.6 %shard_map.94.after = f32[8,40,128]{2,1,0:T(8,128)} custom-call(s32[1,4096]{1,0:T(1,128)} %bitcast.1, s32[2,8,4096]{2,1,0:T(8,128)} %corner_slot_far.3, f32[8,4096]{1,0:T(8,128)} %corner_weight_far.3, s32[3,8,256]{2,1,0:T(8,128)} %place.1), custom_call_target="tpu_custom_call" | custom-call | tf_op jit(solution)/shard_map/pallas_call | solution.py:170
  5.3 7.3 %all-to-all-start = ((f32[8,40,128]{2,1,0:T(8,128)}), f32[8,40,128]{2,1,0:T(8,128)S(1)}, u32[]{:S(2)}, u32[]{:S(2)}) async-start(f32[8,40,128]{2,1,0:T(8,128)} %shard_map.94.after), calls=%async_computation | async-start | bytes 327680 | tf_op jit(solution)/shard_map/all_to_all | solution.py:743
  12.6 0.0 copy-start.1
  12.6 7.3 %shard_map.95 = (f32[96,128]{1,0:T(8,128)}, bf16[128,4096]{1,0:T(8,128)(2,1)}, s32[1,4096]{1,0:T(1,128)}, f32[3,16,256]{2,1,0:T(8,128)}) custom-call(f32[3,4096]{1,0:T(4,128)} %positions.1, s32[2,3840]{1,0:T(2,128)} %bonds.1, f32[8,40,128]{2,1,0:T(8,128)} %shard_map.94.after), custom_call_target="tpu_custom_call" | custom-call | tf_op jit(solution)/shard_map/pallas_call | solution.py:570
  19.9 0.2 all-to-all-done.received
  20.1 0.0 copy-start
  20.1 0.8 %copy-done = f32[3,16,256]{2,1,0:T(8,128)S(1)} copy-done((f32[3,16,256]{2,1,0:T(8,128)S(1)}, f32[3,16,256]{2,1,0:T(8,128)}, u32[]{:S(2)}) %copy-start) | copy-done | bytes 49176
  20.9 5.0 %shard_map.96 = (f32[24,80,128]{2,1,0:T(8,128)S(1)}, f32[18,8,128]{2,1,0:T(8,128)S(1)}, f32[18,8,128]{2,1,0:T(8,128)S(1)}) custom-call(f32[8,40,128]{2,1,0:T(8,128)S(1)} %all-to-all-done.received, f32[3,16,256]{2,1,0:T(8,128)S(1)} %copy-done), custom_call_target="tpu_custom_call" | custom-call | tf_op jit(solution)/shard_map/pallas_call | solution.py:339
  25.9 0.5 collective-permute-start.1
  26.4 0.1 collective-permute-start
  26.5 0.9 %shard_map.97.turned = f32[18,2,80,128]{3,2,1,0:T(8,128)S(1)} custom-call(f32[24,80,128]{2,1,0:T(8,128)S(1)} %get-tuple-element.15.field, f32[18,8,128]{2,1,0:T(8,128)S(1)} %get-tuple-element.16.below, f32[18,8,128]{2,1,0:T(8,128)S(1)} %get-tuple-element.17.above), custom_call_target="tpu_custom_call" | custom-call | tf_op jit(solution)/shard_map/pallas_call | solution.py:371
  27.4 1.1 %collective-permute-done.1.from_above = f32[18,8,128]{2,1,0:T(8,128)S(1)} collective-permute-done((f32[18,8,128]{2,1,0:T(8,128)S(1)}, f32[18,8,128]{2,1,0:T(8,128)S(1)}, u32[]{:S(2)}, u32[]{:S(2)}) %collective-permute-start.1) | collective-permute-done | bytes 73760 | tf_op jit(solution)/shard_map/ppermute | solution.py:459
  28.5 2.0 %collective-permute-done.from_below = f32[18,8,128]{2,1,0:T(8,128)S(1)} collective-permute-done((f32[18,8,128]{2,1,0:T(8,128)S(1)}, f32[18,8,128]{2,1,0:T(8,128)S(1)}, u32[]{:S(2)}, u32[]{:S(2)}) %collective-permute-start) | collective-permute-done | bytes 73760 | tf_op jit(solution)/shard_map/ppermute | solution.py:459
  30.6 0.0 copy-done.1
  30.6 5.0 %shard_map.98 = (f32[8,6,256]{2,1,0:T(8,128)}, f32[18,2,80,128]{3,2,1,0:T(8,128)S(1)}) custom-call(f32[18,2,80,128]{3,2,1,0:T(8,128)S(1)} %shard_map.97.turned, f32[18,8,128]{2,1,0:T(8,128)S(1)} %collective-permute-done.from_below, f32[18,8,128]{2,1,0:T(8,128)S(1)} %collective-permute-done.1.from_above, s32[3,8,256]{2,1,0:T(8,128)S(1)} %copy-done.1), custom_call_target="tpu_custom_call" | custom-call | tf_op jit(solution)/shard_map/pallas_call | solution.py:432
  35.5 5.8 %all-to-all-start.1 = ((f32[8,6,256]{2,1,0:T(8,128)}), f32[8,6,256]{2,1,0:T(8,128)S(1)}, u32[]{:S(2)}, u32[]{:S(2)}) async-start(f32[8,6,256]{2,1,0:T(8,128)} %get-tuple-element.18), calls=%async_computation.1 | async-start | bytes 131072 | tf_op jit(solution)/shard_map/all_to_all | solution.py:750
  41.3 1.3 %shard_map.100 = f32[2,16,64,64]{3,2,1,0:T(8,128)} custom-call(f32[18,2,80,128]{3,2,1,0:T(8,128)S(1)} %get-tuple-element.24.whole), custom_call_target="tpu_custom_call" | custom-call | tf_op jit(solution)/shard_map/pallas_call | solution.py:450
  42.6 5.6 %all-to-all-done.1.slopes = f32[8,6,256]{2,1,0:T(8,128)S(1)} async-done(((f32[8,6,256]{2,1,0:T(8,128)}), f32[8,6,256]{2,1,0:T(8,128)S(1)}, u32[]{:S(2)}, u32[]{:S(2)}) %all-to-all-start.1) | async-done | bytes 49184 | tf_op jit(solution)/shard_map/all_to_all | solution.py:750
  48.2 0.0 copy-start.2
  48.2 0.6 %copy-done.2 = f32[8,6,256]{2,1,0:T(8,128)} copy-done((f32[8,6,256]{2,1,0:T(8,128)}, f32[8,6,256]{2,1,0:T(8,128)S(1)}, u32[]{:S(2)}) %copy-start.2) | copy-done | bytes 49176
  48.9 8.0 %shard_map.99 = (f32[3,4096]{1,0:T(4,128)}, f32[3,4096]{1,0:T(4,128)}) custom-call(s32[1,4096]{1,0:T(1,128)} %bitcast.2, s32[2,8,4096]{2,1,0:T(8,128)} %corner_slot_far.3, f32[8,4096]{1,0:T(8,128)} %corner_weight_far.3, f32[3,4096]{1,0:T(4,128)} %velocities_far.1, f32[8,6,256]{2,1,0:T(8,128)} %copy-done.2, f32[96,128]{1,0:T(8,128)} %get-tuple-element.19.anchor_far, ...), custom_call_target="tpu_custom_call" | custom-call | tf_op jit(solution)/shard_map/pallas_call | solution.py:722
Async XLA Ops:
  5.3 14.9 %all-to-all-start = ((f32[8,40,128]{2,1,0:T(8,128)}), f32[8,40,128]{2,1,0:T(8,128)S(1)}, u32[]{:S(2)}, u32[]{:S(2)}) async-start(f32[8,40,128]{2,1,0:T(8,128)} %shard_map.94.after), calls=%async_computation | async-start | bytes 327680 | tf_op jit(solution)/shard_map/all_to_all | solution.py:743
  12.6 18.0 %copy-start.1 = (s32[3,8,256]{2,1,0:T(8,128)S(1)}, s32[3,8,256]{2,1,0:T(8,128)}, u32[]{:S(2)}) copy-start(s32[3,8,256]{2,1,0:T(8,128)} %place.1) | copy-start | bytes 73732
  20.1 0.8 %copy-start = (f32[3,16,256]{2,1,0:T(8,128)S(1)}, f32[3,16,256]{2,1,0:T(8,128)}, u32[]{:S(2)}) copy-start(f32[3,16,256]{2,1,0:T(8,128)} %get-tuple-element.14.after.apart_far) | copy-start | bytes 147460
  25.9 2.6 %collective-permute-start.1 = (f32[18,8,128]{2,1,0:T(8,128)S(1)}, f32[18,8,128]{2,1,0:T(8,128)S(1)}, u32[]{:S(2)}, u32[]{:S(2)}) collective-permute-start(f32[18,8,128]{2,1,0:T(8,128)S(1)} %get-tuple-element.16.below), channel_id=1, source_target_pairs={{1,0},{2,1},{3,2},{0,3},{5,4},{6,5},{7,6},{4,7},{9,8},{10,9},{11,1... | collective-permute-start | bytes 221192 | tf_op jit(solution)/shard_map/ppermute | solution.py:459
  26.4 4.2 %collective-permute-start = (f32[18,8,128]{2,1,0:T(8,128)S(1)}, f32[18,8,128]{2,1,0:T(8,128)S(1)}, u32[]{:S(2)}, u32[]{:S(2)}) collective-permute-start(f32[18,8,128]{2,1,0:T(8,128)S(1)} %get-tuple-element.17.above), channel_id=1, source_target_pairs={{3,0},{0,1},{1,2},{2,3},{7,4},{4,5},{5,6},{6,7},{11,8},{8,9},{9,10... | collective-permute-start | bytes 221192 | tf_op jit(solution)/shard_map/ppermute | solution.py:459
  35.5 12.7 %all-to-all-start.1 = ((f32[8,6,256]{2,1,0:T(8,128)}), f32[8,6,256]{2,1,0:T(8,128)S(1)}, u32[]{:S(2)}, u32[]{:S(2)}) async-start(f32[8,6,256]{2,1,0:T(8,128)} %get-tuple-element.18), calls=%async_computation.1 | async-start | bytes 131072 | tf_op jit(solution)/shard_map/all_to_all | solution.py:750
  48.2 0.6 %copy-start.2 = (f32[8,6,256]{2,1,0:T(8,128)}, f32[8,6,256]{2,1,0:T(8,128)S(1)}, u32[]{:S(2)}) copy-start(f32[8,6,256]{2,1,0:T(8,128)S(1)} %all-to-all-done.1.slopes) | copy-start | bytes 147460

commit v6 on v5

--- a/solution.py
+++ b/solution.py
@@ -33,6 +33,7 @@
 
 LANES = 128
 VMEM_LIMIT = 20 * 1024 * 1024
+VMEM_STAGE = 4 * 1024 * 1024
 VMEM_WIDE = 60 * 1024 * 1024
 HBM = pl.BlockSpec(memory_space=pltpu.HBM)
 f32 = jnp.float32
@@ -581,20 +582,29 @@
     )(positions, bonds, after)
 
 
+def stage_kernel(*refs):
+    count = (len(refs) - 2) // 2
+    sources, targets, sems = refs[:count], refs[count + 1 : -1], refs[-1]
+    copies = [
+        pltpu.make_async_copy(source, target, sems.at[at]) for at, (source, target) in enumerate(zip(sources, targets))
+    ]
+    for copy in copies:
+        copy.start()
+    for copy in copies:
+        copy.wait()
+
+
+def stage(arrays, after):
+    return pl.pallas_call(
+        stage_kernel,
+        out_shape=[jax.ShapeDtypeStruct(a.shape, a.dtype) for a in arrays],
+        in_specs=[HBM] * len(arrays) + [pl.BlockSpec(memory_space=pl.ANY)],
+        scratch_shapes=[pltpu.SemaphoreType.DMA((len(arrays),))],
+        compiler_params=pltpu.CompilerParams(vmem_limit_bytes=VMEM_STAGE),
+    )(*arrays, after)
+
+
 def finish_kernel(
-    species_far,
-    corner_slot_far,
-    corner_weight_far,
-    velocities_far,
-    slopes,
-    anchor_far,
-    hot_far,
-    high_far,
-    apart_far,
-    new_positions,
-    new_velocities,
-    table,
-    shift,
     species,
     corner_slot,
     corner_weight,
@@ -603,9 +613,12 @@
     hot,
     high,
     apart,
+    slopes,
+    new_positions,
+    new_velocities,
+    table,
+    shift,
     placed,
-    sems,
-    late_sems,
 ):
     plane, _, slots = slopes.shape
     blocks = slots // LANES
@@ -614,25 +627,6 @@
     bead_rows = beads // LANES
     length, chains = apart.shape[1:]
     step = chunk_of(beads, 4)
-    wait = chunk_copies(
-        [
-            (species_far, species),
-            (corner_slot_far, corner_slot),
-            (corner_weight_far, corner_weight),
-            (velocities_far, velocities),
-        ],
-        sems,
-        step,
-        beads // step,
-    )
-    late = [
-        pltpu.make_async_copy(source, target, late_sems.at[at])
-        for at, (source, target) in enumerate(
-            [(anchor_far, anchor), (hot_far, hot), (high_far, high), (apart_far, apart)]
-        )
-    ]
-    for copy in late:
-        copy.start()
 
     def collect(brick, carry):
         for axis in range(3):
@@ -647,7 +641,6 @@
     slope_table = jnp.concatenate(parts_of(table[...], 2), axis=1)
 
     def force_body(j, carry):
-        wait(j)
         where = pl.ds(pl.multiple_of(j * step, step), step)
         kind = species[:, where]
         total = jnp.zeros((3 * highs, step), f32)
@@ -667,8 +660,6 @@
 
     lax.fori_loop(0, beads // step, force_body, 0)
 
-    for copy in late:
-        copy.wait()
     shift_table = jnp.concatenate(parts_of(shift[...], 2), axis=1)
     wide = 4 * chains
     for j in range(beads // wide):
@@ -713,26 +704,20 @@
             new_velocities[axis : axis + 1, where] = move / time_step
 
 
-def finish(species, corner_slot, corner_weight, slopes, velocities, prepared):
-    beads = velocities.shape[1]
+def finish(near, slopes):
+    beads = near[3].shape[1]
     plane, _, slots = slopes.shape
     highs = 2 * (slots // LANES) * plane
-    early = (species, corner_slot, corner_weight, velocities)
-    late = tuple(prepared)
     return pl.pallas_call(
         finish_kernel,
         out_shape=[jax.ShapeDtypeStruct((3, beads), f32)] * 2,
-        in_specs=[HBM] * len(early) + [pl.BlockSpec()] + [HBM] * len(late),
         scratch_shapes=[
             pltpu.VMEM((3 * highs, LANES), f32),
             pltpu.VMEM((3 * beads // LANES, LANES), f32),
-            *(pltpu.VMEM(a.shape, a.dtype) for a in early + late),
-            pltpu.VMEM(prepared[3].shape, f32),
-            pltpu.SemaphoreType.DMA((len(early), beads // chunk_of(beads, 4))),
-            pltpu.SemaphoreType.DMA((len(late),)),
+            pltpu.VMEM(near[7].shape, f32),
         ],
-        compiler_params=pltpu.CompilerParams(vmem_limit_bytes=VMEM_WIDE),
-    )(*early, slopes, *late)
+        compiler_params=pltpu.CompilerParams(vmem_limit_bytes=VMEM_LIMIT),
+    )(*near, slopes)
 
 
 def on_device(positions, velocities, species, corner_slot, corner_weight, slot_cell, bond_pairs):
@@ -749,9 +734,8 @@
     slopes, whole = pick_slopes(turned, from_below, from_above, slot_cell)
     returned = lax.all_to_all(slopes, ("bx", "by"), split_axis=0, concat_axis=0, tiled=True)
     smoothed = smoothed_of(whole)
-    moved, new_velocities = finish(
-        species, corner_slot, corner_weight, returned, velocities, prepared
-    )
+    near = stage((species, corner_slot, corner_weight, velocities, *prepared), slopes)
+    moved, new_velocities = finish(near, returned)
     return (moved, new_velocities, smoothed)
 
 

time: 57.4 us -> 54.9 us (0.956)
  Pallas kernels: 32.2 us -> 30.8 us
  waiting for transfers between devices: 8.96 us -> 8.28 us
  local copies, waits for them, and re-layouts: 1.43 us -> 0.84 us
    pallas_call x1, Pallas kernels: 8.04 us -> 6.09 us  [finish(): pl.pallas_call(finish_kernel, out_shape=[jax.ShapeDtypeStruct((3, beads),...]
    all_to_all x1, waiting for transfers between devices: 5.6 us -> 4.92 us  [on_device(): lax.all_to_all(slopes, ('bx', 'by'), split_axis=0, concat_axis=0, tiled=T...]
    pallas_call x0 -> x1, Pallas kernels: none -> 0.62 us  [stage(): pl.pallas_call(stage_kernel, out_shape=[jax.ShapeDtypeStruct(a.shape, a.d...]
    unnamed x6 -> x20, local copies, waits for them, and re-layouts: 1.43 us -> 0.84 us
  transfers between devices with their start and end apart: 4 -> 4, of which waited for: 4 -> 4; matrix products, arithmetic and copies ran while one was open for 0% -> 0% of each run, Pallas kernels for 17% -> 19%
where the time goes in v6:
time: 54.9 us; the launch traced here: 54.5 us
  Pallas kernels  30.8 us (56%)
  starting transfers between devices  13.8 us (25%)
  waiting for transfers between devices  8.28 us (15%)
  local copies, waits for them, and re-layouts  0.84 us (2%)
  between operations  0.74 us (1%)
    pallas_call x1, Pallas kernels, order_chains(): pl.pallas_call(chains_kernel, out_shape=[jax.ShapeDtypeStruct((3 * beads...  7.33 us
    all_to_all x1, starting transfers between devices, on_device(): lax.all_to_all(packets, ('bx', 'by'), split_axis=0, concat_axis=0, tiled=...  7.29 us
    pallas_call x1, Pallas kernels, finish(): pl.pallas_call(finish_kernel, out_shape=[jax.ShapeDtypeStruct((3, beads),...  6.09 us
    all_to_all x1, starting transfers between devices, on_device(): lax.all_to_all(slopes, ('bx', 'by'), split_axis=0, concat_axis=0, tiled=T...  5.93 us
    pallas_call x1, Pallas kernels, fill(): pl.pallas_call(functools.partial(fill_kernel, bricks, group, slots), out_...  4.97 us
    pallas_call x1, Pallas kernels, pick_slopes(): pl.pallas_call(slope_kernel, out_shape=[jax.ShapeDtypeStruct((plane, 6, s...  4.95 us
    all_to_all x1, waiting for transfers between devices, on_device(): lax.all_to_all(slopes, ('bx', 'by'), split_axis=0, concat_axis=0, tiled=T...  4.92 us
    pallas_call x1, Pallas kernels, deposit(): pl.pallas_call(functools.partial(deposit_kernel, bricks), out_shape=jax.S...  4.63 us
  transfers between devices with their start and end apart: 4, of which 4 were waited for; matrix products, arithmetic and copies ran while one was open for 0% of the time, Pallas kernels for 19%

profile of v6, /device:TPU:0, one launch (start us, length us, event | category | flops | bytes accessed | tf_op | source)
XLA Modules:
  0.0 54.5 jit_solution(15458319827837486281)
XLA Ops:
  0.6 4.6 %shard_map.94.after = f32[8,40,128]{2,1,0:T(8,128)} custom-call(s32[1,4096]{1,0:T(1,128)} %bitcast.1, s32[2,8,4096]{2,1,0:T(8,128)} %refs_1_.1, f32[8,4096]{1,0:T(8,128)} %refs_2_.1, s32[3,8,256]{2,1,0:T(8,128)} %place.1), custom_call_target="tpu_custom_call" | custom-call | tf_op jit(solution)/shard_map/pallas_call | solution.py:171
  5.3 7.3 %all-to-all-start = ((f32[8,40,128]{2,1,0:T(8,128)}), f32[8,40,128]{2,1,0:T(8,128)S(1)}, u32[]{:S(2)}, u32[]{:S(2)}) async-start(f32[8,40,128]{2,1,0:T(8,128)} %shard_map.94.after), calls=%async_computation | async-start | bytes 327680 | tf_op jit(solution)/shard_map/all_to_all | solution.py:728
  12.6 0.0 copy-start.5
  12.6 7.3 %shard_map.95 = (f32[96,128]{1,0:T(8,128)}, bf16[128,4096]{1,0:T(8,128)(2,1)}, s32[1,4096]{1,0:T(1,128)}, f32[3,16,256]{2,1,0:T(8,128)}) custom-call(f32[3,4096]{1,0:T(4,128)} %positions.1, s32[2,3840]{1,0:T(2,128)} %bonds.1, f32[8,40,128]{2,1,0:T(8,128)} %shard_map.94.after), custom_call_target="tpu_custom_call" | custom-call | tf_op jit(solution)/shard_map/pallas_call | solution.py:571
  19.9 0.2 all-to-all-done.received
  20.1 0.0 copy-start.3
  20.1 0.8 %copy-done.3 = f32[3,16,256]{2,1,0:T(8,128)S(1)} copy-done((f32[3,16,256]{2,1,0:T(8,128)S(1)}, f32[3,16,256]{2,1,0:T(8,128)}, u32[]{:S(2)}) %copy-start.3) | copy-done | bytes 49176
  20.9 5.0 %shard_map.96 = (f32[24,80,128]{2,1,0:T(8,128)S(1)}, f32[18,8,128]{2,1,0:T(8,128)S(1)}, f32[18,8,128]{2,1,0:T(8,128)S(1)}) custom-call(f32[8,40,128]{2,1,0:T(8,128)S(1)} %all-to-all-done.received, f32[3,16,256]{2,1,0:T(8,128)S(1)} %copy-done.3), custom_call_target="tpu_custom_call" | custom-call | tf_op jit(solution)/shard_map/pallas_call | solution.py:340
  25.9 0.5 collective-permute-start.1
  26.4 0.1 collective-permute-start
  26.5 0.9 %shard_map.97.turned = f32[18,2,80,128]{3,2,1,0:T(8,128)S(1)} custom-call(f32[24,80,128]{2,1,0:T(8,128)S(1)} %get-tuple-element.26.field, f32[18,8,128]{2,1,0:T(8,128)S(1)} %get-tuple-element.27.below, f32[18,8,128]{2,1,0:T(8,128)S(1)} %get-tuple-element.28.above), custom_call_target="tpu_custom_call" | custom-call | tf_op jit(solution)/shard_map/pallas_call | solution.py:372
  27.4 1.1 %collective-permute-done.1.from_above = f32[18,8,128]{2,1,0:T(8,128)S(1)} collective-permute-done((f32[18,8,128]{2,1,0:T(8,128)S(1)}, f32[18,8,128]{2,1,0:T(8,128)S(1)}, u32[]{:S(2)}, u32[]{:S(2)}) %collective-permute-start.1) | collective-permute-done | bytes 73760 | tf_op jit(solution)/shard_map/ppermute | solution.py:460
  28.6 2.0 %collective-permute-done.from_below = f32[18,8,128]{2,1,0:T(8,128)S(1)} collective-permute-done((f32[18,8,128]{2,1,0:T(8,128)S(1)}, f32[18,8,128]{2,1,0:T(8,128)S(1)}, u32[]{:S(2)}, u32[]{:S(2)}) %collective-permute-start) | collective-permute-done | bytes 73760 | tf_op jit(solution)/shard_map/ppermute | solution.py:460
  30.6 0.0 copy-done.5
  30.6 5.0 %shard_map.98 = (f32[8,6,256]{2,1,0:T(8,128)}, f32[18,2,80,128]{3,2,1,0:T(8,128)S(1)}) custom-call(f32[18,2,80,128]{3,2,1,0:T(8,128)S(1)} %shard_map.97.turned, f32[18,8,128]{2,1,0:T(8,128)S(1)} %collective-permute-done.from_below, f32[18,8,128]{2,1,0:T(8,128)S(1)} %collective-permute-done.1.from_above, s32[3,8,256]{2,1,0:T(8,128)S(1)} %copy-done.5), custom_call_target="tpu_custom_call" | custom-call | tf_op jit(solution)/shard_map/pallas_call | solution.py:433
  35.5 0.0 copy-start.6
  35.5 0.0 copy-start.7
  35.5 0.0 copy-start.8
  35.6 0.0 copy-start.9
  35.6 5.9 %all-to-all-start.1 = ((f32[8,6,256]{2,1,0:T(8,128)}), f32[8,6,256]{2,1,0:T(8,128)S(1)}, u32[]{:S(2)}, u32[]{:S(2)}) async-start(f32[8,6,256]{2,1,0:T(8,128)} %get-tuple-element.29.refs_8_), calls=%async_computation.1 | async-start | bytes 131072 | tf_op jit(solution)/shard_map/all_to_all | solution.py:735
  41.5 1.3 %shard_map.101 = f32[2,16,64,64]{3,2,1,0:T(8,128)} custom-call(f32[18,2,80,128]{3,2,1,0:T(8,128)S(1)} %get-tuple-element.40.whole), custom_call_target="tpu_custom_call" | custom-call | tf_op jit(solution)/shard_map/pallas_call | solution.py:451
  42.8 0.0 copy-done
  42.8 0.0 copy-done.1
  42.8 0.0 copy-done.2
  42.8 0.0 copy-done.4
  42.8 0.0 copy-done.6
  42.8 0.0 copy-done.7
  42.8 0.0 copy-done.8
  42.8 0.0 copy-done.9
  42.9 0.6 %shard_map.99 = (s32[1,4096]{1,0:T(1,128)S(1)}, s32[2,8,4096]{2,1,0:T(8,128)S(1)}, f32[8,4096]{1,0:T(8,128)S(1)}, f32[3,4096]{1,0:T(4,128)S(1)}, f32[96,128]{1,0...) custom-call(s32[1,4096]{1,0:T(1,128)S(1)} %bitcast.2, ...), custom_call_target="tpu_custom_call" | custom-call | tf_op jit(solution)/shard_map/pallas_call | solution.py:598
  43.5 4.9 %all-to-all-done.1.slopes = f32[8,6,256]{2,1,0:T(8,128)S(1)} async-done(((f32[8,6,256]{2,1,0:T(8,128)}), f32[8,6,256]{2,1,0:T(8,128)S(1)}, u32[]{:S(2)}, u32[]{:S(2)}) %all-to-all-start.1) | async-done | bytes 49184 | tf_op jit(solution)/shard_map/all_to_all | solution.py:735
  48.4 6.1 %shard_map.100 = (f32[3,4096]{1,0:T(4,128)}, f32[3,4096]{1,0:T(4,128)}) custom-call(s32[1,4096]{1,0:T(1,128)S(1)} %get-tuple-element.30.species, s32[2,8,4096]{2,1,0:T(8,128)S(1)} %get-tuple-element.31.corner_slot, f32[8,4096]{1,0:T(8,128)S(1)} %get-tuple-element.32.corner_weight, f32[3,4096]{1,0:T(4,128)S(1)} %get-tuple-element.33.velocities, ...), custom_call_target="tpu_custom_call" | custom-call | tf_op jit(solution)/shard_map/pallas_call | solution.py:711
  (4 shorter events, 0.0 us)
Async XLA Ops:
  5.3 14.9 %all-to-all-start = ((f32[8,40,128]{2,1,0:T(8,128)}), f32[8,40,128]{2,1,0:T(8,128)S(1)}, u32[]{:S(2)}, u32[]{:S(2)}) async-start(f32[8,40,128]{2,1,0:T(8,128)} %shard_map.94.after), calls=%async_computation | async-start | bytes 327680 | tf_op jit(solution)/shard_map/all_to_all | solution.py:728
  12.6 18.0 %copy-start.5 = (s32[3,8,256]{2,1,0:T(8,128)S(1)}, s32[3,8,256]{2,1,0:T(8,128)}, u32[]{:S(2)}) copy-start(s32[3,8,256]{2,1,0:T(8,128)} %place.1) | copy-start | bytes 73732
  20.1 0.8 %copy-start.3 = (f32[3,16,256]{2,1,0:T(8,128)S(1)}, f32[3,16,256]{2,1,0:T(8,128)}, u32[]{:S(2)}) copy-start(f32[3,16,256]{2,1,0:T(8,128)} %get-tuple-element.25.after.refs_7_) | copy-start | bytes 147460
  25.9 2.6 %collective-permute-start.1 = (f32[18,8,128]{2,1,0:T(8,128)S(1)}, f32[18,8,128]{2,1,0:T(8,128)S(1)}, u32[]{:S(2)}, u32[]{:S(2)}) collective-permute-start(f32[18,8,128]{2,1,0:T(8,128)S(1)} %get-tuple-element.27.below), channel_id=1, source_target_pairs={{1,0},{2,1},{3,2},{0,3},{5,4},{6,5},{7,6},{4,7},{9,8},{10,9},{11,1... | collective-permute-start | bytes 221192 | tf_op jit(solution)/shard_map/ppermute | solution.py:460
  26.4 4.2 %collective-permute-start = (f32[18,8,128]{2,1,0:T(8,128)S(1)}, f32[18,8,128]{2,1,0:T(8,128)S(1)}, u32[]{:S(2)}, u32[]{:S(2)}) collective-permute-start(f32[18,8,128]{2,1,0:T(8,128)S(1)} %get-tuple-element.28.above), channel_id=1, source_target_pairs={{3,0},{0,1},{1,2},{2,3},{7,4},{4,5},{5,6},{6,7},{11,8},{8,9},{9,10... | collective-permute-start | bytes 221192 | tf_op jit(solution)/shard_map/ppermute | solution.py:460
  35.5 7.3 %copy-start = (s32[2,8,4096]{2,1,0:T(8,128)S(1)}, s32[2,8,4096]{2,1,0:T(8,128)}, u32[]{:S(2)}) copy-start(s32[2,8,4096]{2,1,0:T(8,128)} %refs_1_.1) | copy-start | bytes 786436
  35.5 7.3 %copy-start.1 = (bf16[128,4096]{1,0:T(8,128)(2,1)S(1)}, bf16[128,4096]{1,0:T(8,128)(2,1)}, u32[]{:S(2)}) copy-start(bf16[128,4096]{1,0:T(8,128)(2,1)} %get-tuple-element.23.refs_5_) | copy-start | bytes 3145732
  35.5 7.3 %copy-start.2 = (f32[8,4096]{1,0:T(8,128)S(1)}, f32[8,4096]{1,0:T(8,128)}, u32[]{:S(2)}) copy-start(f32[8,4096]{1,0:T(8,128)} %refs_2_.1) | copy-start | bytes 393220
  35.5 7.3 %copy-start.4 = (f32[3,16,256]{2,1,0:T(8,128)S(1)}, f32[3,16,256]{2,1,0:T(8,128)}, u32[]{:S(2)}) copy-start(f32[3,16,256]{2,1,0:T(8,128)} %get-tuple-element.25.after.refs_7_) | copy-start | bytes 147460
  35.5 7.3 %copy-start.6 = (f32[3,4096]{1,0:T(4,128)S(1)}, f32[3,4096]{1,0:T(4,128)}, u32[]{:S(2)}) copy-start(f32[3,4096]{1,0:T(4,128)} %refs_3_.1) | copy-start | bytes 147460
  35.5 7.3 %copy-start.7 = (s32[4096]{0:T(1024)S(1)}, s32[4096]{0:T(1024)}, u32[]{:S(2)}) copy-start(s32[4096]{0:T(1024)} %param.9) | copy-start | bytes 49156
  35.5 7.3 %copy-start.8 = (f32[96,128]{1,0:T(8,128)S(1)}, f32[96,128]{1,0:T(8,128)}, u32[]{:S(2)}) copy-start(f32[96,128]{1,0:T(8,128)} %get-tuple-element.22.refs_4_) | copy-start | bytes 147460
  35.6 7.3 %copy-start.9 = (s32[1,4096]{1,0:T(1,128)S(1)}, s32[1,4096]{1,0:T(1,128)}, u32[]{:S(2)}) copy-start(s32[1,4096]{1,0:T(1,128)} %get-tuple-element.24.refs_6_) | copy-start | bytes 49156
  35.6 12.8 %all-to-all-start.1 = ((f32[8,6,256]{2,1,0:T(8,128)}), f32[8,6,256]{2,1,0:T(8,128)S(1)}, u32[]{:S(2)}, u32[]{:S(2)}) async-start(f32[8,6,256]{2,1,0:T(8,128)} %get-tuple-element.29.refs_8_), calls=%async_computation.1 | async-start | bytes 131072 | tf_op jit(solution)/shard_map/all_to_all | solution.py:735

commit v7 on v6

--- a/solution.py
+++ b/solution.py
@@ -116,7 +116,7 @@
     blocks = slots // LANES
     highs = 2 * blocks * plane
     beads = corner_weight.shape[1]
-    step = chunk_of(beads, 8)
+    step = chunk_of(beads, 32 if plane <= 8 else 8)
     count_x, count_y = bricks.counts
     wait = chunk_copies(
         [(species_far, species), (corner_slot_far, corner_slot), (corner_weight_far, corner_weight)],
@@ -178,7 +178,7 @@
             pltpu.VMEM(corner_slot.shape, corner_slot.dtype),
             pltpu.VMEM(corner_weight.shape, corner_weight.dtype),
             pltpu.VMEM(slot_cell.shape, slot_cell.dtype),
-            pltpu.SemaphoreType.DMA((3, species.shape[1] // chunk_of(species.shape[1], 8))),
+            pltpu.SemaphoreType.DMA((3, species.shape[1] // chunk_of(species.shape[1], 32 if plane <= 8 else 8))),
             pltpu.SemaphoreType.DMA(()),
         ],
         compiler_params=pltpu.CompilerParams(vmem_limit_bytes=VMEM_WIDE),
@@ -626,7 +626,7 @@
     beads = corner_weight.shape[1]
     bead_rows = beads // LANES
     length, chains = apart.shape[1:]
-    step = chunk_of(beads, 4)
+    step = chunk_of(beads, 8)
 
     def collect(brick, carry):
         for axis in range(3):
@@ -658,7 +658,7 @@
             to_rows(shift, axis * bead_rows + j * (step // LANES), time_step * half)
         return carry
 
-    lax.fori_loop(0, beads // step, force_body, 0)
+    lax.fori_loop(0, beads // step, force_body, 0, unroll=beads // step if plane <= 8 else 1)
 
     shift_table = jnp.concatenate(parts_of(shift[...], 2), axis=1)
     wide = 4 * chains

time: 54.9 us -> 53.2 us (0.969)
  Pallas kernels: 30.8 us -> 29.1 us
    pallas_call x1, Pallas kernels: 6.09 us -> 4.86 us  [finish(): pl.pallas_call(finish_kernel, out_shape=[jax.ShapeDtypeStruct((3, beads),...]
where the time goes in v7:
time: 53.2 us; the launch traced here: 52.8 us
  Pallas kernels  29.1 us (55%)
  starting transfers between devices  13.8 us (26%)
  waiting for transfers between devices  8.32 us (16%)
  local copies, waits for them, and re-layouts  0.84 us (2%)
  between operations  0.74 us (1%)
    pallas_call x1, Pallas kernels, order_chains(): pl.pallas_call(chains_kernel, out_shape=[jax.ShapeDtypeStruct((3 * beads...  7.33 us
    all_to_all x1, starting transfers between devices, on_device(): lax.all_to_all(packets, ('bx', 'by'), split_axis=0, concat_axis=0, tiled=...  7.29 us
    all_to_all x1, starting transfers between devices, on_device(): lax.all_to_all(slopes, ('bx', 'by'), split_axis=0, concat_axis=0, tiled=T...  5.91 us
    pallas_call x1, Pallas kernels, fill(): pl.pallas_call(functools.partial(fill_kernel, bricks, group, slots), out_...  4.96 us
    pallas_call x1, Pallas kernels, pick_slopes(): pl.pallas_call(slope_kernel, out_shape=[jax.ShapeDtypeStruct((plane, 6, s...  4.96 us
    all_to_all x1, waiting for transfers between devices, on_device(): lax.all_to_all(slopes, ('bx', 'by'), split_axis=0, concat_axis=0, tiled=T...  4.92 us
    pallas_call x1, Pallas kernels, finish(): pl.pallas_call(finish_kernel, out_shape=[jax.ShapeDtypeStruct((3, beads),...  4.86 us
    pallas_call x1, Pallas kernels, deposit(): pl.pallas_call(functools.partial(deposit_kernel, bricks), out_shape=jax.S...  4.15 us
  transfers between devices with their start and end apart: 4, of which 4 were waited for; matrix products, arithmetic and copies ran while one was open for 0% of the time, Pallas kernels for 19%

profile of v7, /device:TPU:0, one launch (start us, length us, event | category | flops | bytes accessed | tf_op | source)
XLA Modules:
  0.0 52.8 jit_solution(90271279670010008)
XLA Ops:
  0.6 4.1 %shard_map.94.after = f32[8,40,128]{2,1,0:T(8,128)} custom-call(s32[1,4096]{1,0:T(1,128)} %bitcast.1, s32[2,8,4096]{2,1,0:T(8,128)} %refs_1_.1, f32[8,4096]{1,0:T(8,128)} %refs_2_.1, s32[3,8,256]{2,1,0:T(8,128)} %place.1), custom_call_target="tpu_custom_call" | custom-call | tf_op jit(solution)/shard_map/pallas_call | solution.py:171
  4.8 7.3 %all-to-all-start = ((f32[8,40,128]{2,1,0:T(8,128)}), f32[8,40,128]{2,1,0:T(8,128)S(1)}, u32[]{:S(2)}, u32[]{:S(2)}) async-start(f32[8,40,128]{2,1,0:T(8,128)} %shard_map.94.after), calls=%async_computation | async-start | bytes 327680 | tf_op jit(solution)/shard_map/all_to_all | solution.py:728
  12.1 0.0 copy-start.5
  12.1 7.3 %shard_map.95 = (f32[96,128]{1,0:T(8,128)}, bf16[128,4096]{1,0:T(8,128)(2,1)}, s32[1,4096]{1,0:T(1,128)}, f32[3,16,256]{2,1,0:T(8,128)}) custom-call(f32[3,4096]{1,0:T(4,128)} %positions.1, s32[2,3840]{1,0:T(2,128)} %bonds.1, f32[8,40,128]{2,1,0:T(8,128)} %shard_map.94.after), custom_call_target="tpu_custom_call" | custom-call | tf_op jit(solution)/shard_map/pallas_call | solution.py:571
  19.4 0.2 all-to-all-done.received
  19.6 0.0 copy-start.3
  19.6 0.8 %copy-done.3 = f32[3,16,256]{2,1,0:T(8,128)S(1)} copy-done((f32[3,16,256]{2,1,0:T(8,128)S(1)}, f32[3,16,256]{2,1,0:T(8,128)}, u32[]{:S(2)}) %copy-start.3) | copy-done | bytes 49176
  20.4 5.0 %shard_map.96 = (f32[24,80,128]{2,1,0:T(8,128)S(1)}, f32[18,8,128]{2,1,0:T(8,128)S(1)}, f32[18,8,128]{2,1,0:T(8,128)S(1)}) custom-call(f32[8,40,128]{2,1,0:T(8,128)S(1)} %all-to-all-done.received, f32[3,16,256]{2,1,0:T(8,128)S(1)} %copy-done.3), custom_call_target="tpu_custom_call" | custom-call | tf_op jit(solution)/shard_map/pallas_call | solution.py:340
  25.4 0.5 collective-permute-start.1
  25.9 0.1 collective-permute-start
  26.0 0.9 %shard_map.97.turned = f32[18,2,80,128]{3,2,1,0:T(8,128)S(1)} custom-call(f32[24,80,128]{2,1,0:T(8,128)S(1)} %get-tuple-element.26.field, f32[18,8,128]{2,1,0:T(8,128)S(1)} %get-tuple-element.27.below, f32[18,8,128]{2,1,0:T(8,128)S(1)} %get-tuple-element.28.above), custom_call_target="tpu_custom_call" | custom-call | tf_op jit(solution)/shard_map/pallas_call | solution.py:372
  26.9 1.0 %collective-permute-done.1.from_above = f32[18,8,128]{2,1,0:T(8,128)S(1)} collective-permute-done((f32[18,8,128]{2,1,0:T(8,128)S(1)}, f32[18,8,128]{2,1,0:T(8,128)S(1)}, u32[]{:S(2)}, u32[]{:S(2)}) %collective-permute-start.1) | collective-permute-done | bytes 73760 | tf_op jit(solution)/shard_map/ppermute | solution.py:460
  27.9 2.2 %collective-permute-done.from_below = f32[18,8,128]{2,1,0:T(8,128)S(1)} collective-permute-done((f32[18,8,128]{2,1,0:T(8,128)S(1)}, f32[18,8,128]{2,1,0:T(8,128)S(1)}, u32[]{:S(2)}, u32[]{:S(2)}) %collective-permute-start) | collective-permute-done | bytes 73760 | tf_op jit(solution)/shard_map/ppermute | solution.py:460
  30.1 0.0 copy-done.5
  30.1 5.0 %shard_map.98 = (f32[8,6,256]{2,1,0:T(8,128)}, f32[18,2,80,128]{3,2,1,0:T(8,128)S(1)}) custom-call(f32[18,2,80,128]{3,2,1,0:T(8,128)S(1)} %shard_map.97.turned, f32[18,8,128]{2,1,0:T(8,128)S(1)} %collective-permute-done.from_below, f32[18,8,128]{2,1,0:T(8,128)S(1)} %collective-permute-done.1.from_above, s32[3,8,256]{2,1,0:T(8,128)S(1)} %copy-done.5), custom_call_target="tpu_custom_call" | custom-call | tf_op jit(solution)/shard_map/pallas_call | solution.py:433
  35.1 0.0 copy-start.6
  35.1 0.0 copy-start.7
  35.1 0.0 copy-start.8
  35.1 0.0 copy-start.9
  35.1 5.9 %all-to-all-start.1 = ((f32[8,6,256]{2,1,0:T(8,128)}), f32[8,6,256]{2,1,0:T(8,128)S(1)}, u32[]{:S(2)}, u32[]{:S(2)}) async-start(f32[8,6,256]{2,1,0:T(8,128)} %get-tuple-element.29.refs_8_), calls=%async_computation.1 | async-start | bytes 131072 | tf_op jit(solution)/shard_map/all_to_all | solution.py:735
  41.0 1.3 %shard_map.101 = f32[2,16,64,64]{3,2,1,0:T(8,128)} custom-call(f32[18,2,80,128]{3,2,1,0:T(8,128)S(1)} %get-tuple-element.40.whole), custom_call_target="tpu_custom_call" | custom-call | tf_op jit(solution)/shard_map/pallas_call | solution.py:451
  42.3 0.0 copy-done
  42.3 0.0 copy-done.1
  42.3 0.0 copy-done.2
  42.3 0.0 copy-done.4
  42.3 0.0 copy-done.6
  42.3 0.0 copy-done.7
  42.4 0.0 copy-done.8
  42.4 0.0 copy-done.9
  42.4 0.6 %shard_map.99 = (s32[1,4096]{1,0:T(1,128)S(1)}, s32[2,8,4096]{2,1,0:T(8,128)S(1)}, f32[8,4096]{1,0:T(8,128)S(1)}, f32[3,4096]{1,0:T(4,128)S(1)}, f32[96,128]{1,0...) custom-call(s32[1,4096]{1,0:T(1,128)S(1)} %bitcast.2, ...), custom_call_target="tpu_custom_call" | custom-call | tf_op jit(solution)/shard_map/pallas_call | solution.py:598
  43.0 4.9 %all-to-all-done.1.slopes = f32[8,6,256]{2,1,0:T(8,128)S(1)} async-done(((f32[8,6,256]{2,1,0:T(8,128)}), f32[8,6,256]{2,1,0:T(8,128)S(1)}, u32[]{:S(2)}, u32[]{:S(2)}) %all-to-all-start.1) | async-done | bytes 49184 | tf_op jit(solution)/shard_map/all_to_all | solution.py:735
  47.9 4.9 %shard_map.100 = (f32[3,4096]{1,0:T(4,128)}, f32[3,4096]{1,0:T(4,128)}) custom-call(s32[1,4096]{1,0:T(1,128)S(1)} %get-tuple-element.30.species, s32[2,8,4096]{2,1,0:T(8,128)S(1)} %get-tuple-element.31.corner_slot, f32[8,4096]{1,0:T(8,128)S(1)} %get-tuple-element.32.corner_weight, f32[3,4096]{1,0:T(4,128)S(1)} %get-tuple-element.33.velocities, ...), custom_call_target="tpu_custom_call" | custom-call | tf_op jit(solution)/shard_map/pallas_call | solution.py:711
  (4 shorter events, 0.0 us)
Async XLA Ops:
  4.8 14.9 %all-to-all-start = ((f32[8,40,128]{2,1,0:T(8,128)}), f32[8,40,128]{2,1,0:T(8,128)S(1)}, u32[]{:S(2)}, u32[]{:S(2)}) async-start(f32[8,40,128]{2,1,0:T(8,128)} %shard_map.94.after), calls=%async_computation | async-start | bytes 327680 | tf_op jit(solution)/shard_map/all_to_all | solution.py:728
  12.1 18.0 %copy-start.5 = (s32[3,8,256]{2,1,0:T(8,128)S(1)}, s32[3,8,256]{2,1,0:T(8,128)}, u32[]{:S(2)}) copy-start(s32[3,8,256]{2,1,0:T(8,128)} %place.1) | copy-start | bytes 73732
  19.6 0.8 %copy-start.3 = (f32[3,16,256]{2,1,0:T(8,128)S(1)}, f32[3,16,256]{2,1,0:T(8,128)}, u32[]{:S(2)}) copy-start(f32[3,16,256]{2,1,0:T(8,128)} %get-tuple-element.25.after.refs_7_) | copy-start | bytes 147460
  25.4 2.5 %collective-permute-start.1 = (f32[18,8,128]{2,1,0:T(8,128)S(1)}, f32[18,8,128]{2,1,0:T(8,128)S(1)}, u32[]{:S(2)}, u32[]{:S(2)}) collective-permute-start(f32[18,8,128]{2,1,0:T(8,128)S(1)} %get-tuple-element.27.below), channel_id=1, source_target_pairs={{1,0},{2,1},{3,2},{0,3},{5,4},{6,5},{7,6},{4,7},{9,8},{10,9},{11,1... | collective-permute-start | bytes 221192 | tf_op jit(solution)/shard_map/ppermute | solution.py:460
  25.9 4.2 %collective-permute-start = (f32[18,8,128]{2,1,0:T(8,128)S(1)}, f32[18,8,128]{2,1,0:T(8,128)S(1)}, u32[]{:S(2)}, u32[]{:S(2)}) collective-permute-start(f32[18,8,128]{2,1,0:T(8,128)S(1)} %get-tuple-element.28.above), channel_id=1, source_target_pairs={{3,0},{0,1},{1,2},{2,3},{7,4},{4,5},{5,6},{6,7},{11,8},{8,9},{9,10... | collective-permute-start | bytes 221192 | tf_op jit(solution)/shard_map/ppermute | solution.py:460
  35.0 7.3 %copy-start = (s32[2,8,4096]{2,1,0:T(8,128)S(1)}, s32[2,8,4096]{2,1,0:T(8,128)}, u32[]{:S(2)}) copy-start(s32[2,8,4096]{2,1,0:T(8,128)} %refs_1_.1) | copy-start | bytes 786436
  35.0 7.3 %copy-start.1 = (bf16[128,4096]{1,0:T(8,128)(2,1)S(1)}, bf16[128,4096]{1,0:T(8,128)(2,1)}, u32[]{:S(2)}) copy-start(bf16[128,4096]{1,0:T(8,128)(2,1)} %get-tuple-element.23.refs_5_) | copy-start | bytes 3145732
  35.0 7.3 %copy-start.2 = (f32[8,4096]{1,0:T(8,128)S(1)}, f32[8,4096]{1,0:T(8,128)}, u32[]{:S(2)}) copy-start(f32[8,4096]{1,0:T(8,128)} %refs_2_.1) | copy-start | bytes 393220
  35.1 7.3 %copy-start.4 = (f32[3,16,256]{2,1,0:T(8,128)S(1)}, f32[3,16,256]{2,1,0:T(8,128)}, u32[]{:S(2)}) copy-start(f32[3,16,256]{2,1,0:T(8,128)} %get-tuple-element.25.after.refs_7_) | copy-start | bytes 147460
  35.1 7.3 %copy-start.6 = (f32[3,4096]{1,0:T(4,128)S(1)}, f32[3,4096]{1,0:T(4,128)}, u32[]{:S(2)}) copy-start(f32[3,4096]{1,0:T(4,128)} %refs_3_.1) | copy-start | bytes 147460
  35.1 7.3 %copy-start.7 = (s32[4096]{0:T(1024)S(1)}, s32[4096]{0:T(1024)}, u32[]{:S(2)}) copy-start(s32[4096]{0:T(1024)} %param.9) | copy-start | bytes 49156
  35.1 7.3 %copy-start.8 = (f32[96,128]{1,0:T(8,128)S(1)}, f32[96,128]{1,0:T(8,128)}, u32[]{:S(2)}) copy-start(f32[96,128]{1,0:T(8,128)} %get-tuple-element.22.refs_4_) | copy-start | bytes 147460
  35.1 7.3 %copy-start.9 = (s32[1,4096]{1,0:T(1,128)S(1)}, s32[1,4096]{1,0:T(1,128)}, u32[]{:S(2)}) copy-start(s32[1,4096]{1,0:T(1,128)} %get-tuple-element.24.refs_6_) | copy-start | bytes 49156
  35.1 12.8 %all-to-all-start.1 = ((f32[8,6,256]{2,1,0:T(8,128)}), f32[8,6,256]{2,1,0:T(8,128)S(1)}, u32[]{:S(2)}, u32[]{:S(2)}) async-start(f32[8,6,256]{2,1,0:T(8,128)} %get-tuple-element.29.refs_8_), calls=%async_computation.1 | async-start | bytes 131072 | tf_op jit(solution)/shard_map/all_to_all | solution.py:735
